TPU v7x, 32 devices: a whole 2x2x4 slice. The times are simulated.
32 devices in a mesh: seq: 16 (over z, x, core), head: 2 (over y).
Axes of the slice: x: 2, y: 2, z: 4, core: 2. Of those that a mesh axis runs over, the one named last changes fastest.
Arguments:
- queries: bfloat16 [8192, 4096], P(('seq', 'head'))
- key_vectors: bfloat16 [8192, 4096], P(('seq', 'head'))
- value_vectors: bfloat16 [8192, 4096], P(('seq', 'head')), may hold values from -6 to 6
- out_grads: bfloat16 [8192, 4096], P(('seq', 'head')), may hold values from -6 to 6
- extra_blocks: int32 [16, 8, 8], P('seq'), may hold values 0 or 1
- summary_rows: int32 [16, 16], P('seq'), may hold values from 0 to 511, as said below
Outputs:
- attention: bfloat16 [8192, 4096], P(('seq', 'head'))
- query_grad: bfloat16 [8192, 4096], P(('seq', 'head'))
- key_grad: bfloat16 [8192, 4096], P(('seq', 'head'))
- value_grad: bfloat16 [8192, 4096], P(('seq', 'head'))
Inputs may be any that keep to these rules, and one draw needn't show every extreme that they name: `summary_rows`: summary row s of a group lies in [s * 32, (s + 1) * 32), so the rows of a group are distinct and ascending.
All inputs are finite; a program needn't handle non-finite values. No bound on the sum of `extra_blocks` on one device may be relied on, other than what follows from the above.
Results may differ from a plain program's by a relative error of at most 0.022.
Values may be sent and summed in bfloat16 or wider, within the bound.
No kernel may reach another device: no remote copies, remote signals or barrier semaphores. Data moves between devices by JAX's collectives and lax.ppermute only.
A program may use at most 128 MiB of HBM per device.

v0:
```python
import math

import jax
import jax.numpy as jnp
from jax import lax
from jax.sharding import PartitionSpec as P

HD = 128


neg_big = -1e30


def head_scores(query_heads, key_heads, factor):
    return (
        jnp.einsum("qhd,khd->hqk", query_heads, key_heads, preferred_element_type=jnp.float32)
        * factor
    )


def local_allowed(extra_map, group_len):
    block_count = extra_map.shape[0]
    block_len = group_len // block_count
    block_ids = jnp.arange(block_count, dtype=jnp.int32)
    block_lag = block_ids[:, None] - block_ids[None, :]
    allowed = (block_lag == 0) | (block_lag == 1) | (extra_map == 1) & (block_lag > 0)
    allowed = jnp.repeat(jnp.repeat(allowed, block_len, axis=0), block_len, axis=1)
    positions = jnp.arange(group_len, dtype=jnp.int32)
    return allowed & (positions[None, :] <= positions[:, None])


def key_window(summary_keys, summary_vals, block_id, key_rows, lower_end, upper_end, per_group):
    offset = block_id * key_rows
    key_block = lax.dynamic_slice_in_dim(summary_keys, offset, key_rows, 0)
    val_block = lax.dynamic_slice_in_dim(summary_vals, offset, key_rows, 0)
    owners = (offset + jnp.arange(key_rows, dtype=jnp.int32)) // per_group
    usable = (owners >= lower_end) & (owners < upper_end)
    return (offset, key_block, val_block, usable[None, None, :])


def block_bounds(lower_end, upper_end, key_rows, per_group):
    begin_block = lower_end * per_group // key_rows
    end_block = (upper_end * per_group + key_rows - 1) // key_rows
    return (begin_block, jnp.where(upper_end > lower_end, end_block, begin_block))


def softmax_stats(
    query_heads, summary_keys, summary_vals, lower_end, upper_end, key_rows, per_group, factor
):
    begin_block, end_block = block_bounds(lower_end, upper_end, key_rows, per_group)

    def softmax_advance(block_id, carried):
        peak, summed = carried
        offset, key_block, val_block, usable = key_window(
            summary_keys, summary_vals, block_id, key_rows, lower_end, upper_end, per_group
        )
        scores = jnp.where(usable, head_scores(query_heads, key_block, factor), neg_big)
        new_peak = jnp.maximum(peak, jnp.max(scores, axis=2))
        summed = summed * jnp.exp(peak - new_peak) + jnp.sum(
            jnp.exp(scores - new_peak[..., None]), axis=2
        )
        return (new_peak, summed)

    shape_hq = (query_heads.shape[1], query_heads.shape[0])
    start_stats = (jnp.full(shape_hq, neg_big, jnp.float32), jnp.zeros(shape_hq, jnp.float32))
    return lax.fori_loop(begin_block, end_block, softmax_advance, start_stats)


def merge_stats(earlier, later):
    peak = jnp.maximum(earlier[0], later[0])
    return (peak, earlier[1] * jnp.exp(earlier[0] - peak) + later[1] * jnp.exp(later[0] - peak))


def weighted_values(
    query_heads,
    log_mass,
    summary_keys,
    summary_vals,
    lower_end,
    upper_end,
    key_rows,
    per_group,
    factor,
):
    begin_block, end_block = block_bounds(lower_end, upper_end, key_rows, per_group)

    def weighted_advance(block_id, summed_values):
        offset, key_block, val_block, usable = key_window(
            summary_keys, summary_vals, block_id, key_rows, lower_end, upper_end, per_group
        )
        weights = jnp.where(
            usable, jnp.exp(head_scores(query_heads, key_block, factor) - log_mass[..., None]), 0.0
        ).astype(jnp.bfloat16)
        return summed_values + jnp.einsum(
            "hqk,khd->qhd", weights, val_block, preferred_element_type=jnp.float32
        )

    return lax.fori_loop(
        begin_block, end_block, weighted_advance, jnp.zeros(query_heads.shape, jnp.float32)
    )


def summary_backward(
    query_heads,
    grad_heads,
    log_mass,
    row_dot,
    summary_keys,
    summary_vals,
    lower_end,
    upper_end,
    key_rows,
    per_group,
    factor,
    carried,
):
    begin_block, end_block = block_bounds(lower_end, upper_end, key_rows, per_group)

    def summary_advance(block_id, running):
        query_acc, key_terms, val_terms = running
        offset, key_block, val_block, usable = key_window(
            summary_keys, summary_vals, block_id, key_rows, lower_end, upper_end, per_group
        )
        attn_probs = jnp.where(
            usable, jnp.exp(head_scores(query_heads, key_block, factor) - log_mass[..., None]), 0.0
        )
        weights = attn_probs.astype(jnp.bfloat16)
        prob_grads = jnp.einsum(
            "qhd,khd->hqk", grad_heads, val_block, preferred_element_type=jnp.float32
        )
        score_grads = (attn_probs * (prob_grads - row_dot[..., None])).astype(jnp.bfloat16)
        query_acc = (
            query_acc
            + jnp.einsum("hqk,khd->qhd", score_grads, key_block, preferred_element_type=jnp.float32)
            * factor
        )
        key_part = (
            jnp.einsum("hqk,qhd->khd", score_grads, query_heads, preferred_element_type=jnp.float32)
            * factor
        )
        val_part = jnp.einsum(
            "hqk,qhd->khd", weights, grad_heads, preferred_element_type=jnp.float32
        )
        key_terms = lax.dynamic_update_slice_in_dim(
            key_terms,
            lax.dynamic_slice_in_dim(key_terms, offset, key_rows, 0) + key_part,
            offset,
            0,
        )
        val_terms = lax.dynamic_update_slice_in_dim(
            val_terms,
            lax.dynamic_slice_in_dim(val_terms, offset, key_rows, 0) + val_part,
            offset,
            0,
        )
        return (query_acc, key_terms, val_terms)

    return lax.fori_loop(begin_block, end_block, summary_advance, carried)


def per_device(queries, key_vectors, value_vectors, out_grads, extra_blocks, summary_rows):
    query_all, key_all, val_all, grad_all = (
        lax.all_to_all(queries, "head", split_axis=1, concat_axis=0, tiled=True),
        lax.all_to_all(key_vectors, "head", split_axis=1, concat_axis=0, tiled=True),
        lax.all_to_all(value_vectors, "head", split_axis=1, concat_axis=0, tiled=True),
        lax.all_to_all(out_grads, "head", split_axis=1, concat_axis=0, tiled=True),
    )
    group_len, local_width = query_all.shape
    head_count = local_width // HD
    factor = HD ** (-0.5)
    query_heads = query_all.reshape(group_len, head_count, HD)
    key_heads = key_all.reshape(group_len, head_count, HD)
    val_heads = val_all.reshape(group_len, head_count, HD)
    grad_heads = grad_all.reshape(group_len, head_count, HD)
    per_group = summary_rows.shape[1]
    seq_count = lax.axis_size("seq")
    group_id = lax.axis_index("seq")
    picker = summary_rows[0][:, None] == jnp.arange(group_len, dtype=jnp.int32)[None, :]
    own_keys = jnp.dot(
        picker.astype(jnp.bfloat16), key_all, preferred_element_type=jnp.float32
    ).astype(jnp.bfloat16)
    own_vals = jnp.dot(
        picker.astype(jnp.bfloat16), val_all, preferred_element_type=jnp.float32
    ).astype(jnp.bfloat16)
    summ_keys_flat, summ_vals_flat = (
        lax.all_gather(own_keys, "seq", axis=0, tiled=True),
        lax.all_gather(own_vals, "seq", axis=0, tiled=True),
    )
    total_rows = summ_keys_flat.shape[0]
    summary_keys = summ_keys_flat.reshape(total_rows, head_count, HD)
    summary_vals = summ_vals_flat.reshape(total_rows, head_count, HD)
    key_rows = per_group * math.gcd(seq_count, max(1, 128 // per_group))
    allowed = local_allowed(extra_blocks[0], group_len)
    local_scores = jnp.where(allowed[None], head_scores(query_heads, key_heads, factor), neg_big)
    local_peak = jnp.max(local_scores, axis=2)
    local_stats = (local_peak, jnp.sum(jnp.exp(local_scores - local_peak[..., None]), axis=2))
    all_stats = merge_stats(
        local_stats,
        softmax_stats(
            query_heads, summary_keys, summary_vals, 0, group_id, key_rows, per_group, factor
        ),
    )
    log_mass = all_stats[0] + jnp.log(all_stats[1])
    summ_values = weighted_values(
        query_heads, log_mass, summary_keys, summary_vals, 0, group_id, key_rows, per_group, factor
    )
    local_probs = jnp.exp(local_scores - log_mass[..., None])
    local_weights = local_probs.astype(jnp.bfloat16)
    attention = (
        summ_values
        + jnp.einsum("hqk,khd->qhd", local_weights, val_heads, preferred_element_type=jnp.float32)
    ).astype(jnp.bfloat16)
    row_dot = jnp.einsum("qhd,qhd->hq", grad_heads, attention, preferred_element_type=jnp.float32)
    local_prob_grads = jnp.einsum(
        "qhd,khd->hqk", grad_heads, val_heads, preferred_element_type=jnp.float32
    )
    local_score_grads = (local_probs * (local_prob_grads - row_dot[..., None])).astype(jnp.bfloat16)
    query_local = (
        jnp.einsum("hqk,khd->qhd", local_score_grads, key_heads, preferred_element_type=jnp.float32)
        * factor
    )
    key_local = (
        jnp.einsum(
            "hqk,qhd->khd", local_score_grads, query_heads, preferred_element_type=jnp.float32
        )
        * factor
    )
    val_local = jnp.einsum(
        "hqk,qhd->khd", local_weights, grad_heads, preferred_element_type=jnp.float32
    )
    empty_terms = jnp.zeros((total_rows, head_count, HD), jnp.float32)
    start_running = (jnp.zeros(query_heads.shape, jnp.float32), empty_terms, empty_terms)
    query_summ, key_terms, val_terms = summary_backward(
        query_heads,
        grad_heads,
        log_mass,
        row_dot,
        summary_keys,
        summary_vals,
        0,
        group_id,
        key_rows,
        per_group,
        factor,
        start_running,
    )
    recv_keys, recv_vals = (
        lax.all_to_all(
            key_terms.astype(jnp.bfloat16), "seq", split_axis=0, concat_axis=0, tiled=True
        ).astype(key_terms.dtype),
        lax.all_to_all(
            val_terms.astype(jnp.bfloat16), "seq", split_axis=0, concat_axis=0, tiled=True
        ).astype(val_terms.dtype),
    )
    summ_key_grad = jnp.sum(recv_keys.reshape(seq_count, per_group, head_count, HD), axis=0)
    summ_val_grad = jnp.sum(recv_vals.reshape(seq_count, per_group, head_count, HD), axis=0)
    picker_f = picker.astype(jnp.float32)
    key_grad = key_local + jnp.einsum(
        "sq,shd->qhd", picker_f, summ_key_grad, precision=lax.Precision.HIGHEST
    )
    value_grad = val_local + jnp.einsum(
        "sq,shd->qhd", picker_f, summ_val_grad, precision=lax.Precision.HIGHEST
    )
    query_grad = query_local + query_summ
    outputs = (
        attention.reshape(group_len, local_width),
        query_grad.astype(jnp.bfloat16).reshape(group_len, local_width),
        key_grad.astype(jnp.bfloat16).reshape(group_len, local_width),
        value_grad.astype(jnp.bfloat16).reshape(group_len, local_width),
    )
    attention_out, query_out, key_out, value_out = (
        lax.all_to_all(outputs[0], "head", split_axis=0, concat_axis=1, tiled=True),
        lax.all_to_all(outputs[1], "head", split_axis=0, concat_axis=1, tiled=True),
        lax.all_to_all(outputs[2], "head", split_axis=0, concat_axis=1, tiled=True),
        lax.all_to_all(outputs[3], "head", split_axis=0, concat_axis=1, tiled=True),
    )
    return (attention_out, query_out, key_out, value_out)


def solution(mesh):
    placed = (
        P(("seq", "head"), None),
        P(("seq", "head"), None),
        P(("seq", "head"), None),
        P(("seq", "head"), None),
        P("seq", None, None),
        P("seq", None),
    )
    return jax.shard_map(
        per_device,
        mesh=mesh,
        in_specs=placed,
        out_specs=(
            P(("seq", "head"), None),
            P(("seq", "head"), None),
            P(("seq", "head"), None),
            P(("seq", "head"), None),
        ),
        check_vma=False,
    )
```

profile of v0, /device:TPU:0, one launch (start us, length us, event | category | flops | bytes accessed | tf_op | source)
XLA Modules:
  0.0 453.2 jit_solution(13521449388905661040)
XLA Ops:
  7.2 3.2 copy.257
  10.3 4.2 all-to-all-start.2
  14.6 4.1 copy.143
  18.6 21.8 %all-to-all-done.2 = bf16[256,2,2048]{2,0,1:T(8,128)(2,1)S(1)} async-done(((bf16[256,2,2048]{2,0,1:T(8,128)(2,1)}), bf16[256,2,2048]{2,0,1:T(8,128)(2,1)S(1)}, u32[]{:S(2)}, u32[]{:S(2)}) %all-to-all-start.2) | async-done | bytes 2097184 | tf_op jit(solution)/shard_map/all_to_all | solution.py:163
  40.4 4.8 %all-to-all-start.1 = ((bf16[256,2,2048]{0,2,1:T(8,128)(2,1)}), bf16[256,2,2048]{0,2,1:T(8,128)(2,1)}, u32[]{:S(2)}, u32[]{:S(2)}) async-start(bf16[256,2,2048]{0,2,1:T(8,128)(2,1)} %bitcast.153), calls=%async_computation.1 | async-start | bytes 4194304 | tf_op jit(solution)/shard_map/all_to_all | solution.py:164
  45.2 4.1 copy.141
  49.3 20.6 %all-to-all-done.1 = bf16[256,2,2048]{0,2,1:T(8,128)(2,1)} async-done(((bf16[256,2,2048]{0,2,1:T(8,128)(2,1)}), bf16[256,2,2048]{0,2,1:T(8,128)(2,1)}, u32[]{:S(2)}, u32[]{:S(2)}) %all-to-all-start.1) | async-done | bytes 2097184 | tf_op jit(solution)/shard_map/all_to_all | solution.py:164
  69.9 4.9 %all-to-all-start = ((bf16[256,2,2048]{0,2,1:T(8,128)(2,1)}), bf16[256,2,2048]{0,2,1:T(8,128)(2,1)}, u32[]{:S(2)}, u32[]{:S(2)}) async-start(bf16[256,2,2048]{0,2,1:T(8,128)(2,1)} %bitcast.151), calls=%async_computation | async-start | bytes 4194304 | tf_op jit(solution)/shard_map/all_to_all | solution.py:165
  74.9 2.9 copy.144
  79.2 3.2 copy.256
  82.4 16.2 %all-to-all-done = bf16[256,2,2048]{0,2,1:T(8,128)(2,1)} async-done(((bf16[256,2,2048]{0,2,1:T(8,128)(2,1)}), bf16[256,2,2048]{0,2,1:T(8,128)(2,1)}, u32[]{:S(2)}, u32[]{:S(2)}) %all-to-all-start) | async-done | bytes 2097184 | tf_op jit(solution)/shard_map/all_to_all | solution.py:165
  98.6 4.8 %all-to-all-start.4 = ((bf16[256,2,2048]{2,0,1:T(8,128)(2,1)}), bf16[256,2,2048]{2,0,1:T(8,128)(2,1)}, u32[]{:S(2)}, u32[]{:S(2)}) async-start(bf16[256,2,2048]{2,0,1:T(8,128)(2,1)} %bitcast.150), calls=%async_computation.4 | async-start | bytes 4194304 | tf_op jit(solution)/shard_map/all_to_all | solution.py:166
  109.0 4.0 copy.142
  113.0 3.6 copy.216
  116.5 9.7 %all-to-all-done.4 = bf16[256,2,2048]{2,0,1:T(8,128)(2,1)} async-done(((bf16[256,2,2048]{2,0,1:T(8,128)(2,1)}), bf16[256,2,2048]{2,0,1:T(8,128)(2,1)}, u32[]{:S(2)}, u32[]{:S(2)}) %all-to-all-start.4) | async-done | bytes 2097184 | tf_op jit(solution)/shard_map/all_to_all | solution.py:166
  132.8 12.9 %fusion.36 = (f32[16,512]{1,0:T(8,128)S(1)}, f32[16,512,512]{1,2,0:T(8,128)}) fusion(pred[512,512]{0,1:T(8,128)(4,1)S(1)} %fusion.46, bf16[512,16,128]{2,1,0:T(8,128)(2,1)} %bitcast.159, bf16[512,16,128]{2,1,0:T(8,128)(2,1)} %bitcast.143), kind=kOutput, calls=%fused_computation.64 | convolution fusion | flops 1086316544 | bytes 21266432 | tf_op jit(solution)/shard_map/qhd,khd->hqk/dot_general | solution.py:16
  145.7 9.8 %exponential_reduce_fusion = f32[16,512]{1,0:T(8,128)} fusion(f32[16,512,512]{1,2,0:T(8,128)} %get-tuple-element.570, f32[16,512]{1,0:T(8,128)S(1)} %get-tuple-element.569, pred[512,512]{0,1:T(8,128)(4,1)S(1)} %fusion.46), kind=kLoop, calls=%fused_computation.61 | loop fusion | flops 16769024 | bytes 17104896 | tf_op jit(solution)/shard_map/reduce_sum | solution.py:196
  157.4 13.1 %all-gather.3.cloned.1.call-done = bf16[256,2048]{1,0:T(8,128)(2,1)} async-done(((bf16[16,2048]{1,0:T(8,128)(2,1)}), bf16[256,2048]{1,0:T(8,128)(2,1)}) %all-gather.3.cloned.1.call-update) | async-done | bytes 1048592 | tf_op jit(solution)/shard_map/all_gather | solution.py:187
  176.2 5.4 %copy.158 = f32[512,16,128]{2,0,1:T(8,128)} copy(f32[512,16,128]{0,2,1:T(8,128)} %get-tuple-element.360) | data formatting | bytes 8388608 | tf_op jit(solution)/shard_map/while | solution.py:98
  181.6 12.1 %bitcast_convert_fusion = (f32[16,512,128]{2,1,0:T(8,128)S(1)}, bf16[512,16,128]{2,0,1:T(8,128)(2,1)}) fusion(f32[512,16,128]{2,0,1:T(8,128)} %copy.158, bf16[512,16,128]{2,1,0:T(8,128)(2,1)} %bitcast.165, f32[16,512,512]{1,2,0:T(8,128)} %get-tuple-element.570, f32[16,512]{1,0:T(8,128)S(1)} %get-tuple-element.891, pred[512,512]{0,1:T(8,128)(4,1)S(1)} %fusion.46), kind=kOutput, calls=%fused_computation.80 | convolution fusion | flops 1093664768 | bytes 29655040 | tf_op jit(solution)/shard_map/hqk,khd->qhd/dot_general | solution.py:211
  193.7 3.5 multiply_reduce_fusion
  204.1 4.3 copy.159
  208.4 4.3 all_to_all.125
  212.7 5.0 %all-to-all-start.3 = ((bf16[2,256,2048]{2,1,0:T(8,128)(2,1)}), bf16[2,256,2048]{2,1,0:T(8,128)(2,1)}, u32[]{:S(2)}, u32[]{:S(2)}) async-start(bf16[2,256,2048]{2,1,0:T(8,128)(2,1)} %all_to_all.125), calls=%async_computation.3 | async-start | bytes 4194304 | tf_op jit(solution)/shard_map/all_to_all | solution.py:272
  217.7 11.9 %multiply_convert_fusion.1 = bf16[16,512,512]{1,2,0:T(8,128)(2,1)} fusion(f32[16,512,512]{1,2,0:T(8,128)} %get-tuple-element.570, f32[16,512]{1,0:T(8,128)S(1)} %get-tuple-element.899, f32[16,512]{1,0:T(8,128)S(1)} %get-tuple-element.892, pred[512,512]{0,1:T(8,128)(4,1)S(1)} %fusion.46, bf16[512,16,128]{2,1,0:T(8,128)(2,1)} %bitcast.166, ...), kind=kOutput, calls=%fused_computation.59 | convolution fusion | flops 1098907648 | bytes 29687808 | tf_op jit(solution)/shard_map/qhd,khd->hqk/dot_general | solution.py:214
  229.6 5.5 %copy.171 = f32[512,16,128]{2,0,1:T(8,128)} copy(f32[512,16,128]{0,2,1:T(8,128)} %get-tuple-element.361) | data formatting | bytes 8388608 | tf_op jit(solution)/shard_map/while | solution.py:158
  235.1 7.6 %fusion.39 = bf16[512,16,128]{2,0,1:T(8,128)(2,1)S(1)} fusion(f32[512,16,128]{2,0,1:T(8,128)} %copy.171, bf16[16,512,512]{1,2,0:T(8,128)(2,1)} %multiply_convert_fusion.1, bf16[512,16,128]{2,1,0:T(8,128)(2,1)S(1)} %bitcast.160), kind=kOutput, calls=%fused_computation.70 | convolution fusion | flops 1076887552 | bytes 16777216 | tf_op jit(solution)/shard_map/hqk,khd->qhd/dot_general | solution.py:219
  246.3 5.0 %all-to-all-start.5 = ((bf16[2,256,2048]{2,1,0:T(8,128)(2,1)}), bf16[2,256,2048]{2,1,0:T(8,128)(2,1)}, u32[]{:S(2)}, u32[]{:S(2)}) async-start(bf16[2,256,2048]{2,1,0:T(8,128)(2,1)} %all_to_all.132), calls=%async_computation.5 | async-start | bytes 4194304 | tf_op jit(solution)/shard_map/all_to_all | solution.py:273
  254.0 12.4 %all-to-all-done.5 = bf16[2,256,2048]{2,1,0:T(8,128)(2,1)} async-done(((bf16[2,256,2048]{2,1,0:T(8,128)(2,1)}), bf16[2,256,2048]{2,1,0:T(8,128)(2,1)}, u32[]{:S(2)}, u32[]{:S(2)}) %all-to-all-start.5) | async-done | bytes 2097184 | tf_op jit(solution)/shard_map/all_to_all | solution.py:273
  266.4 59.3 %all-to-all-start.6 = ((bf16[256,16,128]{2,1,0:T(8,128)(2,1)}), bf16[256,16,128]{2,1,0:T(8,128)(2,1)S(1)}, u32[]{:S(2)}, u32[]{:S(2)}) async-start(bf16[256,16,128]{2,1,0:T(8,128)(2,1)} %convert_element_type.57), calls=%async_computation.6 | async-start | bytes 2097152 | tf_op jit(solution)/shard_map/all_to_all | solution.py:248
  326.8 21.8 %all-to-all-done.6 = bf16[256,16,128]{2,1,0:T(8,128)(2,1)S(1)} async-done(((bf16[256,16,128]{2,1,0:T(8,128)(2,1)}), bf16[256,16,128]{2,1,0:T(8,128)(2,1)S(1)}, u32[]{:S(2)}, u32[]{:S(2)}) %all-to-all-start.6) | async-done | bytes 1048608 | tf_op jit(solution)/shard_map/all_to_all | solution.py:248
  349.6 7.1 %all-to-all-start.8 = ((bf16[256,16,128]{2,1,0:T(8,128)(2,1)}), bf16[256,16,128]{2,1,0:T(8,128)(2,1)S(1)}, u32[]{:S(2)}, u32[]{:S(2)}) async-start(bf16[256,16,128]{2,1,0:T(8,128)(2,1)} %convert_element_type.59), calls=%async_computation.8 | async-start | bytes 2097152 | tf_op jit(solution)/shard_map/all_to_all | solution.py:251
  356.7 6.4 %fusion.73 = f32[16,512,128]{2,1,0:T(8,128)S(1)} fusion(bf16[16,512,512]{1,2,0:T(8,128)(2,1)} %multiply_convert_fusion.1, bf16[512,16,128]{2,1,0:T(8,128)(2,1)} %bitcast.144), kind=kOutput, calls=%fused_computation.115 | convolution fusion | flops 1073741824 | bytes 14680064 | tf_op jit(solution)/shard_map/hqk,qhd->khd/dot_general | solution.py:223
  368.3 4.3 all_to_all.137
  372.6 7.0 %all-to-all-done.8 = bf16[256,16,128]{2,1,0:T(8,128)(2,1)S(1)} async-done(((bf16[256,16,128]{2,1,0:T(8,128)(2,1)}), bf16[256,16,128]{2,1,0:T(8,128)(2,1)S(1)}, u32[]{:S(2)}, u32[]{:S(2)}) %all-to-all-start.8) | async-done | bytes 1048608 | tf_op jit(solution)/shard_map/all_to_all | solution.py:251
  379.6 5.1 %all-to-all-start.7 = ((bf16[2,256,2048]{2,1,0:T(8,128)(2,1)}), bf16[2,256,2048]{2,1,0:T(8,128)(2,1)}, u32[]{:S(2)}, u32[]{:S(2)}) async-start(bf16[2,256,2048]{2,1,0:T(8,128)(2,1)} %all_to_all.137), calls=%async_computation.7 | async-start | bytes 4194304 | tf_op jit(solution)/shard_map/all_to_all | solution.py:274
  384.8 11.6 %fusion.49 = f32[16,512,128]{2,1,0:T(8,128)} fusion(f32[16,512,512]{1,2,0:T(8,128)} %get-tuple-element.570, f32[16,512]{1,0:T(8,128)S(1)} %get-tuple-element.892, pred[512,512]{0,1:T(8,128)(4,1)S(1)} %fusion.46, bf16[512,16,128]{2,1,0:T(8,128)(2,1)S(1)} %bitcast.141), kind=kOutput, calls=%fused_computation.91 | convolution fusion | flops 1090519040 | bytes 23363584 | tf_op jit(solution)/shard_map/hqk,qhd->khd/dot_general | solution.py:228
  396.5 4.2 fusion.37
  403.4 4.2 all_to_all.142
  407.6 3.1 all-to-all-done.7
  410.7 3.8 all-to-all-start.9
  414.5 3.9 copy.160
  418.4 4.1 copy.184
  422.5 3.9 copy.173
  426.4 4.1 copy.185
  430.5 3.9 copy.178
  434.4 4.1 copy.186
  442.1 4.1 copy.187
  (74 shorter events, 47.9 us)
Async XLA Ops:
  10.3 30.1 %all-to-all-start.2 = ((bf16[256,2,2048]{2,0,1:T(8,128)(2,1)}), bf16[256,2,2048]{2,0,1:T(8,128)(2,1)S(1)}, u32[]{:S(2)}, u32[]{:S(2)}) async-start(bf16[256,2,2048]{2,0,1:T(8,128)(2,1)} %bitcast.154), calls=%async_computation.2 | async-start | bytes 4194304 | tf_op jit(solution)/shard_map/all_to_all | solution.py:163
  40.4 8.9 %copy-start.15 = (bf16[256,2,2048]{2,0,1:T(8,128)(2,1)}, bf16[256,2,2048]{2,0,1:T(8,128)(2,1)S(1)}, u32[]{:S(2)}) copy-start(bf16[256,2,2048]{2,0,1:T(8,128)(2,1)S(1)} %all-to-all-done.2) | copy-start | bytes 6291460
  40.4 29.5 %all-to-all-start.1 = ((bf16[256,2,2048]{0,2,1:T(8,128)(2,1)}), bf16[256,2,2048]{0,2,1:T(8,128)(2,1)}, u32[]{:S(2)}, u32[]{:S(2)}) async-start(bf16[256,2,2048]{0,2,1:T(8,128)(2,1)} %bitcast.153), calls=%async_computation.1 | async-start | bytes 4194304 | tf_op jit(solution)/shard_map/all_to_all | solution.py:164
  69.9 8.0 %copy-start.20 = (s32[1,16]{1,0:T(1,128)S(1)}, s32[1,16]{1,0:T(1,128)}, u32[]{:S(2)}) copy-start(s32[1,16]{1,0:T(1,128)} %param.17) | copy-start | bytes 196
  69.9 28.7 %all-to-all-start = ((bf16[256,2,2048]{0,2,1:T(8,128)(2,1)}), bf16[256,2,2048]{0,2,1:T(8,128)(2,1)}, u32[]{:S(2)}, u32[]{:S(2)}) async-start(bf16[256,2,2048]{0,2,1:T(8,128)(2,1)} %bitcast.151), calls=%async_computation | async-start | bytes 4194304 | tf_op jit(solution)/shard_map/all_to_all | solution.py:165
  74.8 80.7 %all-gather.5.cloned.1.call-start = ((), (), s32[]{:S(2)}) async-start(), calls=%async_computation.11 | async-start | bytes 1114112 | tf_op jit(solution)/shard_map/all_gather | solution.py:186
  77.8 20.7 %copy-start.12 = (bf16[2,256,2048]{2,1,0:T(8,128)(2,1)}, bf16[2,256,2048]{2,1,0:T(8,128)(2,1)S(1)}, u32[]{:S(2)}) copy-start(bf16[2,256,2048]{2,1,0:T(8,128)(2,1)S(1)} %copy.144) | copy-start | bytes 6291460
  79.2 24.5 %copy-start.22 = (s32[1,8,8]{2,1,0:T(8,128)S(1)}, s32[1,8,8]{2,1,0:T(8,128)}, u32[]{:S(2)}) copy-start(s32[1,8,8]{2,1,0:T(8,128)} %param.16) | copy-start | bytes 772
  98.6 27.6 %all-to-all-start.4 = ((bf16[256,2,2048]{2,0,1:T(8,128)(2,1)}), bf16[256,2,2048]{2,0,1:T(8,128)(2,1)}, u32[]{:S(2)}, u32[]{:S(2)}) async-start(bf16[256,2,2048]{2,0,1:T(8,128)(2,1)} %bitcast.150), calls=%async_computation.4 | async-start | bytes 4194304 | tf_op jit(solution)/shard_map/all_to_all | solution.py:166
  103.4 67.1 %all-gather.3.cloned.1.call-start = ((), (), s32[]{:S(2)}) async-start(), calls=%async_computation.10 | async-start | bytes 1114112 | tf_op jit(solution)/shard_map/all_gather | solution.py:187
  104.0 3.0 copy-start.13
  106.5 2.5 copy-start.11
  126.2 5.5 %copy-start.14 = (bf16[2,256,2048]{2,1,0:T(8,128)(2,1)S(1)}, bf16[2,256,2048]{2,1,0:T(8,128)(2,1)}, u32[]{:S(2)}) copy-start(bf16[2,256,2048]{2,1,0:T(8,128)(2,1)} %copy.142) | copy-start | bytes 6291460
  128.6 1.3 copy-start.7
  181.6 12.1 %copy-start.8 = (bf16[64,8,16,128]{3,2,1,0:T(8,128)(2,1)S(1)}, bf16[64,8,16,128]{3,2,1,0:T(8,128)(2,1)}, u32[]{:S(2)}) copy-start(bf16[64,8,16,128]{3,2,1,0:T(8,128)(2,1)} %copy-done.7) | copy-start | bytes 6291460
  208.4 9.3 %copy-start.9 = (bf16[64,8,16,128]{3,2,1,0:T(8,128)(2,1)S(1)}, bf16[64,8,16,128]{3,2,1,0:T(8,128)(2,1)}, u32[]{:S(2)}) copy-start(bf16[64,8,16,128]{3,2,1,0:T(8,128)(2,1)} %copy-done.7) | copy-start | bytes 6291460
  212.7 33.6 %all-to-all-start.3 = ((bf16[2,256,2048]{2,1,0:T(8,128)(2,1)}), bf16[2,256,2048]{2,1,0:T(8,128)(2,1)}, u32[]{:S(2)}, u32[]{:S(2)}) async-start(bf16[2,256,2048]{2,1,0:T(8,128)(2,1)} %all_to_all.125), calls=%async_computation.3 | async-start | bytes 4194304 | tf_op jit(solution)/shard_map/all_to_all | solution.py:272
  229.6 5.5 %copy-start.16 = (bf16[64,8,16,128]{3,2,1,0:T(8,128)(2,1)S(1)}, bf16[64,8,16,128]{3,2,1,0:T(8,128)(2,1)}, u32[]{:S(2)}) copy-start(bf16[64,8,16,128]{3,2,1,0:T(8,128)(2,1)} %copy.215) | copy-start | bytes 6291460
  246.3 79.4 %copy-start.4 = (f32[256,16,128]{2,1,0:T(8,128)S(1)}, f32[256,16,128]{2,1,0:T(8,128)}, u32[]{:S(2)}) copy-start(f32[256,16,128]{2,1,0:T(8,128)} %get-tuple-element.363) | copy-start | bytes 6291460
  246.3 20.1 %all-to-all-start.5 = ((bf16[2,256,2048]{2,1,0:T(8,128)(2,1)}), bf16[2,256,2048]{2,1,0:T(8,128)(2,1)}, u32[]{:S(2)}, u32[]{:S(2)}) async-start(bf16[2,256,2048]{2,1,0:T(8,128)(2,1)} %all_to_all.132), calls=%async_computation.5 | async-start | bytes 4194304 | tf_op jit(solution)/shard_map/all_to_all | solution.py:273
  266.4 82.2 %all-to-all-start.6 = ((bf16[256,16,128]{2,1,0:T(8,128)(2,1)}), bf16[256,16,128]{2,1,0:T(8,128)(2,1)S(1)}, u32[]{:S(2)}, u32[]{:S(2)}) async-start(bf16[256,16,128]{2,1,0:T(8,128)(2,1)} %convert_element_type.57), calls=%async_computation.6 | async-start | bytes 2097152 | tf_op jit(solution)/shard_map/all_to_all | solution.py:248
  348.6 1.0 copy-start.17
  349.6 30.0 %all-to-all-start.8 = ((bf16[256,16,128]{2,1,0:T(8,128)(2,1)}), bf16[256,16,128]{2,1,0:T(8,128)(2,1)S(1)}, u32[]{:S(2)}, u32[]{:S(2)}) async-start(bf16[256,16,128]{2,1,0:T(8,128)(2,1)} %convert_element_type.59), calls=%async_computation.8 | async-start | bytes 2097152 | tf_op jit(solution)/shard_map/all_to_all | solution.py:251
  356.7 6.5 %copy-start.18 = (bf16[256,16,128]{2,1,0:T(8,128)(2,1)S(1)}, bf16[256,16,128]{2,1,0:T(8,128)(2,1)}, u32[]{:S(2)}) copy-start(bf16[256,16,128]{2,1,0:T(8,128)(2,1)} %copy-done.17) | copy-start | bytes 3145732
  356.7 6.6 %copy-start.21 = (s32[1,16]{1,0:T(1,128)S(1)}, s32[1,16]{1,0:T(1,128)}, u32[]{:S(2)}) copy-start(s32[1,16]{1,0:T(1,128)} %param.17) | copy-start | bytes 196
  368.3 16.5 %copy-start.10 = (bf16[64,8,16,128]{3,2,1,0:T(8,128)(2,1)S(1)}, bf16[64,8,16,128]{3,2,1,0:T(8,128)(2,1)}, u32[]{:S(2)}) copy-start(bf16[64,8,16,128]{3,2,1,0:T(8,128)(2,1)} %copy-done.7) | copy-start | bytes 6291460
  379.6 31.1 %all-to-all-start.7 = ((bf16[2,256,2048]{2,1,0:T(8,128)(2,1)}), bf16[2,256,2048]{2,1,0:T(8,128)(2,1)}, u32[]{:S(2)}, u32[]{:S(2)}) async-start(bf16[2,256,2048]{2,1,0:T(8,128)(2,1)} %all_to_all.137), calls=%async_computation.7 | async-start | bytes 4194304 | tf_op jit(solution)/shard_map/all_to_all | solution.py:274
  410.7 28.9 %all-to-all-start.9 = ((bf16[2,256,2048]{2,1,0:T(8,128)(2,1)}), bf16[2,256,2048]{2,1,0:T(8,128)(2,1)S(1)}, u32[]{:S(2)}, u32[]{:S(2)}) async-start(bf16[2,256,2048]{2,1,0:T(8,128)(2,1)} %all_to_all.142), calls=%async_computation.9 | async-start | bytes 4194304 | tf_op jit(solution)/shard_map/all_to_all | solution.py:275
Sparse Core Ops, SparseCore 0:
  79.3 39.5 all-gather.4
  132.9 37.4 all-gather.2
where the time goes:
time: 459 us; the launch traced here: 453 us
  waiting for transfers between devices  127 us (28%)
  local copies, waits for them, and re-layouts  117 us (25%)
  starting transfers between devices  104 us (23%)
  matrix products  71.3 us (16%)
  other arithmetic  18.3 us (4%)
  between operations  14.7 us (3%)
    all_to_all x1, starting transfers between devices, per_device(): lax.all_to_all(key_terms.astype(jnp.bfloat16), 'seq', split_axis=0, conca...  59.3 us
    unnamed x43, local copies, waits for them, and re-layouts  39.5 us
    all_to_all x1, waiting for transfers between devices, per_device(): lax.all_to_all(key_terms.astype(jnp.bfloat16), 'seq', split_axis=0, conca...  21.8 us
    all_to_all x1, waiting for transfers between devices, per_device(): lax.all_to_all(queries, 'head', split_axis=1, concat_axis=0, tiled=True)  21.8 us
    all_to_all x1, waiting for transfers between devices, per_device(): lax.all_to_all(key_vectors, 'head', split_axis=1, concat_axis=0, tiled=True)  20.6 us
    all_to_all x1, waiting for transfers between devices, per_device(): lax.all_to_all(value_vectors, 'head', split_axis=1, concat_axis=0, tiled=...  16.2 us
    all_gather x1, waiting for transfers between devices, per_device(): lax.all_gather(own_vals, 'seq', axis=0, tiled=True)  13.1 us
    dot_general x1, matrix products, head_scores(): jnp.einsum('qhd,khd->hqk', query_heads, key_heads, preferred_element_type...  12.9 us
  transfers between devices with their start and end apart: 12, of which 10 were waited for; matrix products, arithmetic and copies ran while one was open for 31% of the time, Pallas kernels for 0%

commit v1 on v0

--- a/solution.py
+++ b/solution.py
@@ -1,14 +1,18 @@
+import functools
 import math
 
 import jax
 import jax.numpy as jnp
 from jax import lax
+from jax.experimental import pallas as pl
+from jax.experimental.pallas import tpu as pltpu
 from jax.sharding import PartitionSpec as P
 
 HD = 128
 
 
 neg_big = -1e30
+pos_big = 3e38
 
 
 def head_scores(query_heads, key_heads, factor):
@@ -277,6 +281,390 @@
     return (attention_out, query_out, key_out, value_out)
 
 
+VMEM_GRANT = 60 * 1024 * 1024
+
+
+def score_caps(extra_map, rows_here, half, group_id, stages, per_group):
+    block_count = extra_map.shape[0]
+    block_len = rows_here * 2 // block_count
+    mine = block_count // 2
+    blocks = jnp.arange(mine, dtype=jnp.int32)
+    query_blocks = half * mine + blocks
+    extra_here = lax.dynamic_slice_in_dim(extra_map, half * mine, mine, 0)
+
+    def expand(first_key_block):
+        lag = query_blocks[None, :] - (first_key_block + blocks)[:, None]
+        extra_part = lax.dynamic_slice_in_dim(extra_here, first_key_block, mine, 1).T
+        allowed = (lag == 0) | (lag == 1) | ((extra_part == 1) & (lag > 0))
+        wide = jnp.broadcast_to(allowed[:, None, :, None], (mine, block_len, mine, block_len))
+        return wide.reshape(rows_here, rows_here)
+
+    positions = jnp.arange(rows_here, dtype=jnp.int32)
+    own = expand(half * mine) & (positions[:, None] <= positions[None, :])
+    lower = expand(0) & (half == 1)
+    core = group_id % 2
+    side = (group_id // 2) % 2
+    level = group_id // 4
+    d_core = jnp.arange(2, dtype=jnp.int32)[:, None, None]
+    d_side = jnp.arange(2, dtype=jnp.int32)[None, :, None]
+    from_level = level - jnp.arange(stages, dtype=jnp.int32)[None, None, :]
+    owner = from_level * 4 + (side + d_side) % 2 * 2 + (core + d_core) % 2
+    usable = jnp.repeat(((from_level >= 0) & (owner < group_id)).reshape(-1), per_group)
+    summ = jnp.broadcast_to(usable[:, None], (usable.shape[0], rows_here))
+    return jnp.where(jnp.concatenate([own, lower, summ], axis=0), pos_big, neg_big)
+
+
+def attention_step(
+    caps_ref,
+    query_ref,
+    key_ref,
+    val_ref,
+    grad_ref,
+    lower_ref,
+    near_ref,
+    side_ref,
+    core_ref,
+    far_ref,
+    *rest,
+):
+    attn_ref, query_grad_ref, local_ref, back_ref, near_grad_ref, far_grad_ref = rest[-6:]
+    rows_here, width = query_ref.shape
+    slots, _, per_group, _ = near_ref.shape
+    part_rows = slots * per_group
+    half_rows = 2 * part_rows
+    factor = HD ** (-0.5)
+    parts = range(width // HD)
+    queries, grads, keys, vals, raws, prob_grads = [], [], [], [], [], []
+    for part in parts:
+        cols = slice(part * HD, (part + 1) * HD)
+        queries.append(query_ref[:, cols])
+        grads.append(grad_ref[:, cols])
+        for kind, (own_ref, into) in enumerate(((key_ref, keys), (val_ref, vals))):
+            into.append(
+                jnp.concatenate(
+                    [
+                        own_ref[:, cols],
+                        lower_ref[kind, :, cols],
+                        near_ref[:, kind, :, cols].reshape(part_rows, HD),
+                        side_ref[:, kind, :, cols].reshape(part_rows, HD),
+                        core_ref[:, kind, :, cols].reshape(part_rows, HD),
+                        far_ref[:, kind, :, cols].reshape(part_rows, HD),
+                    ],
+                    axis=0,
+                )
+            )
+        raws.append(
+            lax.dot_general(
+                keys[part],
+                queries[part],
+                (((1,), (1,)), ((), ())),
+                preferred_element_type=jnp.float32,
+            )
+        )
+        prob_grads.append(
+            lax.dot_general(
+                vals[part], grads[part], (((1,), (1,)), ((), ())), preferred_element_type=jnp.float32
+            )
+        )
+    for part in parts:
+        cols = slice(part * HD, (part + 1) * HD)
+        query, grad = queries[part], grads[part]
+        raw = jnp.minimum(raws[part], caps_ref[...])
+        peak = jnp.max(raw, axis=0, keepdims=True)
+        grown = jnp.exp2((raw - peak) * (factor * math.log2(math.e)))
+        probs = grown * (1.0 / jnp.sum(grown, axis=0, keepdims=True))
+        weights = probs.astype(jnp.bfloat16)
+        attn = lax.dot_general(
+            vals[part], weights, (((0,), (0,)), ((), ())), preferred_element_type=jnp.float32
+        ).astype(jnp.bfloat16)
+        attn_ref[:, cols] = attn.T
+        row_dot = jnp.sum(probs * prob_grads[part], axis=0, keepdims=True)
+        score_grads = (probs * (prob_grads[part] - row_dot)).astype(jnp.bfloat16)
+        query_grad = lax.dot_general(
+            keys[part], score_grads, (((0,), (0,)), ((), ())), preferred_element_type=jnp.float32
+        )
+        query_grad_ref[:, cols] = (query_grad * factor).astype(jnp.bfloat16).T
+        key_terms = (
+            jnp.dot(score_grads, query, preferred_element_type=jnp.float32) * factor
+        ).astype(jnp.bfloat16)
+        val_terms = jnp.dot(weights, grad, preferred_element_type=jnp.float32).astype(
+            jnp.bfloat16
+        )
+        for kind, terms in enumerate((key_terms, val_terms)):
+            local_ref[kind, :, cols] = terms[:rows_here]
+            back_ref[kind, :, cols] = terms[rows_here : 2 * rows_here]
+            first = 2 * rows_here
+            near_grad_ref[:, kind, :, cols] = terms[first : first + half_rows].reshape(
+                2 * slots, per_group, HD
+            )
+            far_grad_ref[:, kind, :, cols] = terms[first + half_rows :].reshape(
+                2 * slots, per_group, HD
+            )
+
+
+def attention_call(
+    caps,
+    full,
+    lower,
+    summaries,
+    first_col,
+    summ_col,
+    wide_done,
+    round_width,
+    round_col,
+    round_done,
+    after,
+):
+    rows_here, total_width = full[0].shape
+    width = lower.shape[2]
+    tile = math.gcd(width, 2 * HD)
+    slots, _, per_group, _ = summaries[0].shape
+    first = first_col // tile
+    summ_first = summ_col // tile
+    round_first = round_col // tile
+    wide_spec = pl.BlockSpec((rows_here, tile), lambda i: (0, first + i))
+    pair_spec = pl.BlockSpec((2, rows_here, tile), lambda i: (0, 0, i))
+    summ_in = pl.BlockSpec((slots, 2, per_group, tile), lambda i: (0, 0, 0, summ_first + i))
+    summ_out = pl.BlockSpec((2 * slots, 2, per_group, tile), lambda i: (0, 0, 0, round_first + i))
+    wide = jax.ShapeDtypeStruct((rows_here, total_width), jnp.bfloat16)
+    pair = jax.ShapeDtypeStruct((2, rows_here, width), jnp.bfloat16)
+    summ = jax.ShapeDtypeStruct((2 * slots, 2, per_group, round_width), jnp.bfloat16)
+    keys = caps.shape[0]
+    heads = width // HD
+    ahead = 6 + len(summaries)
+    aliases = {ahead + i: i for i in range(len(wide_done))}
+    aliases.update({ahead + len(wide_done) + i: 4 + i for i in range(len(round_done))})
+    return pl.pallas_call(
+        attention_step,
+        grid=(width // tile,),
+        in_specs=[pl.BlockSpec(caps.shape, lambda i: (0, 0))]
+        + [wide_spec] * 4
+        + [pair_spec]
+        + [summ_in] * len(summaries)
+        + [pl.BlockSpec(memory_space=pl.ANY)] * (len(aliases) + len(after)),
+        out_specs=[wide_spec, wide_spec, pair_spec, pair_spec, summ_out, summ_out],
+        out_shape=[wide, wide, pair, pair, summ, summ],
+        input_output_aliases=aliases,
+        compiler_params=pltpu.CompilerParams(vmem_limit_bytes=VMEM_GRANT),
+        cost_estimate=pl.CostEstimate(
+            flops=56 * heads * keys * rows_here * HD,
+            bytes_accessed=heads * 16 * 2 * rows_here * HD,
+            transcendentals=heads * keys * rows_here,
+        ),
+    )(caps, *full, lower, *summaries, *wide_done, *round_done, *after)
+
+
+def finish_step(picker_ref, local_ref, back_ref, summ_ref, *rest):
+    picker = picker_ref[...]
+    for kind, out_ref in enumerate(rest[-2:]):
+        spread = lax.dot_general(
+            picker, summ_ref[kind], (((0,), (0,)), ((), ())), preferred_element_type=jnp.float32
+        )
+        total = local_ref[kind].astype(jnp.float32) + back_ref[kind].astype(jnp.float32)
+        out_ref[...] = (total + spread).astype(jnp.bfloat16)
+
+
+def finish_call(picker, local, back, summ, first_col, summ_col, total_width, carried):
+    _, rows_here, width = local.shape
+    tile = math.gcd(width, 4 * HD)
+    first = first_col // tile
+    summ_first = summ_col // tile
+    few = summ.shape[1]
+    pair_spec = pl.BlockSpec((2, rows_here, tile), lambda i: (0, 0, i))
+    wide_spec = pl.BlockSpec((rows_here, tile), lambda i: (0, first + i))
+    wide = jax.ShapeDtypeStruct((rows_here, total_width), jnp.bfloat16)
+    any_spec = pl.BlockSpec(memory_space=pl.ANY)
+    return pl.pallas_call(
+        finish_step,
+        grid=(width // tile,),
+        in_specs=[
+            pl.BlockSpec(picker.shape, lambda i: (0, 0)),
+            pair_spec,
+            pair_spec,
+            pl.BlockSpec((2, few, tile), lambda i: (0, 0, summ_first + i)),
+        ]
+        + [any_spec] * len(carried),
+        out_specs=[wide_spec, wide_spec],
+        out_shape=[wide, wide],
+        input_output_aliases={4 + i: i for i in range(len(carried))},
+        compiler_params=pltpu.CompilerParams(vmem_limit_bytes=VMEM_GRANT),
+        cost_estimate=pl.CostEstimate(
+            flops=4 * few * rows_here * width,
+            bytes_accessed=6 * 2 * rows_here * width,
+            transcendentals=0,
+        ),
+    )(picker, local, back, summ, *carried)
+
+
+def pick_step(picker_ref, key_ref, val_ref, out_ref):
+    picker = picker_ref[...]
+    for kind, ref in enumerate((key_ref, val_ref)):
+        rows = jnp.dot(picker, ref[...], preferred_element_type=jnp.float32)
+        out_ref[kind] = rows.astype(jnp.bfloat16)
+
+
+def pick_call(picker, key_vectors, value_vectors):
+    rows_here, total_width = key_vectors.shape
+    few = picker.shape[0]
+    tile = math.gcd(total_width, 8 * HD)
+    wide_spec = pl.BlockSpec((rows_here, tile), lambda i: (0, i))
+    return pl.pallas_call(
+        pick_step,
+        grid=(total_width // tile,),
+        in_specs=[pl.BlockSpec(picker.shape, lambda i: (0, 0)), wide_spec, wide_spec],
+        out_specs=pl.BlockSpec((2, few, tile), lambda i: (0, 0, i)),
+        out_shape=jax.ShapeDtypeStruct((2, few, total_width), jnp.bfloat16),
+        compiler_params=pltpu.CompilerParams(vmem_limit_bytes=VMEM_GRANT),
+    )(picker, key_vectors, value_vectors)
+
+
+def wait_for(array, other):
+    zero = jnp.minimum(jnp.abs(other[(0,) * other.ndim].astype(jnp.float32)), 0.0)
+    return array + zero.astype(array.dtype)
+
+
+def add_rounded(*terms):
+    total = terms[0].astype(jnp.float32)
+    for term in terms[1:]:
+        total = total + term.astype(jnp.float32)
+    return total.astype(jnp.bfloat16)
+
+
+def token_split(queries, key_vectors, value_vectors, out_grads, extra_blocks, summary_rows):
+    rows_here, total_width = queries.shape
+    seq_count = lax.axis_size("seq")
+    stages = seq_count // 4
+    group_id = lax.axis_index("seq")
+    half = lax.axis_index("head")
+    per_group = summary_rows.shape[1]
+    few = per_group // 2
+    flip_core = [(i, i ^ 1) for i in range(seq_count)]
+    flip_side = [(i, i ^ 2) for i in range(seq_count)]
+    flip_half = [(0, 1), (1, 0)]
+
+    def climb(step):
+        return [(i, i + 4 * step) for i in range(seq_count - 4 * step)]
+
+    def descend(step):
+        return [(i + 4 * step, i) for i in range(seq_count - 4 * step)]
+
+    rows_mine = lax.dynamic_slice_in_dim(summary_rows[0], half * few, few, 0) - half * rows_here
+    picker = (
+        rows_mine[:, None] == jnp.arange(rows_here, dtype=jnp.int32)[None, :]
+    ).astype(jnp.bfloat16)
+
+    unit = total_width // 8
+    chunks = [1, 2, 2, 2, 1]
+    gather_rounds = [(0, 2), (2, 5)]
+    reduce_rounds = [(0, 2), (2, 4), (4, 5)]
+    edges = [sum(chunks[:i]) for i in range(len(chunks) + 1)]
+
+    mine = pick_call(picker, key_vectors, value_vectors)
+    other = lax.ppermute(mine, "head", flip_half)
+
+    def lower_pair(chunk):
+        cols = slice(edges[chunk] * unit, edges[chunk + 1] * unit)
+        pair = jnp.stack([key_vectors[:, cols], value_vectors[:, cols]])
+        return lax.ppermute(pair, "head", [(0, 1)])
+
+    def gather(first, last, after, direct):
+        cols = slice(edges[first] * unit, edges[last] * unit)
+        ladder = jnp.concatenate([mine[:, :, cols], other[:, :, cols]], axis=1)[None]
+        for item in after:
+            ladder = wait_for(ladder, item)
+        if direct:
+            ladder = jnp.concatenate(
+                [ladder] + [lax.ppermute(ladder, "seq", climb(i)) for i in range(1, stages)],
+                axis=0,
+            )
+        size = ladder.shape[0]
+        while size < stages:
+            more = min(size, stages - size)
+            ladder = jnp.concatenate(
+                [ladder, lax.ppermute(ladder[:more], "seq", climb(size))], axis=0
+            )
+            size += more
+        side = lax.ppermute(ladder, "seq", flip_side)
+        return (
+            ladder,
+            side,
+            lax.ppermute(ladder, "seq", flip_core),
+            lax.ppermute(side, "seq", flip_core),
+        )
+
+    def reduce(near_grad, far_grad):
+        chip = add_rounded(near_grad, lax.ppermute(far_grad, "seq", flip_core))
+        plane = add_rounded(chip[:stages], lax.ppermute(chip[stages:], "seq", flip_side))
+        sizes = [1]
+        while sizes[-1] < stages:
+            sizes.append(min(2 * sizes[-1], stages))
+        for size, wider in zip(sizes[-2::-1], sizes[:0:-1]):
+            more = wider - size
+            moved = lax.ppermute(plane[size:wider], "seq", descend(size))
+            head_part = add_rounded(plane[:more], moved)
+            plane = (
+                head_part
+                if more == size
+                else jnp.concatenate([head_part, plane[more:size]], axis=0)
+            )
+        group = plane[0]
+        return add_rounded(group[:, :few], lax.ppermute(group[:, few:], "head", flip_half))
+
+    caps = score_caps(extra_blocks[0], rows_here, half, group_id, stages, per_group)
+    full = (queries, key_vectors, value_vectors, out_grads)
+
+    lowers = [lower_pair(chunk) for chunk in range(len(chunks))]
+    gathered = {}
+    wide_done = ()
+    finished = ()
+    waiting = []
+    backs = []
+    summs = []
+    for first, last in reduce_rounds:
+        round_done = ()
+        round_width = (edges[last] - edges[first]) * unit
+        for chunk in range(first, last):
+            if chunk == 0:
+                gathered[0] = gather(*gather_rounds[0], (), True)
+                begin, end = gather_rounds[1]
+                gathered[begin] = gather(begin, end, (gathered[0][0],), False)
+            gather_first = max(begin for begin in gathered if begin <= chunk)
+            after = ((lowers[1],), (), backs[:1], backs[1:2], ())[chunk]
+            out = attention_call(
+                caps,
+                full,
+                lowers[chunk],
+                gathered[gather_first],
+                edges[chunk] * unit,
+                (edges[chunk] - edges[gather_first]) * unit,
+                wide_done,
+                round_width,
+                (edges[chunk] - edges[first]) * unit,
+                round_done,
+                after,
+            )
+            wide_done = tuple(out[:2])
+            round_done = tuple(out[4:])
+            back = lax.ppermute(out[3], "head", [(1, 0)])
+            backs.append(back)
+            waiting.append((chunk, out[2], back))
+        summ = reduce(*round_done)
+        summs.append(summ)
+        for chunk, local, back in waiting:
+            finished = finish_call(
+                picker,
+                local,
+                back,
+                summ,
+                edges[chunk] * unit,
+                (edges[chunk] - edges[first]) * unit,
+                total_width,
+                finished,
+            )
+        waiting = []
+    return (*wide_done, *finished)
+
+
 def solution(mesh):
     placed = (
         P(("seq", "head"), None),
@@ -286,8 +674,9 @@
         P("seq", None, None),
         P("seq", None),
     )
+    paired = mesh.shape["head"] == 2 and mesh.shape["seq"] % 4 == 0
     return jax.shard_map(
-        per_device,
+        token_split if paired else per_device,
         mesh=mesh,
         in_specs=placed,
         out_specs=(

time: 459 us -> 230 us (0.50)
  local copies, waits for them, and re-layouts: 117 us -> 13.2 us
  matrix products: 71.3 us -> 0 us
  Pallas kernels: 0 us -> 59.9 us
  waiting for transfers between devices: 127 us -> 75.9 us
  starting transfers between devices: 104 us -> 64.1 us
  between operations: 14.7 us -> 2.02 us
  other arithmetic: 18.3 us -> 13.3 us
    all_to_all x10 -> x0, waiting for transfers between devices: 114 us -> none  [the longest x1 21.8 us: per_device(): lax.all_to_all(key_terms.astype(jnp.bfloat16), 'seq', split_axis=0, conca...]
    all_to_all x10 -> x0, starting transfers between devices: 104 us -> none  [the longest x1 59.3 us: per_device(): lax.all_to_all(key_terms.astype(jnp.bfloat16), 'seq', split_axis=0, conca...]
    ppermute x0 -> x37, waiting for transfers between devices: none -> 75.9 us  [the longest x5 31.2 us: lower_pair(): return lax.ppermute(pair, 'head', [(0, 1)])]
    dot_general x10 -> x0, matrix products: 71.3 us -> none  [the longest x1 12.9 us: head_scores(): jnp.einsum('qhd,khd->hqk', query_heads, key_heads, preferred_element_type...]
    ppermute x0 -> x37, starting transfers between devices: none -> 64.1 us  [the longest x5 14.1 us: lower_pair(): return lax.ppermute(pair, 'head', [(0, 1)])]
    pallas_call x0 -> x11, Pallas kernels: none -> 59.9 us  [the longest x5 43.2 us: attention_call(): pl.pallas_call(attention_step, grid=(width // tile,), in_specs=[pl.BlockS...]
    all_to_all x12 -> x0, local copies, waits for them, and re-layouts: 42.7 us -> none  [the longest x2 8.24 us: per_device(): lax.all_to_all(outputs[0], 'head', split_axis=0, concat_axis=1, tiled=True)]
    unnamed x43 -> x37, local copies, waits for them, and re-layouts: 39.5 us -> 5.55 us
  transfers between devices with their start and end apart: 12 -> 37, of which waited for: 10 -> 13; matrix products, arithmetic and copies ran while one was open for 31% -> 9% of each run, Pallas kernels for 0% -> 23%
where the time goes in v1:
time: 230 us; the launch traced here: 228 us
  waiting for transfers between devices  75.9 us (33%)
  starting transfers between devices  64.1 us (28%)
  Pallas kernels  59.9 us (26%)
  other arithmetic  13.3 us (6%)
  local copies, waits for them, and re-layouts  13.2 us (6%)
    pallas_call x5, Pallas kernels, attention_call(): pl.pallas_call(attention_step, grid=(width // tile,), in_specs=[pl.BlockS...  43.2 us
    ppermute x5, waiting for transfers between devices, lower_pair(): return lax.ppermute(pair, 'head', [(0, 1)])  31.2 us
    ppermute x6, waiting for transfers between devices, reduce(): moved = lax.ppermute(plane[size:wider], 'seq', descend(size))  27.6 us
    ppermute x5, starting transfers between devices, lower_pair(): return lax.ppermute(pair, 'head', [(0, 1)])  14.1 us
    pallas_call x5, Pallas kernels, finish_call(): pl.pallas_call(finish_step, grid=(width // tile,), in_specs=[pl.BlockSpec...  12.3 us
    ppermute x3, waiting for transfers between devices, reduce(): lax.ppermute(chip[stages:], 'seq', flip_side)  10.6 us
    ppermute x3, starting transfers between devices, gather(): lax.ppermute(ladder, 'seq', climb(i))  9.73 us
    ppermute x2, starting transfers between devices, gather(): lax.ppermute(ladder[:more], 'seq', climb(size))  9.11 us
  transfers between devices with their start and end apart: 37, of which 13 were waited for; matrix products, arithmetic and copies ran while one was open for 9% of the time, Pallas kernels for 23%

profile of v1, /device:TPU:0, one launch (start us, length us, event | category | flops | bytes accessed | tf_op | source)
XLA Modules:
  0.0 228.5 jit_solution(10179381557461130973)
XLA Ops:
  2.0 4.4 %shard_map.93 = bf16[2,8,4096]{2,1,0:T(8,128)(2,1)} custom-call(bf16[8,256]{1,0:T(8,128)(2,1)} %fusion.4.picker_ref, bf16[256,4096]{1,0:T(8,128)(2,1)} %key_ref.11, bf16[256,4096]{1,0:T(8,128)(2,1)} %val_ref.11), custom_call_target="tpu_custom_call" | custom-call | tf_op jit(solution)/shard_map/pallas_call | solution.py:511
  6.4 3.0 %collective-permute-start.1 = (bf16[2,8,4096]{2,1,0:T(8,128)(2,1)}, bf16[2,8,4096]{2,1,0:T(8,128)(2,1)}, u32[]{:S(2)}, u32[]{:S(2)}) collective-permute-start(bf16[2,8,4096]{2,1,0:T(8,128)(2,1)} %shard_map.93), channel_id=1, source_target_pairs={{0,1},{1,0},{2,3},{3,2},{4,5},{5,4},{6,7},{7,6},{8,9},{9,8},{10,11... | collective-permute-start | bytes 393224 | tf_op jit(solution)/shard_map/ppermute | solution.py:563
  9.4 1.8 slice_bitcast_fusion.6
  12.0 2.9 %collective-permute-start.16 = (bf16[2,256,512]{2,1,0:T(8,128)(2,1)}, bf16[2,256,512]{2,1,0:T(8,128)(2,1)}, u32[]{:S(2)}, u32[]{:S(2)}) collective-permute-start(bf16[2,256,512]{2,1,0:T(8,128)(2,1)} %pad_maximum_fusion.5), channel_id=1, source_target_pairs={{0,1},{2,3},{4,5},{6,7},{8,9},{10,11},{12,13},{14,15},{16,17},{18,... | collective-permute-start | bytes 1572872 | tf_op jit(solution)/shard_map/ppermute | solution.py:568
  16.2 2.3 %collective-permute-start.9 = (bf16[2,256,1024]{2,1,0:T(8,128)(2,1)S(1)}, bf16[2,256,1024]{2,1,0:T(8,128)(2,1)}, u32[]{:S(2)}, u32[]{:S(2)}) collective-permute-start(bf16[2,256,1024]{2,1,0:T(8,128)(2,1)S(1)} %pad_maximum_fusion.2), channel_id=1, source_target_pairs={{0,1},{2,3},{4,5},{6,7},{8,9},{10,11},{12,13},{14,15},{16,17},{18,... | collective-permute-start | bytes 3145736 | tf_op jit(solution)/shard_map/ppermute | solution.py:568
  21.2 6.0 %collective-permute-start.12 = (bf16[1,2,16,1536]{3,2,1,0:T(8,128)(2,1)S(1)}, bf16[1,2,16,1536]{3,2,1,0:T(8,128)(2,1)S(1)}, u32[]{:S(2)}, u32[]{:S(2)}) collective-permute-start(bf16[1,2,16,1536]{3,2,1,0:T(8,128)(2,1)S(1)} %maximum_bitcast_fusion), channel_id=1, source_target_pairs={{0,24},{2,26},{4,28},{6,30},{1,25},{3,27},{5,29},{7,31}} | collective-permute-start | bytes 294920 | tf_op jit(solution)/shard_map/ppermute | solution.py:577
  27.2 1.3 collective-permute-start.11
  28.5 2.5 %collective-permute-start.10 = (bf16[1,2,16,1536]{3,2,1,0:T(8,128)(2,1)S(1)}, bf16[1,2,16,1536]{3,2,1,0:T(8,128)(2,1)S(1)}, u32[]{:S(2)}, u32[]{:S(2)}) collective-permute-start(bf16[1,2,16,1536]{3,2,1,0:T(8,128)(2,1)S(1)} %maximum_bitcast_fusion), channel_id=1, source_target_pairs={{0,8},{2,10},{4,12},{6,14},{8,16},{10,18},{12,20},{14,22},{16,24},... | collective-permute-start | bytes 294920 | tf_op jit(solution)/shard_map/ppermute | solution.py:577
  32.6 1.9 collective-permute-start.2
  35.3 1.5 collective-permute-start.13
  38.1 7.2 %collective-permute-start.3 = (bf16[2,2,16,2560]{3,2,1,0:T(8,128)(2,1)}, bf16[2,2,16,2560]{3,2,1,0:T(8,128)(2,1)}, u32[]{:S(2)}, u32[]{:S(2)}) collective-permute-start(bf16[2,2,16,2560]{3,2,1,0:T(8,128)(2,1)} %pad_maximum_fusion.7), channel_id=1, source_target_pairs={{0,16},{2,18},{4,20},{6,22},{8,24},{10,26},{12,28},{14,30},{1,17},... | collective-permute-start | bytes 983048 | tf_op jit(solution)/shard_map/ppermute | solution.py:584
  47.6 4.2 %collective-permute-done.3 = bf16[2,2,16,2560]{3,2,1,0:T(8,128)(2,1)} collective-permute-done((bf16[2,2,16,2560]{3,2,1,0:T(8,128)(2,1)}, bf16[2,2,16,2560]{3,2,1,0:T(8,128)(2,1)}, u32[]{:S(2)}, u32[]{:S(2)}) %collective-permute-start.3) | collective-permute-done | bytes 327712 | tf_op jit(solution)/shard_map/ppermute | solution.py:584
  51.9 1.9 pad_maximum_fusion.3.near_ref
  53.7 1.5 collective-permute-start.4
  56.0 6.3 %shard_map.94 = (bf16[256,4096]{1,0:T(8,128)(2,1)}, bf16[256,4096]{1,0:T(8,128)(2,1)}, bf16[2,256,512]{2,1,0:T(8,128)(2,1)}, bf16[2,256,512]{2,1,0:T(8,128)(2,1)...) custom-call(f32[768,256]{1,0:T(8,128)} %add_select_fusion.caps_ref, bf16[256,4096]{1,0:T(8,128)(2,1)} %query_ref.9, ...), custom_call_target="tpu_custom_call" | custom-call | flops 5637144576 | bytes 4194304 | tf_op jit(solution)/shard_map/pallas_call | solution.py:437
  62.3 10.2 %shard_map.95 = (bf16[256,4096]{1,0:T(8,128)(2,1)}, bf16[256,4096]{1,0:T(8,128)(2,1)}, bf16[2,256,1024]{2,1,0:T(8,128)(2,1)}, bf16[2,256,1024]{2,1,0:T(8,128)(2,...) custom-call(f32[768,256]{1,0:T(8,128)} %add_select_fusion.caps_ref, ...), custom_call_target="tpu_custom_call", output_to_operand_aliasing={{0}: (10, {}), {1}: (11, {}), {4}: (12, {}), {5}: (13, {})} | custom-call | flops 11274289152 | bytes 8388608 | tf_op jit(solution)/shard_map/pallas_call | solution.py:437
  72.7 1.5 collective-permute-start.8
  75.1 2.1 collective-permute-start
  77.8 1.3 collective-permute-start.17
  80.2 17.5 %collective-permute-done.8.lower_ref = bf16[2,256,1024]{2,1,0:T(8,128)(2,1)S(1)} collective-permute-done((bf16[2,256,1024]{2,1,0:T(8,128)(2,1)S(1)}, bf16[2,256,1024]{2,1,0:T(8,128)(2,1)S(1)}, u32[]{:S(2)}, u32[]{:S(2)}) %collective-permute-start.8) | collective-permute-done | bytes 1048608 | tf_op jit(solution)/shard_map/ppermute | solution.py:568
  97.7 5.4 %collective-permute-start.7 = (bf16[2,256,1024]{2,1,0:T(8,128)(2,1)S(1)}, bf16[2,256,1024]{2,1,0:T(8,128)(2,1)}, u32[]{:S(2)}, u32[]{:S(2)}) collective-permute-start(bf16[2,256,1024]{2,1,0:T(8,128)(2,1)S(1)} %pad_maximum_fusion), channel_id=1, source_target_pairs={{0,1},{2,3},{4,5},{6,7},{8,9},{10,11},{12,13},{14,15},{16,17},{18,... | collective-permute-start | bytes 3145736 | tf_op jit(solution)/shard_map/ppermute | solution.py:568
  105.9 10.1 %shard_map.96 = (bf16[256,4096]{1,0:T(8,128)(2,1)}, bf16[256,4096]{1,0:T(8,128)(2,1)}, bf16[2,256,1024]{2,1,0:T(8,128)(2,1)}, bf16[2,256,1024]{2,1,0:T(8,128)(2,...) custom-call(f32[768,256]{1,0:T(8,128)} %add_select_fusion.caps_ref, ...), custom_call_target="tpu_custom_call", output_to_operand_aliasing={{0}: (10, {}), {1}: (11, {})} | custom-call | flops 11274289152 | bytes 8388608 | tf_op jit(solution)/shard_map/pallas_call | solution.py:437
  116.0 1.5 collective-permute-start.31
  117.5 13.7 %collective-permute-done.7.lower_ref = bf16[2,256,1024]{2,1,0:T(8,128)(2,1)} collective-permute-done((bf16[2,256,1024]{2,1,0:T(8,128)(2,1)S(1)}, bf16[2,256,1024]{2,1,0:T(8,128)(2,1)}, u32[]{:S(2)}, u32[]{:S(2)}) %collective-permute-start.7) | collective-permute-done | bytes 1048608 | tf_op jit(solution)/shard_map/ppermute | solution.py:568
  132.3 10.2 %shard_map.97 = (bf16[256,4096]{1,0:T(8,128)(2,1)}, bf16[256,4096]{1,0:T(8,128)(2,1)}, bf16[2,256,1024]{2,1,0:T(8,128)(2,1)}, bf16[2,256,1024]{2,1,0:T(8,128)(2,...) custom-call(f32[768,256]{1,0:T(8,128)} %add_select_fusion.caps_ref, ...), custom_call_target="tpu_custom_call", output_to_operand_aliasing={{0}: (10, {}), {1}: (11, {}), {4}: (12, {}), {5}: (13, {})} | custom-call | flops 11274289152 | bytes 8388608 | tf_op jit(solution)/shard_map/pallas_call | solution.py:437
  142.5 6.4 %shard_map.98 = (bf16[256,4096]{1,0:T(8,128)(2,1)}, bf16[256,4096]{1,0:T(8,128)(2,1)}, bf16[2,256,512]{2,1,0:T(8,128)(2,1)}, bf16[2,256,512]{2,1,0:T(8,128)(2,1)...) custom-call(f32[768,256]{1,0:T(8,128)} %add_select_fusion.caps_ref, ...), custom_call_target="tpu_custom_call", output_to_operand_aliasing={{0}: (10, {}), {1}: (11, {})} | custom-call | flops 5637144576 | bytes 4194304 | tf_op jit(solution)/shard_map/pallas_call | solution.py:437
  149.0 1.4 collective-permute-start.19
  150.4 1.3 collective-permute-start.25
  153.2 1.3 collective-permute-start.34
  155.6 7.6 %collective-permute-done.34 = bf16[2,2,16,1536]{3,2,1,0:T(8,128)(2,1)S(1)} collective-permute-done((bf16[2,2,16,1536]{3,2,1,0:T(8,128)(2,1)S(1)}, bf16[2,2,16,1536]{3,2,1,0:T(8,128)(2,1)S(1)}, u32[]{:S(2)}, u32[]{:S(2)}) %collective-permute-start.34) | collective-permute-done | bytes 196640 | tf_op jit(solution)/shard_map/ppermute | solution.py:603
  163.8 4.4 %collective-permute-done.21 = bf16[4,2,16,512]{3,2,1,0:T(8,128)(2,1)S(1)} collective-permute-done((bf16[4,2,16,512]{3,2,1,0:T(8,128)(2,1)S(1)}, bf16[4,2,16,512]{3,2,1,0:T(8,128)(2,1)S(1)}, u32[]{:S(2)}, u32[]{:S(2)}) %collective-permute-start.21) | collective-permute-done | bytes 131104 | tf_op jit(solution)/shard_map/ppermute | solution.py:597
  169.5 1.3 collective-permute-start.22
  171.3 6.8 %collective-permute-done.35 = bf16[1,2,16,1536]{3,2,1,0:T(8,128)(2,1)S(1)} collective-permute-done((bf16[1,2,16,1536]{3,2,1,0:T(8,128)(2,1)S(1)}, bf16[1,2,16,1536]{3,2,1,0:T(8,128)(2,1)S(1)}, u32[]{:S(2)}, u32[]{:S(2)}) %collective-permute-start.35) | collective-permute-done | bytes 98336 | tf_op jit(solution)/shard_map/ppermute | solution.py:603
  178.7 1.6 collective-permute-done.22
  180.3 2.7 %collective-permute-start.36 = (bf16[2,8,1536]{2,1,0:T(8,128)(2,1)S(1)}, bf16[2,8,1536]{2,1,0:T(8,128)(2,1)S(1)}, u32[]{:S(2)}, u32[]{:S(2)}) collective-permute-start(bf16[2,8,1536]{2,1,0:T(8,128)(2,1)S(1)} %slice.184), channel_id=1, source_target_pairs={{0,1},{1,0},{2,3},{3,2},{4,5},{5,4},{6,7},{7,6},{8,9},{9,8},{10,11... | collective-permute-start | bytes 147464 | tf_op jit(solution)/shard_map/ppermute | solution.py:611
  183.0 6.2 %collective-permute-done.27 = bf16[4,2,16,2048]{3,2,1,0:T(8,128)(2,1)S(1)} collective-permute-done((bf16[4,2,16,2048]{3,2,1,0:T(8,128)(2,1)S(1)}, bf16[4,2,16,2048]{3,2,1,0:T(8,128)(2,1)S(1)}, u32[]{:S(2)}, u32[]{:S(2)}) %collective-permute-start.27) | collective-permute-done | bytes 524320 | tf_op jit(solution)/shard_map/ppermute | solution.py:597
  190.7 1.3 collective-permute-start.28
  192.6 2.3 shard_map.99
  194.9 2.6 %shard_map.100 = (bf16[256,4096]{1,0:T(8,128)(2,1)}, bf16[256,4096]{1,0:T(8,128)(2,1)}) custom-call(bf16[8,256]{1,0:T(8,128)(2,1)} %fusion.4.picker_ref, bf16[2,256,1024]{2,1,0:T(8,128)(2,1)} %get-tuple-element.70.local_ref, bf16[2,256,1024]{2,1,0:T(8,128)(2,1)} %copy-done.6, ...), custom_call_target="tpu_custom_call", output_to_operand_aliasing={{0}: (4, {}), {1}: (5, {})} | custom-call | flops 8388608 | bytes 3145728 | tf_op jit(solution)/shard_map/pallas_call | solution.py:477
  197.5 8.5 %collective-permute-done.28 = bf16[2,2,16,2048]{3,2,1,0:T(8,128)(2,1)S(1)} collective-permute-done((bf16[2,2,16,2048]{3,2,1,0:T(8,128)(2,1)S(1)}, bf16[2,2,16,2048]{3,2,1,0:T(8,128)(2,1)S(1)}, u32[]{:S(2)}, u32[]{:S(2)}) %collective-permute-start.28) | collective-permute-done | bytes 262176 | tf_op jit(solution)/shard_map/ppermute | solution.py:603
  206.0 1.3 collective-permute-start.29
  207.4 2.3 %collective-permute-start.24 = (bf16[2,8,512]{2,1,0:T(8,128)(2,1)S(1)}, bf16[2,8,512]{2,1,0:T(8,128)(2,1)S(1)}, u32[]{:S(2)}, u32[]{:S(2)}) collective-permute-start(bf16[2,8,512]{2,1,0:T(8,128)(2,1)S(1)} %slice.168), channel_id=1, source_target_pairs={{0,1},{1,0},{2,3},{3,2},{4,5},{5,4},{6,7},{7,6},{8,9},{9,8},{10,11... | collective-permute-start | bytes 49160 | tf_op jit(solution)/shard_map/ppermute | solution.py:611
  209.7 3.2 %collective-permute-done.29 = bf16[1,2,16,2048]{3,2,1,0:T(8,128)(2,1)S(1)} collective-permute-done((bf16[1,2,16,2048]{3,2,1,0:T(8,128)(2,1)S(1)}, bf16[1,2,16,2048]{3,2,1,0:T(8,128)(2,1)S(1)}, u32[]{:S(2)}, u32[]{:S(2)}) %collective-permute-start.29) | collective-permute-done | bytes 131104 | tf_op jit(solution)/shard_map/ppermute | solution.py:603
  212.9 2.3 %collective-permute-start.30 = (bf16[2,8,2048]{2,1,0:T(8,128)(2,1)S(1)}, bf16[2,8,2048]{2,1,0:T(8,128)(2,1)S(1)}, u32[]{:S(2)}, u32[]{:S(2)}) collective-permute-start(bf16[2,8,2048]{2,1,0:T(8,128)(2,1)S(1)} %slice.176), channel_id=1, source_target_pairs={{0,1},{1,0},{2,3},{3,2},{4,5},{5,4},{6,7},{7,6},{8,9},{9,8},{10,11... | collective-permute-start | bytes 196616 | tf_op jit(solution)/shard_map/ppermute | solution.py:611
  215.9 1.6 collective-permute-done.30
  219.2 2.6 %shard_map.101 = (bf16[256,4096]{1,0:T(8,128)(2,1)}, bf16[256,4096]{1,0:T(8,128)(2,1)}) custom-call(bf16[8,256]{1,0:T(8,128)(2,1)} %fusion.4.picker_ref, bf16[2,256,1024]{2,1,0:T(8,128)(2,1)} %get-tuple-element.68.local_ref, bf16[2,256,1024]{2,1,0:T(8,128)(2,1)} %copy-done.4, ...), custom_call_target="tpu_custom_call", output_to_operand_aliasing={{0}: (4, {}), {1}: (5, {})} | custom-call | flops 8388608 | bytes 3145728 | tf_op jit(solution)/shard_map/pallas_call | solution.py:477
  222.8 2.6 %shard_map.102 = (bf16[256,4096]{1,0:T(8,128)(2,1)}, bf16[256,4096]{1,0:T(8,128)(2,1)}) custom-call(bf16[8,256]{1,0:T(8,128)(2,1)} %fusion.4.picker_ref, bf16[2,256,1024]{2,1,0:T(8,128)(2,1)} %get-tuple-element.64.local_ref, bf16[2,256,1024]{2,1,0:T(8,128)(2,1)} %copy-done.5, ...), custom_call_target="tpu_custom_call", output_to_operand_aliasing={{0}: (4, {}), {1}: (5, {})} | custom-call | flops 8388608 | bytes 3145728 | tf_op jit(solution)/shard_map/pallas_call | solution.py:477
  226.2 2.2 shard_map.103
  (144 shorter events, 30.6 us)
Async XLA Ops:
  2.0 7.3 %copy-start = (bf16[256,4096]{1,0:T(8,128)(2,1)S(1)}, bf16[256,4096]{1,0:T(8,128)(2,1)}, u32[]{:S(2)}) copy-start(bf16[256,4096]{1,0:T(8,128)(2,1)} %key_ref.11) | copy-start | bytes 6291460
  6.4 8.5 %copy-start.1 = (bf16[256,4096]{1,0:T(8,128)(2,1)S(1)}, bf16[256,4096]{1,0:T(8,128)(2,1)}, u32[]{:S(2)}) copy-start(bf16[256,4096]{1,0:T(8,128)(2,1)} %val_ref.11) | copy-start | bytes 6291460
  6.4 13.5 %collective-permute-start.1 = (bf16[2,8,4096]{2,1,0:T(8,128)(2,1)}, bf16[2,8,4096]{2,1,0:T(8,128)(2,1)}, u32[]{:S(2)}, u32[]{:S(2)}) collective-permute-start(bf16[2,8,4096]{2,1,0:T(8,128)(2,1)} %shard_map.93), channel_id=1, source_target_pairs={{0,1},{1,0},{2,3},{3,2},{4,5},{5,4},{6,7},{7,6},{8,9},{9,8},{10,11... | collective-permute-start | bytes 393224 | tf_op jit(solution)/shard_map/ppermute | solution.py:563
  12.0 43.2 %collective-permute-start.16 = (bf16[2,256,512]{2,1,0:T(8,128)(2,1)}, bf16[2,256,512]{2,1,0:T(8,128)(2,1)}, u32[]{:S(2)}, u32[]{:S(2)}) collective-permute-start(bf16[2,256,512]{2,1,0:T(8,128)(2,1)} %pad_maximum_fusion.5), channel_id=1, source_target_pairs={{0,1},{2,3},{4,5},{6,7},{8,9},{10,11},{12,13},{14,15},{16,17},{18,... | collective-permute-start | bytes 1572872 | tf_op jit(solution)/shard_map/ppermute | solution.py:568
  16.1 2.4 %copy-start.10 = (bf16[2,8,4096]{2,1,0:T(8,128)(2,1)S(1)}, bf16[2,8,4096]{2,1,0:T(8,128)(2,1)}, u32[]{:S(2)}) copy-start(bf16[2,8,4096]{2,1,0:T(8,128)(2,1)} %shard_map.93) | copy-start | bytes 393220
  16.1 2.4 %copy-start.12 = (s32[1,8,8]{2,1,0:T(8,128)S(1)}, s32[1,8,8]{2,1,0:T(8,128)}, u32[]{:S(2)}) copy-start(s32[1,8,8]{2,1,0:T(8,128)} %param.10) | copy-start | bytes 772
  16.2 39.0 %collective-permute-start.9 = (bf16[2,256,1024]{2,1,0:T(8,128)(2,1)S(1)}, bf16[2,256,1024]{2,1,0:T(8,128)(2,1)}, u32[]{:S(2)}, u32[]{:S(2)}) collective-permute-start(bf16[2,256,1024]{2,1,0:T(8,128)(2,1)S(1)} %pad_maximum_fusion.2), channel_id=1, source_target_pairs={{0,1},{2,3},{4,5},{6,7},{8,9},{10,11},{12,13},{14,15},{16,17},{18,... | collective-permute-start | bytes 3145736 | tf_op jit(solution)/shard_map/ppermute | solution.py:568
  21.2 11.3 %collective-permute-start.12 = (bf16[1,2,16,1536]{3,2,1,0:T(8,128)(2,1)S(1)}, bf16[1,2,16,1536]{3,2,1,0:T(8,128)(2,1)S(1)}, u32[]{:S(2)}, u32[]{:S(2)}) collective-permute-start(bf16[1,2,16,1536]{3,2,1,0:T(8,128)(2,1)S(1)} %maximum_bitcast_fusion), channel_id=1, source_target_pairs={{0,24},{2,26},{4,28},{6,30},{1,25},{3,27},{5,29},{7,31}} | collective-permute-start | bytes 294920 | tf_op jit(solution)/shard_map/ppermute | solution.py:577
  27.2 7.3 %collective-permute-start.11 = (bf16[1,2,16,1536]{3,2,1,0:T(8,128)(2,1)S(1)}, bf16[1,2,16,1536]{3,2,1,0:T(8,128)(2,1)S(1)}, u32[]{:S(2)}, u32[]{:S(2)}) collective-permute-start(bf16[1,2,16,1536]{3,2,1,0:T(8,128)(2,1)S(1)} %maximum_bitcast_fusion), channel_id=1, source_target_pairs={{0,16},{2,18},{4,20},{6,22},{8,24},{10,26},{12,28},{14,30},{1,17},... | collective-permute-start | bytes 294920 | tf_op jit(solution)/shard_map/ppermute | solution.py:577
  28.5 6.0 %collective-permute-start.10 = (bf16[1,2,16,1536]{3,2,1,0:T(8,128)(2,1)S(1)}, bf16[1,2,16,1536]{3,2,1,0:T(8,128)(2,1)S(1)}, u32[]{:S(2)}, u32[]{:S(2)}) collective-permute-start(bf16[1,2,16,1536]{3,2,1,0:T(8,128)(2,1)S(1)} %maximum_bitcast_fusion), channel_id=1, source_target_pairs={{0,8},{2,10},{4,12},{6,14},{8,16},{10,18},{12,20},{14,22},{16,24},... | collective-permute-start | bytes 294920 | tf_op jit(solution)/shard_map/ppermute | solution.py:577
  32.6 4.7 %collective-permute-start.2 = (bf16[1,2,16,2560]{3,2,1,0:T(8,128)(2,1)S(1)}, bf16[1,2,16,2560]{3,2,1,0:T(8,128)(2,1)S(1)}, u32[]{:S(2)}, u32[]{:S(2)}) collective-permute-start(bf16[1,2,16,2560]{3,2,1,0:T(8,128)(2,1)S(1)} %maximum_add_fusion), channel_id=1, source_target_pairs={{0,8},{2,10},{4,12},{6,14},{8,16},{10,18},{12,20},{14,22},{16,24},... | collective-permute-start | bytes 491528 | tf_op jit(solution)/shard_map/ppermute | solution.py:584
  35.3 10.8 %collective-permute-start.13 = (bf16[4,2,16,1536]{3,2,1,0:T(8,128)(2,1)}, bf16[4,2,16,1536]{3,2,1,0:T(8,128)(2,1)}, u32[]{:S(2)}, u32[]{:S(2)}) collective-permute-start(bf16[4,2,16,1536]{3,2,1,0:T(8,128)(2,1)} %pad_maximum_fusion.6.near_ref), channel_id=1, source_target_pairs={{0,4},{2,6},{4,0},{6,2},{8,12},{10,14},{12,8},{14,10},{16,20},{18,... | collective-permute-start | bytes 1179656 | tf_op jit(solution)/shard_map/ppermute | solution.py:587
  38.1 13.8 %collective-permute-start.3 = (bf16[2,2,16,2560]{3,2,1,0:T(8,128)(2,1)}, bf16[2,2,16,2560]{3,2,1,0:T(8,128)(2,1)}, u32[]{:S(2)}, u32[]{:S(2)}) collective-permute-start(bf16[2,2,16,2560]{3,2,1,0:T(8,128)(2,1)} %pad_maximum_fusion.7), channel_id=1, source_target_pairs={{0,16},{2,18},{4,20},{6,22},{8,24},{10,26},{12,28},{14,30},{1,17},... | collective-permute-start | bytes 983048 | tf_op jit(solution)/shard_map/ppermute | solution.py:584
  46.0 9.2 %collective-permute-start.14 = (bf16[4,2,16,1536]{3,2,1,0:T(8,128)(2,1)}, bf16[4,2,16,1536]{3,2,1,0:T(8,128)(2,1)S(1)}, u32[]{:S(2)}, u32[]{:S(2)}) collective-permute-start(bf16[4,2,16,1536]{3,2,1,0:T(8,128)(2,1)} %pad_maximum_fusion.6.near_ref), channel_id=1, source_target_pairs={{0,2},{2,0},{4,6},{6,4},{8,10},{10,8},{12,14},{14,12},{16,18},{18,... | collective-permute-start | bytes 1179656 | tf_op jit(solution)/shard_map/ppermute | solution.py:591
  46.1 9.1 %collective-permute-start.15 = (bf16[4,2,16,1536]{3,2,1,0:T(8,128)(2,1)}, bf16[4,2,16,1536]{3,2,1,0:T(8,128)(2,1)}, u32[]{:S(2)}, u32[]{:S(2)}) collective-permute-start(bf16[4,2,16,1536]{3,2,1,0:T(8,128)(2,1)} %collective-permute-done.13.side_ref), channel_id=1, source_target_pairs={{0,2},{2,0},{4,6},{6,4},{8,10},{10,8},{12,14},{14,12},{16,18},{18,... | collective-permute-start | bytes 1179656 | tf_op jit(solution)/shard_map/ppermute | solution.py:592
  53.7 23.9 %collective-permute-start.4 = (bf16[4,2,16,2560]{3,2,1,0:T(8,128)(2,1)}, bf16[4,2,16,2560]{3,2,1,0:T(8,128)(2,1)}, u32[]{:S(2)}, u32[]{:S(2)}) collective-permute-start(bf16[4,2,16,2560]{3,2,1,0:T(8,128)(2,1)} %pad_maximum_fusion.3.near_ref), channel_id=1, source_target_pairs={{0,4},{2,6},{4,0},{6,2},{8,12},{10,14},{12,8},{14,10},{16,20},{18,... | collective-permute-start | bytes 1966088 | tf_op jit(solution)/shard_map/ppermute | solution.py:587
  62.3 10.3 %copy-start.2 = (bf16[1,256,1024]{2,1,0:T(8,128)(2,1)S(1)}, bf16[1,256,1024]{2,1,0:T(8,128)(2,1)}, u32[]{:S(2)}) copy-start(bf16[1,256,1024]{2,1,0:T(8,128)(2,1)} %get-tuple-element.102) | copy-start | bytes 1572868
  72.5 1.7 copy-start.7
  72.5 5.3 %collective-permute-start.32 = (bf16[8,2,16,1536]{3,2,1,0:T(8,128)(2,1)}, bf16[8,2,16,1536]{3,2,1,0:T(8,128)(2,1)S(1)}, u32[]{:S(2)}, u32[]{:S(2)}) collective-permute-start(bf16[8,2,16,1536]{3,2,1,0:T(8,128)(2,1)} %get-tuple-element.72), channel_id=1, source_target_pairs={{0,2},{2,0},{4,6},{6,4},{8,10},{10,8},{12,14},{14,12},{16,18},{18,... | collective-permute-start | bytes 2359304 | tf_op jit(solution)/shard_map/ppermute | solution.py:596
  72.7 5.1 %copy-start.16 = (bf16[2,256,512]{2,1,0:T(8,128)(2,1)S(1)}, bf16[2,256,512]{2,1,0:T(8,128)(2,1)}, u32[]{:S(2)}) copy-start(bf16[2,256,512]{2,1,0:T(8,128)(2,1)} %get-tuple-element.50) | copy-start | bytes 1572868
  72.7 6.4 %copy-start.8 = (bf16[8,2,16,1536]{3,2,1,0:T(8,128)(2,1)S(1)}, bf16[8,2,16,1536]{3,2,1,0:T(8,128)(2,1)}, u32[]{:S(2)}) copy-start(bf16[8,2,16,1536]{3,2,1,0:T(8,128)(2,1)} %get-tuple-element.71) | copy-start | bytes 2359300
  72.7 25.0 %collective-permute-start.8 = (bf16[2,256,1024]{2,1,0:T(8,128)(2,1)S(1)}, bf16[2,256,1024]{2,1,0:T(8,128)(2,1)S(1)}, u32[]{:S(2)}, u32[]{:S(2)}) collective-permute-start(bf16[2,256,1024]{2,1,0:T(8,128)(2,1)S(1)} %pad_maximum_fusion.1), channel_id=1, source_target_pairs={{0,1},{2,3},{4,5},{6,7},{8,9},{10,11},{12,13},{14,15},{16,17},{18,... | collective-permute-start | bytes 3145736 | tf_op jit(solution)/shard_map/ppermute | solution.py:568
  75.1 67.4 %collective-permute-start = (bf16[2,256,512]{2,1,0:T(8,128)(2,1)}, bf16[2,256,512]{2,1,0:T(8,128)(2,1)}, u32[]{:S(2)}, u32[]{:S(2)}) collective-permute-start(bf16[2,256,512]{2,1,0:T(8,128)(2,1)} %pad_maximum_fusion.4), channel_id=1, source_target_pairs={{0,1},{2,3},{4,5},{6,7},{8,9},{10,11},{12,13},{14,15},{16,17},{18,... | collective-permute-start | bytes 1572872 | tf_op jit(solution)/shard_map/ppermute | solution.py:568
  77.2 25.9 %collective-permute-start.5 = (bf16[4,2,16,2560]{3,2,1,0:T(8,128)(2,1)}, bf16[4,2,16,2560]{3,2,1,0:T(8,128)(2,1)S(1)}, u32[]{:S(2)}, u32[]{:S(2)}) collective-permute-start(bf16[4,2,16,2560]{3,2,1,0:T(8,128)(2,1)} %pad_maximum_fusion.3.near_ref), channel_id=1, source_target_pairs={{0,2},{2,0},{4,6},{6,4},{8,10},{10,8},{12,14},{14,12},{16,18},{18,... | collective-permute-start | bytes 1966088 | tf_op jit(solution)/shard_map/ppermute | solution.py:591
  77.7 27.3 %collective-permute-start.6 = (bf16[4,2,16,2560]{3,2,1,0:T(8,128)(2,1)}, bf16[4,2,16,2560]{3,2,1,0:T(8,128)(2,1)S(1)}, u32[]{:S(2)}, u32[]{:S(2)}) collective-permute-start(bf16[4,2,16,2560]{3,2,1,0:T(8,128)(2,1)} %collective-permute-done.4.side_ref), channel_id=1, source_target_pairs={{0,2},{2,0},{4,6},{6,4},{8,10},{10,8},{12,14},{14,12},{16,18},{18,... | collective-permute-start | bytes 1966088 | tf_op jit(solution)/shard_map/ppermute | solution.py:592
  77.8 26.6 %collective-permute-start.17 = (bf16[2,256,512]{2,1,0:T(8,128)(2,1)S(1)}, bf16[2,256,512]{2,1,0:T(8,128)(2,1)S(1)}, u32[]{:S(2)}, u32[]{:S(2)}) collective-permute-start(bf16[2,256,512]{2,1,0:T(8,128)(2,1)S(1)} %copy-done.16), channel_id=1, source_target_pairs={{1,0},{3,2},{5,4},{7,6},{9,8},{11,10},{13,12},{15,14},{17,16},{19,... | collective-permute-start | bytes 1572872 | tf_op jit(solution)/shard_map/ppermute | solution.py:648
  97.7 6.7 %copy-start.13 = (bf16[2,256,1024]{2,1,0:T(8,128)(2,1)}, bf16[2,256,1024]{2,1,0:T(8,128)(2,1)S(1)}, u32[]{:S(2)}) copy-start(bf16[2,256,1024]{2,1,0:T(8,128)(2,1)S(1)} %collective-permute-done.8.lower_ref) | copy-start | bytes 3145732
  97.7 33.5 %collective-permute-start.7 = (bf16[2,256,1024]{2,1,0:T(8,128)(2,1)S(1)}, bf16[2,256,1024]{2,1,0:T(8,128)(2,1)}, u32[]{:S(2)}, u32[]{:S(2)}) collective-permute-start(bf16[2,256,1024]{2,1,0:T(8,128)(2,1)S(1)} %pad_maximum_fusion), channel_id=1, source_target_pairs={{0,1},{2,3},{4,5},{6,7},{8,9},{10,11},{12,13},{14,15},{16,17},{18,... | collective-permute-start | bytes 3145736 | tf_op jit(solution)/shard_map/ppermute | solution.py:568
  103.1 1.9 copy-start.14
  103.1 28.2 %collective-permute-start.18 = (bf16[2,256,1024]{2,1,0:T(8,128)(2,1)}, bf16[2,256,1024]{2,1,0:T(8,128)(2,1)S(1)}, u32[]{:S(2)}, u32[]{:S(2)}) collective-permute-start(bf16[2,256,1024]{2,1,0:T(8,128)(2,1)} %get-tuple-element.55), channel_id=1, source_target_pairs={{1,0},{3,2},{5,4},{7,6},{9,8},{11,10},{13,12},{15,14},{17,16},{19,... | collective-permute-start | bytes 3145736 | tf_op jit(solution)/shard_map/ppermute | solution.py:648
  104.4 47.3 %collective-permute-start.33 = (bf16[4,2,16,1536]{3,2,1,0:T(8,128)(2,1)}, bf16[4,2,16,1536]{3,2,1,0:T(8,128)(2,1)}, u32[]{:S(2)}, u32[]{:S(2)}) collective-permute-start(bf16[4,2,16,1536]{3,2,1,0:T(8,128)(2,1)} %slice.178), channel_id=1, source_target_pairs={{0,4},{2,6},{4,0},{6,2},{8,12},{10,14},{12,8},{14,10},{16,20},{18,... | collective-permute-start | bytes 1179656 | tf_op jit(solution)/shard_map/ppermute | solution.py:597
  116.0 102.2 %collective-permute-start.31 = (bf16[2,256,1024]{2,1,0:T(8,128)(2,1)}, bf16[2,256,1024]{2,1,0:T(8,128)(2,1)S(1)}, u32[]{:S(2)}, u32[]{:S(2)}) collective-permute-start(bf16[2,256,1024]{2,1,0:T(8,128)(2,1)} %get-tuple-element.69), channel_id=1, source_target_pairs={{1,0},{3,2},{5,4},{7,6},{9,8},{11,10},{13,12},{15,14},{17,16},{19,... | collective-permute-start | bytes 3145736 | tf_op jit(solution)/shard_map/ppermute | solution.py:648
  148.9 21.9 %copy-start.3 = (bf16[8,2,16,2048]{3,2,1,0:T(8,128)(2,1)S(1)}, bf16[8,2,16,2048]{3,2,1,0:T(8,128)(2,1)}, u32[]{:S(2)}) copy-start(bf16[8,2,16,2048]{3,2,1,0:T(8,128)(2,1)} %get-tuple-element.66) | copy-start | bytes 3145732
  148.9 4.4 %collective-permute-start.20 = (bf16[8,2,16,512]{3,2,1,0:T(8,128)(2,1)}, bf16[8,2,16,512]{3,2,1,0:T(8,128)(2,1)S(1)}, u32[]{:S(2)}, u32[]{:S(2)}) collective-permute-start(bf16[8,2,16,512]{3,2,1,0:T(8,128)(2,1)} %get-tuple-element.63), channel_id=1, source_target_pairs={{0,2},{2,0},{4,6},{6,4},{8,10},{10,8},{12,14},{14,12},{16,18},{18,... | collective-permute-start | bytes 786440 | tf_op jit(solution)/shard_map/ppermute | solution.py:596
  149.0 76.5 %collective-permute-start.19 = (bf16[2,256,512]{2,1,0:T(8,128)(2,1)}, bf16[2,256,512]{2,1,0:T(8,128)(2,1)S(1)}, u32[]{:S(2)}, u32[]{:S(2)}) collective-permute-start(bf16[2,256,512]{2,1,0:T(8,128)(2,1)} %get-tuple-element.61), channel_id=1, source_target_pairs={{1,0},{3,2},{5,4},{7,6},{9,8},{11,10},{13,12},{15,14},{17,16},{19,... | collective-permute-start | bytes 1572872 | tf_op jit(solution)/shard_map/ppermute | solution.py:648
  150.4 71.4 %collective-permute-start.25 = (bf16[2,256,1024]{2,1,0:T(8,128)(2,1)}, bf16[2,256,1024]{2,1,0:T(8,128)(2,1)S(1)}, u32[]{:S(2)}, u32[]{:S(2)}) collective-permute-start(bf16[2,256,1024]{2,1,0:T(8,128)(2,1)} %get-tuple-element.65), channel_id=1, source_target_pairs={{1,0},{3,2},{5,4},{7,6},{9,8},{11,10},{13,12},{15,14},{17,16},{19,... | collective-permute-start | bytes 3145736 | tf_op jit(solution)/shard_map/ppermute | solution.py:648
  151.7 17.8 %collective-permute-start.26 = (bf16[8,2,16,2048]{3,2,1,0:T(8,128)(2,1)}, bf16[8,2,16,2048]{3,2,1,0:T(8,128)(2,1)S(1)}, u32[]{:S(2)}, u32[]{:S(2)}) collective-permute-start(bf16[8,2,16,2048]{3,2,1,0:T(8,128)(2,1)} %get-tuple-element.67), channel_id=1, source_target_pairs={{0,2},{2,0},{4,6},{6,4},{8,10},{10,8},{12,14},{14,12},{16,18},{18,... | collective-permute-start | bytes 3145736 | tf_op jit(solution)/shard_map/ppermute | solution.py:596
  153.2 9.9 %collective-permute-start.34 = (bf16[2,2,16,1536]{3,2,1,0:T(8,128)(2,1)S(1)}, bf16[2,2,16,1536]{3,2,1,0:T(8,128)(2,1)S(1)}, u32[]{:S(2)}, u32[]{:S(2)}) collective-permute-start(bf16[2,2,16,1536]{3,2,1,0:T(8,128)(2,1)S(1)} %slice.180), channel_id=1, source_target_pairs={{16,0},{18,2},{20,4},{22,6},{24,8},{26,10},{28,12},{30,14},{17,1},... | collective-permute-start | bytes 589832 | tf_op jit(solution)/shard_map/ppermute | solution.py:603
  163.2 5.0 %collective-permute-start.21 = (bf16[4,2,16,512]{3,2,1,0:T(8,128)(2,1)S(1)}, bf16[4,2,16,512]{3,2,1,0:T(8,128)(2,1)S(1)}, u32[]{:S(2)}, u32[]{:S(2)}) collective-permute-start(bf16[4,2,16,512]{3,2,1,0:T(8,128)(2,1)S(1)} %slice.162), channel_id=1, source_target_pairs={{0,4},{2,6},{4,0},{6,2},{8,12},{10,14},{12,8},{14,10},{16,20},{18,... | collective-permute-start | bytes 393224 | tf_op jit(solution)/shard_map/ppermute | solution.py:597
  168.2 10.0 %collective-permute-start.35 = (bf16[1,2,16,1536]{3,2,1,0:T(8,128)(2,1)S(1)}, bf16[1,2,16,1536]{3,2,1,0:T(8,128)(2,1)S(1)}, u32[]{:S(2)}, u32[]{:S(2)}) collective-permute-start(bf16[1,2,16,1536]{3,2,1,0:T(8,128)(2,1)S(1)} %slice.182), channel_id=1, source_target_pairs={{8,0},{10,2},{12,4},{14,6},{16,8},{18,10},{20,12},{22,14},{24,16},... | collective-permute-start | bytes 294920 | tf_op jit(solution)/shard_map/ppermute | solution.py:603
  169.5 10.7 %collective-permute-start.22 = (bf16[2,2,16,512]{3,2,1,0:T(8,128)(2,1)S(1)}, bf16[2,2,16,512]{3,2,1,0:T(8,128)(2,1)S(1)}, u32[]{:S(2)}, u32[]{:S(2)}) collective-permute-start(bf16[2,2,16,512]{3,2,1,0:T(8,128)(2,1)S(1)} %slice.164), channel_id=1, source_target_pairs={{16,0},{18,2},{20,4},{22,6},{24,8},{26,10},{28,12},{30,14},{17,1},... | collective-permute-start | bytes 196616 | tf_op jit(solution)/shard_map/ppermute | solution.py:603
  178.1 11.1 %collective-permute-start.27 = (bf16[4,2,16,2048]{3,2,1,0:T(8,128)(2,1)S(1)}, bf16[4,2,16,2048]{3,2,1,0:T(8,128)(2,1)S(1)}, u32[]{:S(2)}, u32[]{:S(2)}) collective-permute-start(bf16[4,2,16,2048]{3,2,1,0:T(8,128)(2,1)S(1)} %slice.170), channel_id=1, source_target_pairs={{0,4},{2,6},{4,0},{6,2},{8,12},{10,14},{12,8},{14,10},{16,20},{18,... | collective-permute-start | bytes 1572872 | tf_op jit(solution)/shard_map/ppermute | solution.py:597
  180.3 10.4 %collective-permute-start.36 = (bf16[2,8,1536]{2,1,0:T(8,128)(2,1)S(1)}, bf16[2,8,1536]{2,1,0:T(8,128)(2,1)S(1)}, u32[]{:S(2)}, u32[]{:S(2)}) collective-permute-start(bf16[2,8,1536]{2,1,0:T(8,128)(2,1)S(1)} %slice.184), channel_id=1, source_target_pairs={{0,1},{1,0},{2,3},{3,2},{4,5},{5,4},{6,7},{7,6},{8,9},{9,8},{10,11... | collective-permute-start | bytes 147464 | tf_op jit(solution)/shard_map/ppermute | solution.py:611
  189.2 18.1 %collective-permute-start.23 = (bf16[1,2,16,512]{3,2,1,0:T(8,128)(2,1)S(1)}, bf16[1,2,16,512]{3,2,1,0:T(8,128)(2,1)S(1)}, u32[]{:S(2)}, u32[]{:S(2)}) collective-permute-start(bf16[1,2,16,512]{3,2,1,0:T(8,128)(2,1)S(1)} %slice.166), channel_id=1, source_target_pairs={{8,0},{10,2},{12,4},{14,6},{16,8},{18,10},{20,12},{22,14},{24,16},... | collective-permute-start | bytes 98312 | tf_op jit(solution)/shard_map/ppermute | solution.py:603
  190.7 15.3 %collective-permute-start.28 = (bf16[2,2,16,2048]{3,2,1,0:T(8,128)(2,1)S(1)}, bf16[2,2,16,2048]{3,2,1,0:T(8,128)(2,1)S(1)}, u32[]{:S(2)}, u32[]{:S(2)}) collective-permute-start(bf16[2,2,16,2048]{3,2,1,0:T(8,128)(2,1)S(1)} %slice.172), channel_id=1, source_target_pairs={{16,0},{18,2},{20,4},{22,6},{24,8},{26,10},{28,12},{30,14},{17,1},... | collective-permute-start | bytes 786440 | tf_op jit(solution)/shard_map/ppermute | solution.py:603
  206.0 6.9 %collective-permute-start.29 = (bf16[1,2,16,2048]{3,2,1,0:T(8,128)(2,1)S(1)}, bf16[1,2,16,2048]{3,2,1,0:T(8,128)(2,1)S(1)}, u32[]{:S(2)}, u32[]{:S(2)}) collective-permute-start(bf16[1,2,16,2048]{3,2,1,0:T(8,128)(2,1)S(1)} %slice.174), channel_id=1, source_target_pairs={{8,0},{10,2},{12,4},{14,6},{16,8},{18,10},{20,12},{22,14},{24,16},... | collective-permute-start | bytes 393224 | tf_op jit(solution)/shard_map/ppermute | solution.py:603
  207.4 7.9 %collective-permute-start.24 = (bf16[2,8,512]{2,1,0:T(8,128)(2,1)S(1)}, bf16[2,8,512]{2,1,0:T(8,128)(2,1)S(1)}, u32[]{:S(2)}, u32[]{:S(2)}) collective-permute-start(bf16[2,8,512]{2,1,0:T(8,128)(2,1)S(1)} %slice.168), channel_id=1, source_target_pairs={{0,1},{1,0},{2,3},{3,2},{4,5},{5,4},{6,7},{7,6},{8,9},{9,8},{10,11... | collective-permute-start | bytes 49160 | tf_op jit(solution)/shard_map/ppermute | solution.py:611
  212.9 4.6 %collective-permute-start.30 = (bf16[2,8,2048]{2,1,0:T(8,128)(2,1)S(1)}, bf16[2,8,2048]{2,1,0:T(8,128)(2,1)S(1)}, u32[]{:S(2)}, u32[]{:S(2)}) collective-permute-start(bf16[2,8,2048]{2,1,0:T(8,128)(2,1)S(1)} %slice.176), channel_id=1, source_target_pairs={{0,1},{1,0},{2,3},{3,2},{4,5},{5,4},{6,7},{7,6},{8,9},{9,8},{10,11... | collective-permute-start | bytes 196616 | tf_op jit(solution)/shard_map/ppermute | solution.py:611
  (7 other events, 6.9 us)

commit v2 on v0

--- a/solution.py
+++ b/solution.py
@@ -1,14 +1,18 @@
+import functools
 import math
 
 import jax
 import jax.numpy as jnp
 from jax import lax
+from jax.experimental import pallas as pl
+from jax.experimental.pallas import tpu as pltpu
 from jax.sharding import PartitionSpec as P
 
 HD = 128
 
 
 neg_big = -1e30
+pos_big = 3e38
 
 
 def head_scores(query_heads, key_heads, factor):
@@ -277,6 +281,461 @@
     return (attention_out, query_out, key_out, value_out)
 
 
+VMEM_GRANT = 60 * 1024 * 1024
+
+
+def caps_step(place_ref, usable_ref, extra_ref, caps_ref):
+    rows_here = caps_ref.shape[1]
+    mine = extra_ref.shape[0] // 2
+    block_len = rows_here // mine
+    half = place_ref[0]
+    lane = lax.broadcasted_iota(jnp.int32, (block_len, rows_here), 1)
+    row = lax.broadcasted_iota(jnp.int32, (block_len, rows_here), 0)
+    lane_block = lane // block_len
+    for part in range(2):
+        for key_block in range(mine):
+            group_block = key_block if part else half * mine + key_block
+            allowed = jnp.zeros((block_len, rows_here), jnp.int32)
+            for query_block in range(mine):
+                lag = half * mine + query_block - group_block
+                extra = extra_ref[half * mine + query_block, group_block]
+                rule = jnp.where(
+                    (lag == 0) | (lag == 1) | ((extra == 1) & (lag > 0)), jnp.int32(1), jnp.int32(0)
+                )
+                if part:
+                    rule = rule * half
+                allowed = jnp.where(lane_block == query_block, rule, allowed)
+            caps = jnp.where(allowed == 1, pos_big, neg_big)
+            if not part:
+                caps = jnp.where(row + key_block * block_len <= lane, caps, neg_big)
+            first = part * rows_here + key_block * block_len
+            caps_ref[first : first + block_len, :] = caps
+    slots = usable_ref.shape[0]
+    per_group = (caps_ref.shape[0] - 2 * rows_here) // slots
+    for slot in range(slots):
+        first = 2 * rows_here + slot * per_group
+        caps_ref[first : first + per_group, :] = jnp.full(
+            (per_group, rows_here), jnp.where(usable_ref[slot] == 1, pos_big, neg_big), jnp.float32
+        )
+
+
+def caps_call(half, usable, extra_map, rows_here, per_group):
+    keys = 2 * rows_here + usable.shape[0] * per_group
+    smem = pl.BlockSpec(memory_space=pltpu.SMEM)
+    return pl.pallas_call(
+        caps_step,
+        in_specs=[smem] * 3,
+        out_shape=jax.ShapeDtypeStruct((keys, rows_here), jnp.float32),
+        compiler_params=pltpu.CompilerParams(vmem_limit_bytes=VMEM_GRANT),
+    )(half[None], usable, extra_map)
+
+
+def summary_slots(group_id, stages):
+    d_core = jnp.arange(2, dtype=jnp.int32)[:, None, None]
+    d_side = jnp.arange(2, dtype=jnp.int32)[None, :, None]
+    level = group_id // 4 - jnp.arange(stages, dtype=jnp.int32)[None, None, :]
+    side = (group_id // 2 + d_side) % 2
+    owner = level * 4 + side * 2 + (group_id + d_core) % 2
+    return ((level >= 0) & (owner < group_id)).astype(jnp.int32).reshape(-1)
+
+
+def attention_step(
+    summ_parts,
+    caps_ref,
+    query_ref,
+    key_ref,
+    val_ref,
+    grad_ref,
+    lower_ref,
+    *rest,
+):
+    attn_ref, query_grad_ref, local_ref, back_ref, *summ_grad_refs, mark_ref = rest[-7:]
+    mark_ref[...] = jnp.zeros(mark_ref.shape, mark_ref.dtype)
+    rows_here, width = query_ref.shape
+    part_slots, _, per_group, _ = rest[0].shape
+    part_rows = part_slots * per_group
+    half_slots = summ_parts * part_slots // 2
+    half_rows = half_slots * per_group
+
+    def summary(kind, cols):
+        return [ref[:, kind, :, cols].reshape(part_rows, HD) for ref in rest[:summ_parts]]
+
+    factor = HD ** (-0.5)
+    parts = range(width // HD)
+    queries, grads, keys, vals, raws, prob_grads = [], [], [], [], [], []
+    for part in parts:
+        cols = slice(part * HD, (part + 1) * HD)
+        queries.append(query_ref[:, cols])
+        grads.append(grad_ref[:, cols])
+        for kind, (own_ref, into) in enumerate(((key_ref, keys), (val_ref, vals))):
+            into.append(
+                jnp.concatenate(
+                    [
+                        own_ref[:, cols],
+                        lower_ref[kind, :, cols],
+                        *summary(kind, cols),
+                    ],
+                    axis=0,
+                )
+            )
+        raws.append(
+            lax.dot_general(
+                keys[part],
+                queries[part],
+                (((1,), (1,)), ((), ())),
+                preferred_element_type=jnp.float32,
+            )
+        )
+        prob_grads.append(
+            lax.dot_general(
+                vals[part], grads[part], (((1,), (1,)), ((), ())), preferred_element_type=jnp.float32
+            )
+        )
+    for part in parts:
+        cols = slice(part * HD, (part + 1) * HD)
+        query, grad = queries[part], grads[part]
+        raw = jnp.minimum(raws[part], caps_ref[...])
+        peak = jnp.max(raw, axis=0, keepdims=True)
+        grown = jnp.exp2((raw - peak) * (factor * math.log2(math.e)))
+        probs = grown * (1.0 / jnp.sum(grown, axis=0, keepdims=True))
+        weights = probs.astype(jnp.bfloat16)
+        attn = lax.dot_general(
+            vals[part], weights, (((0,), (0,)), ((), ())), preferred_element_type=jnp.float32
+        ).astype(jnp.bfloat16)
+        attn_ref[:, cols] = attn.T
+        row_dot = jnp.sum(probs * prob_grads[part], axis=0, keepdims=True)
+        score_grads = (probs * (prob_grads[part] - row_dot)).astype(jnp.bfloat16)
+        query_grad = lax.dot_general(
+            keys[part], score_grads, (((0,), (0,)), ((), ())), preferred_element_type=jnp.float32
+        )
+        query_grad_ref[:, cols] = (query_grad * factor).astype(jnp.bfloat16).T
+        key_terms = (
+            jnp.dot(score_grads, query, preferred_element_type=jnp.float32) * factor
+        ).astype(jnp.bfloat16)
+        val_terms = jnp.dot(weights, grad, preferred_element_type=jnp.float32).astype(
+            jnp.bfloat16
+        )
+        for kind, terms in enumerate((key_terms, val_terms)):
+            local_ref[kind, :, cols] = terms[:rows_here]
+            back_ref[kind, :, cols] = terms[rows_here : 2 * rows_here]
+            first = 2 * rows_here
+            for i, ref in enumerate(summ_grad_refs):
+                begin = first + i * half_rows
+                ref[:, kind, :, cols] = terms[begin : begin + half_rows].reshape(
+                    half_slots, per_group, HD
+                )
+
+
+def attention_call(
+    caps,
+    full,
+    lower,
+    width,
+    lower_col,
+    summaries,
+    first_col,
+    summ_col,
+    wide_done,
+    round_width,
+    round_col,
+    round_done,
+    after,
+):
+    rows_here, total_width = full[0].shape
+    tile = math.gcd(width, 2 * HD)
+    slots, _, per_group, _ = summaries[0].shape
+    half_slots = len(summaries) * slots // 2
+    first = first_col // tile
+    summ_first = summ_col // tile
+    lower_first = lower_col // tile
+    round_first = round_col // tile
+    wide_spec = pl.BlockSpec((rows_here, tile), lambda i: (0, first + i))
+    pair_spec = pl.BlockSpec((2, rows_here, tile), lambda i: (0, 0, i))
+    summ_in = pl.BlockSpec((slots, 2, per_group, tile), lambda i: (0, 0, 0, summ_first + i))
+    summ_out = pl.BlockSpec(
+        (half_slots, 2, per_group, tile), lambda i: (0, 0, 0, round_first + i)
+    )
+    wide = jax.ShapeDtypeStruct((rows_here, total_width), jnp.bfloat16)
+    pair = jax.ShapeDtypeStruct((2, rows_here, width), jnp.bfloat16)
+    wide_pair = jax.ShapeDtypeStruct((2, rows_here, total_width), jnp.bfloat16)
+    wide_pair_spec = pl.BlockSpec((2, rows_here, tile), lambda i: (0, 0, first + i))
+    summ = jax.ShapeDtypeStruct((half_slots, 2, per_group, round_width), jnp.bfloat16)
+    mark = jax.ShapeDtypeStruct((per_group, total_width // 2), jnp.bfloat16)
+    keys = caps.shape[0]
+    heads = width // HD
+    ahead = 6 + len(summaries)
+    aliases = {ahead + i: i for i in range(len(wide_done))}
+    aliases.update({ahead + len(wide_done) + i: 4 + i for i in range(len(round_done))})
+    return pl.pallas_call(
+        functools.partial(attention_step, len(summaries)),
+        grid=(width // tile,),
+        in_specs=[pl.BlockSpec(caps.shape, lambda i: (0, 0))]
+        + [wide_spec] * 4
+        + [pl.BlockSpec((2, rows_here, tile), lambda i: (0, 0, lower_first + i))]
+        + [summ_in] * len(summaries)
+        + [pl.BlockSpec(memory_space=pl.ANY)] * (len(aliases) + len(after)),
+        out_specs=[
+            wide_spec,
+            wide_spec,
+            wide_pair_spec,
+            pair_spec,
+            summ_out,
+            summ_out,
+            pl.BlockSpec(mark.shape, lambda i: (0, 0)),
+        ],
+        out_shape=[wide, wide, wide_pair, pair, summ, summ, mark],
+        input_output_aliases=aliases,
+        compiler_params=pltpu.CompilerParams(vmem_limit_bytes=VMEM_GRANT),
+        cost_estimate=pl.CostEstimate(
+            flops=56 * heads * keys * rows_here * HD,
+            bytes_accessed=heads * 16 * 2 * rows_here * HD,
+            transcendentals=heads * keys * rows_here,
+        ),
+    )(caps, *full, lower, *summaries, *wide_done, *round_done, *after)
+
+
+def finish_step(bounds, picker_ref, summ_ref, local_ref, *refs):
+    outs = refs[-2:]
+    count = len(bounds) - 1
+    step = pl.program_id(0)
+    picker = picker_ref[...]
+    for part in range(count):
+
+        @pl.when((step >= bounds[part]) & (step < bounds[part + 1]))
+        def _():
+            back_ref = refs[part]
+            for kind, out_ref in enumerate(outs):
+                spread = lax.dot_general(
+                    picker,
+                    summ_ref[kind],
+                    (((0,), (0,)), ((), ())),
+                    preferred_element_type=jnp.float32,
+                )
+                total = local_ref[kind].astype(jnp.float32) + back_ref[kind].astype(jnp.float32)
+                out_ref[...] = (total + spread).astype(jnp.bfloat16)
+
+
+def finish_call(picker, summ, local, backs):
+    rows_here = picker.shape[1]
+    few, total_width = summ.shape[1:]
+    tile = functools.reduce(math.gcd, [part.shape[2] for part in backs], 4 * HD)
+    bounds = [sum(part.shape[2] for part in backs[:i]) // tile for i in range(len(backs) + 1)]
+
+    def part_spec(part):
+        low, high = bounds[part], bounds[part + 1]
+        return pl.BlockSpec(
+            (2, rows_here, tile), lambda i: (0, 0, jnp.clip(i - low, 0, high - low - 1))
+        )
+
+    specs = [part_spec(part) for part in range(len(backs))]
+    wide_spec = pl.BlockSpec((rows_here, tile), lambda i: (0, i))
+    wide = jax.ShapeDtypeStruct((rows_here, total_width), jnp.bfloat16)
+    return pl.pallas_call(
+        functools.partial(finish_step, bounds),
+        grid=(bounds[-1],),
+        in_specs=[
+            pl.BlockSpec(picker.shape, lambda i: (0, 0)),
+            pl.BlockSpec((2, few, tile), lambda i: (0, 0, i)),
+        ]
+        + [pl.BlockSpec((2, rows_here, tile), lambda i: (0, 0, i))]
+        + specs,
+        out_specs=[wide_spec, wide_spec],
+        out_shape=[wide, wide],
+        compiler_params=pltpu.CompilerParams(vmem_limit_bytes=VMEM_GRANT),
+        cost_estimate=pl.CostEstimate(
+            flops=4 * few * rows_here * total_width,
+            bytes_accessed=6 * 2 * rows_here * total_width,
+            transcendentals=0,
+        ),
+    )(picker, summ, local, *backs)
+
+
+def pick_step(place_ref, rows_ref, key_ref, val_ref, out_ref, picker_ref):
+    few, rows_here = picker_ref.shape
+    half = place_ref[0]
+    row = lax.broadcasted_iota(jnp.int32, (few, rows_here), 0)
+    wanted = jnp.full((few, rows_here), -1, jnp.int32)
+    for i in range(few):
+        wanted = jnp.where(row == i, rows_ref[0, half * few + i] - half * rows_here, wanted)
+    hit = lax.broadcasted_iota(jnp.int32, (few, rows_here), 1) == wanted
+    picker = jnp.where(hit, 1.0, 0.0).astype(jnp.bfloat16)
+    picker_ref[...] = picker
+    for kind, ref in enumerate((key_ref, val_ref)):
+        rows = jnp.dot(picker, ref[...], preferred_element_type=jnp.float32)
+        out_ref[kind] = rows.astype(jnp.bfloat16)
+
+
+def pick_call(half, summary_rows, key_vectors, value_vectors):
+    rows_here, total_width = key_vectors.shape
+    few = summary_rows.shape[1] // 2
+    tile = math.gcd(total_width, 8 * HD)
+    wide_spec = pl.BlockSpec((rows_here, tile), lambda i: (0, i))
+    smem = pl.BlockSpec(memory_space=pltpu.SMEM)
+    return pl.pallas_call(
+        pick_step,
+        grid=(total_width // tile,),
+        in_specs=[smem, smem, wide_spec, wide_spec],
+        out_specs=[
+            pl.BlockSpec((2, few, tile), lambda i: (0, 0, i)),
+            pl.BlockSpec((few, rows_here), lambda i: (0, 0)),
+        ],
+        out_shape=[
+            jax.ShapeDtypeStruct((2, few, total_width), jnp.bfloat16),
+            jax.ShapeDtypeStruct((few, rows_here), jnp.bfloat16),
+        ],
+        compiler_params=pltpu.CompilerParams(vmem_limit_bytes=VMEM_GRANT),
+    )(half[None], summary_rows, key_vectors, value_vectors)
+
+
+def wait_for(array, mark):
+    return array + mark[:, : array.shape[-1]]
+
+
+def wait_for_moved(array, moved):
+    return array + jnp.minimum(jnp.abs(moved[0, :1, :1]), 0)
+
+
+def add_rounded(*terms):
+    total = terms[0].astype(jnp.float32)
+    for term in terms[1:]:
+        total = total + term.astype(jnp.float32)
+    return total.astype(jnp.bfloat16)
+
+
+def token_split(queries, key_vectors, value_vectors, out_grads, extra_blocks, summary_rows):
+    rows_here, total_width = queries.shape
+    seq_count = lax.axis_size("seq")
+    stages = seq_count // 4
+    group_id = lax.axis_index("seq")
+    half = lax.axis_index("head")
+    per_group = summary_rows.shape[1]
+    few = per_group // 2
+    flip_core = [(i, i ^ 1) for i in range(seq_count)]
+    flip_side = [(i, i ^ 2) for i in range(seq_count)]
+    flip_half = [(0, 1), (1, 0)]
+
+    def climb(step):
+        return [(i, i + 4 * step) for i in range(seq_count - 4 * step)]
+
+    def descend(step):
+        return [(i + 4 * step, i) for i in range(seq_count - 4 * step)]
+
+    unit = total_width // 8
+    chunks = [1, 3, 2, 2]
+    gather_starts = [0, 2]
+    edges = [sum(chunks[:i]) for i in range(len(chunks) + 1)]
+
+    mine, picker = pick_call(half, summary_rows, key_vectors, value_vectors)
+    other = lax.ppermute(mine, "head", flip_half)
+
+    def lower_pair(first, last, zeros=None):
+        cols = slice(edges[first] * unit, edges[last] * unit)
+        pair = jnp.stack([key_vectors[:, cols], value_vectors[:, cols]])
+        if zeros is not None:
+            pair = pair + zeros[:1, : pair.shape[2]]
+        lowers.append(lax.ppermute(pair, "head", [(0, 1)]))
+        lower_starts.append(first)
+
+    both = jnp.concatenate([mine, other], axis=1)
+
+    def span(first, last):
+        return slice(edges[first] * unit, edges[last] * unit)
+
+    def climb_stages(first, last):
+        ladder = both[:, :, span(first, last)][None]
+        return jnp.concatenate(
+            [ladder] + [lax.ppermute(ladder, "seq", climb(i)) for i in range(1, stages)], axis=0
+        )
+
+    def with_other_core(near):
+        return near, lax.ppermute(near, "seq", flip_core)
+
+    def reduce_chip(near_grad, far_grad):
+        return add_rounded(near_grad, lax.ppermute(far_grad, "seq", flip_core))
+
+    def reduce_plane(chip):
+        return add_rounded(chip[:stages], lax.ppermute(chip[stages:], "seq", flip_side))
+
+    def reduce_group(plane):
+        return add_rounded(
+            plane[0],
+            *[lax.ppermute(plane[i], "seq", descend(i)) for i in range(1, stages)],
+        )
+
+    def reduce_group_halving(plane):
+        while plane.shape[0] > 1 and plane.shape[0] % 2 == 0:
+            size = plane.shape[0] // 2
+            plane = add_rounded(plane[:size], lax.ppermute(plane[size:], "seq", descend(size)))
+        return reduce_group(plane) if plane.shape[0] > 1 else plane[0]
+
+    def reduce_half(groups):
+        group = jnp.concatenate(groups, axis=2)
+        return add_rounded(group[:, :few], lax.ppermute(group[:, few:], "head", flip_half))
+
+    usable = summary_slots(group_id, stages)
+    caps = caps_call(half, usable, extra_blocks[0], rows_here, per_group)
+    full = (queries, key_vectors, value_vectors, out_grads)
+
+    lowers = []
+    lower_starts = []
+    gathered = []
+    marks = []
+    wide_done = ()
+    backs = []
+
+    def attend(chunk, source, reduce_first, reduce_last, round_done, after):
+        nonlocal wide_done
+        low = max(start for start in lower_starts if start <= chunk)
+        out = attention_call(
+            caps,
+            full,
+            lowers[lower_starts.index(low)],
+            (edges[chunk + 1] - edges[chunk]) * unit,
+            (edges[chunk] - edges[low]) * unit,
+            gathered[source],
+            edges[chunk] * unit,
+            (edges[chunk] - edges[gather_starts[source]]) * unit,
+            wide_done,
+            (edges[reduce_last] - edges[reduce_first]) * unit,
+            (edges[chunk] - edges[reduce_first]) * unit,
+            round_done,
+            after,
+        )
+        wide_done = tuple(out[:3])
+        backs.append(lax.ppermute(out[3], "head", [(1, 0)]))
+        marks.append(out[-1])
+        return tuple(out[4:-1])
+
+
+    lower_pair(0, 2)
+    ladder = climb_stages(0, 2)
+    side = lax.ppermute(ladder, "seq", flip_side)
+    lower_pair(2, 3, jnp.minimum(jnp.abs(side[0, 0]), 0))
+    gathered.append(with_other_core(jnp.concatenate([ladder, side], axis=0)))
+    ladder = climb_stages(2, 4)
+    side = lax.ppermute(ladder, "seq", flip_side)
+    done = attend(0, 0, 0, 2, (), ())
+    lower_pair(3, 4, marks[0])
+    near = wait_for(jnp.concatenate([ladder, side], axis=0), marks[0])
+    gathered.append(with_other_core(near))
+    done = attend(1, 0, 0, 2, done, ())
+    chip_a = reduce_chip(*done)
+    done = attend(2, 1, 2, 3, (), (backs[0],))
+    chip_a = wait_for(chip_a, marks[2])
+    plane_a = reduce_plane(chip_a)
+    chip_b = reduce_chip(*done)
+    done = attend(3, 1, 3, 4, (), (backs[1], chip_a))
+    chip_b = wait_for(chip_b, marks[3])
+    plane_b = reduce_plane(chip_b)
+    chip_c = wait_for_moved(reduce_chip(*done), backs[2])
+    plane_c = reduce_plane(chip_c)
+    group_a = reduce_group_halving(plane_a)
+    group_b = reduce_group(jnp.concatenate([plane_b, plane_c], axis=3))
+    group_b = wait_for_moved(group_b, backs[3])
+    finished = finish_call(picker, reduce_half([group_a, group_b]), wide_done[2], backs)
+    return (*wide_done[:2], *finished)
+
+
 def solution(mesh):
     placed = (
         P(("seq", "head"), None),
@@ -286,8 +745,9 @@
         P("seq", None, None),
         P("seq", None),
     )
+    paired = mesh.shape["head"] == 2 and mesh.shape["seq"] % 4 == 0
     return jax.shard_map(
-        per_device,
+        token_split if paired else per_device,
         mesh=mesh,
         in_specs=placed,
         out_specs=(

time: 459 us -> 193 us (0.42)
  local copies, waits for them, and re-layouts: 117 us -> 12 us
  matrix products: 71.3 us -> 0 us
  waiting for transfers between devices: 127 us -> 58.9 us
  Pallas kernels: 0 us -> 55.5 us
  starting transfers between devices: 104 us -> 52.1 us
  between operations: 14.7 us -> 2.62 us
  other arithmetic: 18.3 us -> 10.7 us
    all_to_all x10 -> x0, waiting for transfers between devices: 114 us -> none  [the longest x1 21.8 us: per_device(): lax.all_to_all(key_terms.astype(jnp.bfloat16), 'seq', split_axis=0, conca...]
    all_to_all x10 -> x0, starting transfers between devices: 104 us -> none  [the longest x1 59.3 us: per_device(): lax.all_to_all(key_terms.astype(jnp.bfloat16), 'seq', split_axis=0, conca...]
    dot_general x10 -> x0, matrix products: 71.3 us -> none  [the longest x1 12.9 us: head_scores(): jnp.einsum('qhd,khd->hqk', query_heads, key_heads, preferred_element_type...]
    ppermute x0 -> x30, waiting for transfers between devices: none -> 58.9 us  [the longest x4 18.7 us: attend(): backs.append(lax.ppermute(out[3], 'head', [(1, 0)]))]
    pallas_call x0 -> x7, Pallas kernels: none -> 55.5 us  [the longest x4 40.4 us: attention_call(): pl.pallas_call(functools.partial(attention_step, len(summaries)), grid=(w...]
    ppermute x0 -> x30, starting transfers between devices: none -> 52.1 us  [the longest x6 17.7 us: climb_stages(): lax.ppermute(ladder, 'seq', climb(i))]
    all_to_all x12 -> x0, local copies, waits for them, and re-layouts: 42.7 us -> none  [the longest x2 8.24 us: per_device(): lax.all_to_all(outputs[0], 'head', split_axis=0, concat_axis=1, tiled=True)]
    unnamed x43 -> x38, local copies, waits for them, and re-layouts: 39.5 us -> 3.13 us
  transfers between devices with their start and end apart: 12 -> 30, of which waited for: 10 -> 13; matrix products, arithmetic and copies ran while one was open for 31% -> 10% of each run, Pallas kernels for 0% -> 22%
where the time goes in v2:
time: 193 us; the launch traced here: 192 us
  waiting for transfers between devices  58.9 us (31%)
  Pallas kernels  55.5 us (29%)
  starting transfers between devices  52.1 us (27%)
  local copies, waits for them, and re-layouts  12 us (6%)
  other arithmetic  10.7 us (6%)
  between operations  2.62 us (1%)
    pallas_call x4, Pallas kernels, attention_call(): pl.pallas_call(functools.partial(attention_step, len(summaries)), grid=(w...  40.4 us
    ppermute x4, waiting for transfers between devices, attend(): backs.append(lax.ppermute(out[3], 'head', [(1, 0)]))  18.7 us
    ppermute x6, starting transfers between devices, climb_stages(): lax.ppermute(ladder, 'seq', climb(i))  17.7 us
    ppermute x2, waiting for transfers between devices, token_split(): side = lax.ppermute(ladder, 'seq', flip_side)  12.1 us
    ppermute x3, starting transfers between devices, lower_pair(): lowers.append(lax.ppermute(pair, 'head', [(0, 1)]))  11.1 us
    pallas_call x1, Pallas kernels, finish_call(): pl.pallas_call(functools.partial(finish_step, bounds), grid=(bounds[-1],)...  8.95 us
    ppermute x3, waiting for transfers between devices, reduce_group(): lax.ppermute(plane[i], 'seq', descend(i))  7.81 us
    ppermute x3, waiting for transfers between devices, lower_pair(): lowers.append(lax.ppermute(pair, 'head', [(0, 1)]))  5.27 us
  transfers between devices with their start and end apart: 30, of which 13 were waited for; matrix products, arithmetic and copies ran while one was open for 10% of the time, Pallas kernels for 22%

profile of v2, /device:TPU:0, one launch (start us, length us, event | category | flops | bytes accessed | tf_op | source)
XLA Modules:
  0.0 191.8 jit_solution(9886347343794052534)
XLA Ops:
  0.6 4.4 %shard_map.94 = (bf16[2,8,4096]{2,1,0:T(8,128)(2,1)}, bf16[8,256]{1,0:T(8,128)(2,1)}) custom-call(s32[1]{0:T(128)} %bitcast.place_ref, s32[1,16]{1,0:T(1,128)} %rows_ref.1, bf16[256,4096]{1,0:T(8,128)(2,1)} %key_ref.9, bf16[256,4096]{1,0:T(8,128)(2,1)} %val_ref.9), custom_call_target="tpu_custom_call" | custom-call | tf_op jit(solution)/shard_map/pallas_call | solution.py:574
  5.0 3.0 %collective-permute-start.1 = (bf16[2,8,4096]{2,1,0:T(8,128)(2,1)}, bf16[2,8,4096]{2,1,0:T(8,128)(2,1)}, u32[]{:S(2)}, u32[]{:S(2)}) collective-permute-start(bf16[2,8,4096]{2,1,0:T(8,128)(2,1)} %get-tuple-element.35), channel_id=1, source_target_pairs={{0,1},{1,0},{2,3},{3,2},{4,5},{5,4},{6,7},{7,6},{8,9},{9,8},{10,11... | collective-permute-start | bytes 393224 | tf_op jit(solution)/shard_map/ppermute | solution.py:629
  8.0 1.4 slice_bitcast_fusion
  9.4 1.5 pad_maximum_fusion
  10.9 3.3 %collective-permute-start = (bf16[2,256,2048]{2,1,0:T(8,128)(2,1)}, bf16[2,256,2048]{2,1,0:T(8,128)(2,1)}, u32[]{:S(2)}, u32[]{:S(2)}) collective-permute-start(bf16[2,256,2048]{2,1,0:T(8,128)(2,1)} %pad_maximum_fusion), channel_id=1, source_target_pairs={{0,1},{2,3},{4,5},{6,7},{8,9},{10,11},{12,13},{14,15},{16,17},{18,... | collective-permute-start | bytes 6291464 | tf_op jit(solution)/shard_map/ppermute | solution.py:636
  14.2 2.4 %slice_bitcast_fusion.2 = (bf16[1,256,1024]{2,1,0:T(8,128)(2,1)}, bf16[1,256,1024]{2,1,0:T(8,128)(2,1)S(1)}, bf16[1,256,1024]{2,1,0:T(8,128)(2,1)S(1)}, bf16[1,256,1024]{2,1,0:T(8,128)(2,1)}) fusion(bf16[256,4096]{1,0:T(8,128)(2,1)} %val_ref.9, bf16[256,4096]{1,0:T(8,128)(2,1)S(1)} %copy-done), kind=kLoop, calls=%fused_computation.23 | loop fusion | bytes 4194304 | tf_op jit(solution)/shard_map/stack | solution.py:633
  17.4 1.7 shard_map.93.caps_ref
  20.1 4.0 %collective-permute-start.2 = (bf16[1,2,16,2048]{3,2,1,0:T(8,128)(2,1)S(1)}, bf16[1,2,16,2048]{3,2,1,0:T(8,128)(2,1)S(1)}, u32[]{:S(2)}, u32[]{:S(2)}) collective-permute-start(bf16[1,2,16,2048]{3,2,1,0:T(8,128)(2,1)S(1)} %get-tuple-element.74), channel_id=1, source_target_pairs={{0,8},{2,10},{4,12},{6,14},{8,16},{10,18},{12,20},{14,22},{16,24},... | collective-permute-start | bytes 393224 | tf_op jit(solution)/shard_map/ppermute | solution.py:647
  24.1 4.5 %collective-permute-start.3 = (bf16[1,2,16,2048]{3,2,1,0:T(8,128)(2,1)S(1)}, bf16[1,2,16,2048]{3,2,1,0:T(8,128)(2,1)S(1)}, u32[]{:S(2)}, u32[]{:S(2)}) collective-permute-start(bf16[1,2,16,2048]{3,2,1,0:T(8,128)(2,1)S(1)} %get-tuple-element.74), channel_id=1, source_target_pairs={{0,16},{2,18},{4,20},{6,22},{8,24},{10,26},{12,28},{14,30},{1,17},... | collective-permute-start | bytes 393224 | tf_op jit(solution)/shard_map/ppermute | solution.py:647
  28.6 1.3 collective-permute-start.4
  30.0 1.3 collective-permute-start.10
  31.3 1.3 collective-permute-start.8
  32.6 5.3 %collective-permute-start.9 = (bf16[1,2,16,2048]{3,2,1,0:T(8,128)(2,1)S(1)}, bf16[1,2,16,2048]{3,2,1,0:T(8,128)(2,1)S(1)}, u32[]{:S(2)}, u32[]{:S(2)}) collective-permute-start(bf16[1,2,16,2048]{3,2,1,0:T(8,128)(2,1)S(1)} %get-tuple-element.73), channel_id=1, source_target_pairs={{0,16},{2,18},{4,20},{6,22},{8,24},{10,26},{12,28},{14,30},{1,17},... | collective-permute-start | bytes 393224 | tf_op jit(solution)/shard_map/ppermute | solution.py:647
  38.0 1.6 collective-permute-start.5
  40.4 1.4 collective-permute-done.9
  41.9 1.6 collective-permute-start.11
  43.6 9.4 %collective-permute-done.5 = bf16[4,2,16,2048]{3,2,1,0:T(8,128)(2,1)S(1)} collective-permute-done((bf16[4,2,16,2048]{3,2,1,0:T(8,128)(2,1)S(1)}, bf16[4,2,16,2048]{3,2,1,0:T(8,128)(2,1)S(1)}, u32[]{:S(2)}, u32[]{:S(2)}) %collective-permute-start.5) | collective-permute-done | bytes 524320 | tf_op jit(solution)/shard_map/ppermute | solution.py:712
  54.3 2.3 %collective-permute-start.13 = (bf16[2,256,1024]{2,1,0:T(8,128)(2,1)}, bf16[2,256,1024]{2,1,0:T(8,128)(2,1)}, u32[]{:S(2)}, u32[]{:S(2)}) collective-permute-start(bf16[2,256,1024]{2,1,0:T(8,128)(2,1)} %maximum_add_fusion.1), channel_id=1, source_target_pairs={{0,1},{2,3},{4,5},{6,7},{8,9},{10,11},{12,13},{14,15},{16,17},{18,... | collective-permute-start | bytes 3145736 | tf_op jit(solution)/shard_map/ppermute | solution.py:636
  56.5 2.7 %collective-permute-done.11 = bf16[4,2,16,2048]{3,2,1,0:T(8,128)(2,1)S(1)} collective-permute-done((bf16[4,2,16,2048]{3,2,1,0:T(8,128)(2,1)S(1)}, bf16[4,2,16,2048]{3,2,1,0:T(8,128)(2,1)S(1)}, u32[]{:S(2)}, u32[]{:S(2)}) %collective-permute-start.11) | collective-permute-done | bytes 524320 | tf_op jit(solution)/shard_map/ppermute | solution.py:716
  60.3 6.3 %shard_map.95 = (bf16[256,4096]{1,0:T(8,128)(2,1)}, bf16[256,4096]{1,0:T(8,128)(2,1)}, bf16[2,256,4096]{2,1,0:T(8,128)(2,1)}, bf16[2,256,512]{2,1,0:T(8,128)(2,1...) custom-call(f32[768,256]{1,0:T(8,128)} %shard_map.93.caps_ref, ...), custom_call_target="tpu_custom_call" | custom-call | flops 5637144576 | bytes 4194304 | tf_op jit(solution)/shard_map/pallas_call | solution.py:469
  66.7 2.0 %broadcast_add_fusion.rest_0_ = bf16[8,2,16,2048]{3,2,1,0:T(8,128)(2,1)} fusion(bf16[8,2,16,2048]{3,2,1,0:T(8,128)(2,1)S(1)} %constant_dynamic-update-slice_fusion.7, bf16[16,2048]{1,0:T(8,128)(2,1)} %get-tuple-element.36), kind=kLoop, calls=%fused_computation.25 | loop fusion | flops 524288 | bytes 2162688 | tf_op jit(solution)/shard_map/add | solution.py:591
  68.6 1.3 collective-permute-start.14
  69.9 13.8 %shard_map.96 = (bf16[256,4096]{1,0:T(8,128)(2,1)}, bf16[256,4096]{1,0:T(8,128)(2,1)}, bf16[2,256,4096]{2,1,0:T(8,128)(2,1)}, bf16[2,256,1536]{2,1,0:T(8,128)(2,...) custom-call(f32[768,256]{1,0:T(8,128)} %shard_map.93.caps_ref, ...), custom_call_target="tpu_custom_call", output_to_operand_aliasing={{0}: (8, {}), {1}: (9, {}), {2}: (10, {}), {4}: (11, {}), {... | custom-call | flops 16911433728 | bytes 12582912 | tf_op jit(solution)/shard_map/pallas_call | solution.py:469
  84.3 1.3 collective-permute-start.15
  87.4 5.6 %collective-permute-start.7 = (bf16[2,256,1024]{2,1,0:T(8,128)(2,1)}, bf16[2,256,1024]{2,1,0:T(8,128)(2,1)}, u32[]{:S(2)}, u32[]{:S(2)}) collective-permute-start(bf16[2,256,1024]{2,1,0:T(8,128)(2,1)} %maximum_add_fusion), channel_id=1, source_target_pairs={{0,1},{2,3},{4,5},{6,7},{8,9},{10,11},{12,13},{14,15},{16,17},{18,... | collective-permute-start | bytes 3145736 | tf_op jit(solution)/shard_map/ppermute | solution.py:636
  93.9 10.1 %shard_map.97 = (bf16[256,4096]{1,0:T(8,128)(2,1)}, bf16[256,4096]{1,0:T(8,128)(2,1)}, bf16[2,256,4096]{2,1,0:T(8,128)(2,1)}, bf16[2,256,1024]{2,1,0:T(8,128)(2,...) custom-call(f32[768,256]{1,0:T(8,128)} %shard_map.93.caps_ref, ...), custom_call_target="tpu_custom_call", output_to_operand_aliasing={{0}: (8, {}), {1}: (9, {}), {2}: (10, {})} | custom-call | flops 11274289152 | bytes 8388608 | tf_op jit(solution)/shard_map/pallas_call | solution.py:469
  104.0 1.9 %fusion.rest_6_ = bf16[8,2,16,2048]{3,2,1,0:T(8,128)(2,1)S(1)} fusion(bf16[8,2,16,2048]{3,2,1,0:T(8,128)(2,1)} %collective-permute-done.16, bf16[8,2,16,2048]{3,2,1,0:T(8,128)(2,1)} %get-tuple-element.50, bf16[16,2048]{1,0:T(8,128)(2,1)} %get-tuple-element.52), kind=kLoop, calls=%fused_computation.2 | loop fusion | flops 2621440 | bytes 3211264 | tf_op jit(solution)/shard_map/add | solution.py:591
  106.9 1.5 collective-permute-start.17
  108.4 1.3 collective-permute-start.23
  109.7 5.3 %collective-permute-done.7.lower_ref = bf16[2,256,1024]{2,1,0:T(8,128)(2,1)} collective-permute-done((bf16[2,256,1024]{2,1,0:T(8,128)(2,1)}, bf16[2,256,1024]{2,1,0:T(8,128)(2,1)}, u32[]{:S(2)}, u32[]{:S(2)}) %collective-permute-start.7) | collective-permute-done | bytes 1048608 | tf_op jit(solution)/shard_map/ppermute | solution.py:636
  115.0 8.7 %collective-permute-done.15.rest_5_.refs_1_ = bf16[2,256,1536]{2,1,0:T(8,128)(2,1)S(1)} collective-permute-done((bf16[2,256,1536]{2,1,0:T(8,128)(2,1)}, bf16[2,256,1536]{2,1,0:T(8,128)(2,1)S(1)}, u32[]{:S(2)}, u32[]{:S(2)}) %collective-permute-start.15) | collective-permute-done | bytes 1572896 | tf_op jit(solution)/shard_map/ppermute | solution.py:705
  124.9 10.1 %shard_map.98 = (bf16[256,4096]{1,0:T(8,128)(2,1)}, bf16[256,4096]{1,0:T(8,128)(2,1)}, bf16[2,256,4096]{2,1,0:T(8,128)(2,1)}, bf16[2,256,1024]{2,1,0:T(8,128)(2,...) custom-call(f32[768,256]{1,0:T(8,128)} %shard_map.93.caps_ref, ...), custom_call_target="tpu_custom_call", output_to_operand_aliasing={{0}: (8, {}), {1}: (9, {}), {2}: (10, {})} | custom-call | flops 11274289152 | bytes 8388608 | tf_op jit(solution)/shard_map/pallas_call | solution.py:469
  135.1 1.3 add_convert_fusion.3
  136.5 1.5 collective-permute-start.18
  138.2 1.6 collective-permute-start.21
  139.8 1.3 collective-permute-start.28
  141.1 5.1 %collective-permute-done.23.refs_2_ = bf16[2,256,1024]{2,1,0:T(8,128)(2,1)} collective-permute-done((bf16[2,256,1024]{2,1,0:T(8,128)(2,1)}, bf16[2,256,1024]{2,1,0:T(8,128)(2,1)}, u32[]{:S(2)}, u32[]{:S(2)}) %collective-permute-start.23) | collective-permute-done | bytes 1048608 | tf_op jit(solution)/shard_map/ppermute | solution.py:705
  148.3 1.6 collective-permute-start.24
  149.9 1.3 collective-permute-start.19
  151.3 4.1 %collective-permute-done.24 = bf16[4,2,16,1024]{3,2,1,0:T(8,128)(2,1)S(1)} collective-permute-done((bf16[4,2,16,1024]{3,2,1,0:T(8,128)(2,1)S(1)}, bf16[4,2,16,1024]{3,2,1,0:T(8,128)(2,1)S(1)}, u32[]{:S(2)}, u32[]{:S(2)}) %collective-permute-start.24) | collective-permute-done | bytes 262176 | tf_op jit(solution)/shard_map/ppermute | solution.py:657
  155.6 1.3 collective-permute-start.25
  156.9 1.3 collective-permute-start.26
  158.2 1.3 collective-permute-start.27
  159.5 3.6 %collective-permute-done.19 = bf16[1,2,16,2048]{3,2,1,0:T(8,128)(2,1)S(1)} collective-permute-done((bf16[1,2,16,2048]{3,2,1,0:T(8,128)(2,1)S(1)}, bf16[1,2,16,2048]{3,2,1,0:T(8,128)(2,1)S(1)}, u32[]{:S(2)}, u32[]{:S(2)}) %collective-permute-start.19) | collective-permute-done | bytes 131104 | tf_op jit(solution)/shard_map/ppermute | solution.py:668
  163.1 4.9 %collective-permute-done.28.refs_3_ = bf16[2,256,1024]{2,1,0:T(8,128)(2,1)S(1)} collective-permute-done((bf16[2,256,1024]{2,1,0:T(8,128)(2,1)S(1)}, bf16[2,256,1024]{2,1,0:T(8,128)(2,1)S(1)}, u32[]{:S(2)}, u32[]{:S(2)}) %collective-permute-start.28) | collective-permute-done | bytes 1048608 | tf_op jit(solution)/shard_map/ppermute | solution.py:705
  170.0 7.0 %collective-permute-done.26 = bf16[2,16,2048]{2,1,0:T(8,128)(2,1)S(1)} collective-permute-done((bf16[2,16,2048]{2,1,0:T(8,128)(2,1)S(1)}, bf16[2,16,2048]{2,1,0:T(8,128)(2,1)S(1)}, u32[]{:S(2)}, u32[]{:S(2)}) %collective-permute-start.26) | collective-permute-done | bytes 131104 | tf_op jit(solution)/shard_map/ppermute | solution.py:662
  177.2 5.0 %collective-permute-done.29 = bf16[2,8,4096]{2,1,0:T(8,128)(2,1)S(1)} collective-permute-done((bf16[2,8,4096]{2,1,0:T(8,128)(2,1)S(1)}, bf16[2,8,4096]{2,1,0:T(8,128)(2,1)S(1)}, u32[]{:S(2)}, u32[]{:S(2)}) %collective-permute-start.29) | collective-permute-done | bytes 131104 | tf_op jit(solution)/shard_map/ppermute | solution.py:673
  182.8 8.9 %shard_map.99 = (bf16[256,4096]{1,0:T(8,128)(2,1)}, bf16[256,4096]{1,0:T(8,128)(2,1)}) custom-call(bf16[8,256]{1,0:T(8,128)(2,1)} %get-tuple-element.55.picker_ref, bf16[2,8,4096]{2,1,0:T(8,128)(2,1)} %add_convert_fusion.7.summ_ref, bf16[2,256,4096]{2,1,0:T(8,128)(2,1)} %get-tuple-element.63.local_ref, bf16[2,256,512]{2,1,0:T(8,128)(2,1)} %copy-done.8, ...), custom_call_target="tpu_custom_call" | custom-call | flops 33554432 | bytes 12582912 | tf_op jit(solution)/shard_map/pallas_call | solution.py:533
  (99 shorter events, 14.7 us)
Async XLA Ops:
  0.6 7.4 %copy-start = (bf16[256,4096]{1,0:T(8,128)(2,1)S(1)}, bf16[256,4096]{1,0:T(8,128)(2,1)}, u32[]{:S(2)}) copy-start(bf16[256,4096]{1,0:T(8,128)(2,1)} %key_ref.9) | copy-start | bytes 6291460
  5.0 14.1 %collective-permute-start.1 = (bf16[2,8,4096]{2,1,0:T(8,128)(2,1)}, bf16[2,8,4096]{2,1,0:T(8,128)(2,1)}, u32[]{:S(2)}, u32[]{:S(2)}) collective-permute-start(bf16[2,8,4096]{2,1,0:T(8,128)(2,1)} %get-tuple-element.35), channel_id=1, source_target_pairs={{0,1},{1,0},{2,3},{3,2},{4,5},{5,4},{6,7},{7,6},{8,9},{9,8},{10,11... | collective-permute-start | bytes 393224 | tf_op jit(solution)/shard_map/ppermute | solution.py:629
  9.4 4.8 %copy-start.9 = (bf16[2,8,4096]{2,1,0:T(8,128)(2,1)S(1)}, bf16[2,8,4096]{2,1,0:T(8,128)(2,1)}, u32[]{:S(2)}) copy-start(bf16[2,8,4096]{2,1,0:T(8,128)(2,1)} %get-tuple-element.35) | copy-start | bytes 393220
  10.9 48.5 %collective-permute-start = (bf16[2,256,2048]{2,1,0:T(8,128)(2,1)}, bf16[2,256,2048]{2,1,0:T(8,128)(2,1)}, u32[]{:S(2)}, u32[]{:S(2)}) collective-permute-start(bf16[2,256,2048]{2,1,0:T(8,128)(2,1)} %pad_maximum_fusion), channel_id=1, source_target_pairs={{0,1},{2,3},{4,5},{6,7},{8,9},{10,11},{12,13},{14,15},{16,17},{18,... | collective-permute-start | bytes 6291464 | tf_op jit(solution)/shard_map/ppermute | solution.py:636
  20.1 11.1 %collective-permute-start.2 = (bf16[1,2,16,2048]{3,2,1,0:T(8,128)(2,1)S(1)}, bf16[1,2,16,2048]{3,2,1,0:T(8,128)(2,1)S(1)}, u32[]{:S(2)}, u32[]{:S(2)}) collective-permute-start(bf16[1,2,16,2048]{3,2,1,0:T(8,128)(2,1)S(1)} %get-tuple-element.74), channel_id=1, source_target_pairs={{0,8},{2,10},{4,12},{6,14},{8,16},{10,18},{12,20},{14,22},{16,24},... | collective-permute-start | bytes 393224 | tf_op jit(solution)/shard_map/ppermute | solution.py:647
  24.1 8.5 %collective-permute-start.3 = (bf16[1,2,16,2048]{3,2,1,0:T(8,128)(2,1)S(1)}, bf16[1,2,16,2048]{3,2,1,0:T(8,128)(2,1)S(1)}, u32[]{:S(2)}, u32[]{:S(2)}) collective-permute-start(bf16[1,2,16,2048]{3,2,1,0:T(8,128)(2,1)S(1)} %get-tuple-element.74), channel_id=1, source_target_pairs={{0,16},{2,18},{4,20},{6,22},{8,24},{10,26},{12,28},{14,30},{1,17},... | collective-permute-start | bytes 393224 | tf_op jit(solution)/shard_map/ppermute | solution.py:647
  28.6 9.3 %collective-permute-start.4 = (bf16[1,2,16,2048]{3,2,1,0:T(8,128)(2,1)S(1)}, bf16[1,2,16,2048]{3,2,1,0:T(8,128)(2,1)S(1)}, u32[]{:S(2)}, u32[]{:S(2)}) collective-permute-start(bf16[1,2,16,2048]{3,2,1,0:T(8,128)(2,1)S(1)} %get-tuple-element.74), channel_id=1, source_target_pairs={{0,24},{2,26},{4,28},{6,30},{1,25},{3,27},{5,29},{7,31}} | collective-permute-start | bytes 393224 | tf_op jit(solution)/shard_map/ppermute | solution.py:647
  30.0 9.6 %collective-permute-start.10 = (bf16[1,2,16,2048]{3,2,1,0:T(8,128)(2,1)S(1)}, bf16[1,2,16,2048]{3,2,1,0:T(8,128)(2,1)S(1)}, u32[]{:S(2)}, u32[]{:S(2)}) collective-permute-start(bf16[1,2,16,2048]{3,2,1,0:T(8,128)(2,1)S(1)} %get-tuple-element.73), channel_id=1, source_target_pairs={{0,24},{2,26},{4,28},{6,30},{1,25},{3,27},{5,29},{7,31}} | collective-permute-start | bytes 393224 | tf_op jit(solution)/shard_map/ppermute | solution.py:647
  31.3 9.1 %collective-permute-start.8 = (bf16[1,2,16,2048]{3,2,1,0:T(8,128)(2,1)S(1)}, bf16[1,2,16,2048]{3,2,1,0:T(8,128)(2,1)S(1)}, u32[]{:S(2)}, u32[]{:S(2)}) collective-permute-start(bf16[1,2,16,2048]{3,2,1,0:T(8,128)(2,1)S(1)} %get-tuple-element.73), channel_id=1, source_target_pairs={{0,8},{2,10},{4,12},{6,14},{8,16},{10,18},{12,20},{14,22},{16,24},... | collective-permute-start | bytes 393224 | tf_op jit(solution)/shard_map/ppermute | solution.py:647
  32.6 9.3 %collective-permute-start.9 = (bf16[1,2,16,2048]{3,2,1,0:T(8,128)(2,1)S(1)}, bf16[1,2,16,2048]{3,2,1,0:T(8,128)(2,1)S(1)}, u32[]{:S(2)}, u32[]{:S(2)}) collective-permute-start(bf16[1,2,16,2048]{3,2,1,0:T(8,128)(2,1)S(1)} %get-tuple-element.73), channel_id=1, source_target_pairs={{0,16},{2,18},{4,20},{6,22},{8,24},{10,26},{12,28},{14,30},{1,17},... | collective-permute-start | bytes 393224 | tf_op jit(solution)/shard_map/ppermute | solution.py:647
  38.0 15.1 %copy-start.2 = (bf16[1,256,1024]{2,1,0:T(8,128)(2,1)S(1)}, bf16[1,256,1024]{2,1,0:T(8,128)(2,1)}, u32[]{:S(2)}) copy-start(bf16[1,256,1024]{2,1,0:T(8,128)(2,1)} %get-tuple-element.68) | copy-start | bytes 1572868
  38.0 15.1 %copy-start.3 = (bf16[1,256,1024]{2,1,0:T(8,128)(2,1)S(1)}, bf16[1,256,1024]{2,1,0:T(8,128)(2,1)}, u32[]{:S(2)}) copy-start(bf16[1,256,1024]{2,1,0:T(8,128)(2,1)} %get-tuple-element.80) | copy-start | bytes 1572868
  38.0 14.9 %collective-permute-start.5 = (bf16[4,2,16,2048]{3,2,1,0:T(8,128)(2,1)S(1)}, bf16[4,2,16,2048]{3,2,1,0:T(8,128)(2,1)S(1)}, u32[]{:S(2)}, u32[]{:S(2)}) collective-permute-start(bf16[4,2,16,2048]{3,2,1,0:T(8,128)(2,1)S(1)} %pad_maximum_fusion.1), channel_id=1, source_target_pairs={{0,4},{2,6},{4,0},{6,2},{8,12},{10,14},{12,8},{14,10},{16,20},{18,... | collective-permute-start | bytes 1572872 | tf_op jit(solution)/shard_map/ppermute | solution.py:712
  41.9 17.4 %collective-permute-start.11 = (bf16[4,2,16,2048]{3,2,1,0:T(8,128)(2,1)S(1)}, bf16[4,2,16,2048]{3,2,1,0:T(8,128)(2,1)S(1)}, u32[]{:S(2)}, u32[]{:S(2)}) collective-permute-start(bf16[4,2,16,2048]{3,2,1,0:T(8,128)(2,1)S(1)} %pad_maximum_fusion.2), channel_id=1, source_target_pairs={{0,4},{2,6},{4,0},{6,2},{8,12},{10,14},{12,8},{14,10},{16,20},{18,... | collective-permute-start | bytes 1572872 | tf_op jit(solution)/shard_map/ppermute | solution.py:716
  53.0 6.4 %copy-start.11 = (bf16[8,2,16,2048]{3,2,1,0:T(8,128)(2,1)}, bf16[8,2,16,2048]{3,2,1,0:T(8,128)(2,1)S(1)}, u32[]{:S(2)}) copy-start(bf16[8,2,16,2048]{3,2,1,0:T(8,128)(2,1)S(1)} %constant_dynamic-update-slice_fusion.2.rest_0_) | copy-start | bytes 3145732
  53.0 6.4 %collective-permute-start.6 = (bf16[8,2,16,2048]{3,2,1,0:T(8,128)(2,1)S(1)}, bf16[8,2,16,2048]{3,2,1,0:T(8,128)(2,1)S(1)}, u32[]{:S(2)}, u32[]{:S(2)}) collective-permute-start(bf16[8,2,16,2048]{3,2,1,0:T(8,128)(2,1)S(1)} %constant_dynamic-update-slice_fusion.2.rest_0_), channel_id=1, source_target_pairs={{0,2},{2,0},{4,6},{6,4},{8,10},{10,8},{12,14},{14,12},{16,18},{18,... | collective-permute-start | bytes 3145736 | tf_op jit(solution)/shard_map/ppermute | solution.py:651
  54.3 33.2 %collective-permute-start.13 = (bf16[2,256,1024]{2,1,0:T(8,128)(2,1)}, bf16[2,256,1024]{2,1,0:T(8,128)(2,1)}, u32[]{:S(2)}, u32[]{:S(2)}) collective-permute-start(bf16[2,256,1024]{2,1,0:T(8,128)(2,1)} %maximum_add_fusion.1), channel_id=1, source_target_pairs={{0,1},{2,3},{4,5},{6,7},{8,9},{10,11},{12,13},{14,15},{16,17},{18,... | collective-permute-start | bytes 3145736 | tf_op jit(solution)/shard_map/ppermute | solution.py:636
  59.3 1.0 copy-start.13
  66.7 2.0 %copy-start.14 = (bf16[2,256,512]{2,1,0:T(8,128)(2,1)S(1)}, bf16[2,256,512]{2,1,0:T(8,128)(2,1)}, u32[]{:S(2)}) copy-start(bf16[2,256,512]{2,1,0:T(8,128)(2,1)} %get-tuple-element.45) | copy-start | bytes 1572868
  68.6 24.4 %collective-permute-start.12 = (bf16[8,2,16,2048]{3,2,1,0:T(8,128)(2,1)}, bf16[8,2,16,2048]{3,2,1,0:T(8,128)(2,1)}, u32[]{:S(2)}, u32[]{:S(2)}) collective-permute-start(bf16[8,2,16,2048]{3,2,1,0:T(8,128)(2,1)} %broadcast_add_fusion.rest_0_), channel_id=1, source_target_pairs={{0,2},{2,0},{4,6},{6,4},{8,10},{10,8},{12,14},{14,12},{16,18},{18,... | collective-permute-start | bytes 3145736 | tf_op jit(solution)/shard_map/ppermute | solution.py:651
  68.6 24.4 %collective-permute-start.14 = (bf16[2,256,512]{2,1,0:T(8,128)(2,1)S(1)}, bf16[2,256,512]{2,1,0:T(8,128)(2,1)S(1)}, u32[]{:S(2)}, u32[]{:S(2)}) collective-permute-start(bf16[2,256,512]{2,1,0:T(8,128)(2,1)S(1)} %copy-done.14), channel_id=1, source_target_pairs={{1,0},{3,2},{5,4},{7,6},{9,8},{11,10},{13,12},{15,14},{17,16},{19,... | collective-permute-start | bytes 1572872 | tf_op jit(solution)/shard_map/ppermute | solution.py:705
  83.8 20.2 %collective-permute-start.16 = (bf16[8,2,16,2048]{3,2,1,0:T(8,128)(2,1)}, bf16[8,2,16,2048]{3,2,1,0:T(8,128)(2,1)}, u32[]{:S(2)}, u32[]{:S(2)}) collective-permute-start(bf16[8,2,16,2048]{3,2,1,0:T(8,128)(2,1)} %get-tuple-element.51), channel_id=1, source_target_pairs={{0,2},{2,0},{4,6},{6,4},{8,10},{10,8},{12,14},{14,12},{16,18},{18,... | collective-permute-start | bytes 3145736 | tf_op jit(solution)/shard_map/ppermute | solution.py:654
  84.3 39.3 %collective-permute-start.15 = (bf16[2,256,1536]{2,1,0:T(8,128)(2,1)}, bf16[2,256,1536]{2,1,0:T(8,128)(2,1)S(1)}, u32[]{:S(2)}, u32[]{:S(2)}) collective-permute-start(bf16[2,256,1536]{2,1,0:T(8,128)(2,1)} %get-tuple-element.49), channel_id=1, source_target_pairs={{1,0},{3,2},{5,4},{7,6},{9,8},{11,10},{13,12},{15,14},{17,16},{19,... | collective-permute-start | bytes 4718600 | tf_op jit(solution)/shard_map/ppermute | solution.py:705
  87.4 27.6 %collective-permute-start.7 = (bf16[2,256,1024]{2,1,0:T(8,128)(2,1)}, bf16[2,256,1024]{2,1,0:T(8,128)(2,1)}, u32[]{:S(2)}, u32[]{:S(2)}) collective-permute-start(bf16[2,256,1024]{2,1,0:T(8,128)(2,1)} %maximum_add_fusion), channel_id=1, source_target_pairs={{0,1},{2,3},{4,5},{6,7},{8,9},{10,11},{12,13},{14,15},{16,17},{18,... | collective-permute-start | bytes 3145736 | tf_op jit(solution)/shard_map/ppermute | solution.py:636
  93.1 0.8 copy-start.8
  105.9 17.7 %copy-start.1 = (bf16[8,2,16,2048]{3,2,1,0:T(8,128)(2,1)}, bf16[8,2,16,2048]{3,2,1,0:T(8,128)(2,1)S(1)}, u32[]{:S(2)}) copy-start(bf16[8,2,16,2048]{3,2,1,0:T(8,128)(2,1)S(1)} %fusion.rest_6_) | copy-start | bytes 3145732
  106.9 28.3 %collective-permute-start.17 = (bf16[4,2,16,2048]{3,2,1,0:T(8,128)(2,1)}, bf16[4,2,16,2048]{3,2,1,0:T(8,128)(2,1)S(1)}, u32[]{:S(2)}, u32[]{:S(2)}) collective-permute-start(bf16[4,2,16,2048]{3,2,1,0:T(8,128)(2,1)} %slice.125), channel_id=1, source_target_pairs={{0,4},{2,6},{4,0},{6,2},{8,12},{10,14},{12,8},{14,10},{16,20},{18,... | collective-permute-start | bytes 1572872 | tf_op jit(solution)/shard_map/ppermute | solution.py:657
  108.4 37.9 %collective-permute-start.23 = (bf16[2,256,1024]{2,1,0:T(8,128)(2,1)}, bf16[2,256,1024]{2,1,0:T(8,128)(2,1)}, u32[]{:S(2)}, u32[]{:S(2)}) collective-permute-start(bf16[2,256,1024]{2,1,0:T(8,128)(2,1)} %get-tuple-element.61), channel_id=1, source_target_pairs={{1,0},{3,2},{5,4},{7,6},{9,8},{11,10},{13,12},{15,14},{17,16},{19,... | collective-permute-start | bytes 3145736 | tf_op jit(solution)/shard_map/ppermute | solution.py:705
  109.7 28.3 %collective-permute-start.20 = (bf16[8,2,16,1024]{3,2,1,0:T(8,128)(2,1)}, bf16[8,2,16,1024]{3,2,1,0:T(8,128)(2,1)S(1)}, u32[]{:S(2)}, u32[]{:S(2)}) collective-permute-start(bf16[8,2,16,1024]{3,2,1,0:T(8,128)(2,1)} %get-tuple-element.57), channel_id=1, source_target_pairs={{0,2},{2,0},{4,6},{6,4},{8,10},{10,8},{12,14},{14,12},{16,18},{18,... | collective-permute-start | bytes 1572872 | tf_op jit(solution)/shard_map/ppermute | solution.py:654
  123.7 1.2 copy-start.4
  135.0 2.9 %copy-start.10 = (bf16[16,2048]{1,0:T(8,128)(2,1)S(1)}, bf16[16,2048]{1,0:T(8,128)(2,1)}, u32[]{:S(2)}) copy-start(bf16[16,2048]{1,0:T(8,128)(2,1)} %get-tuple-element.58) | copy-start | bytes 196612
  135.0 3.0 %copy-start.6 = (bf16[8,2,16,1024]{3,2,1,0:T(8,128)(2,1)S(1)}, bf16[8,2,16,1024]{3,2,1,0:T(8,128)(2,1)}, u32[]{:S(2)}) copy-start(bf16[8,2,16,1024]{3,2,1,0:T(8,128)(2,1)} %get-tuple-element.56) | copy-start | bytes 1572868
  135.0 4.8 %copy-start.12 = (bf16[2,256,1024]{2,1,0:T(8,128)(2,1)S(1)}, bf16[2,256,1024]{2,1,0:T(8,128)(2,1)}, u32[]{:S(2)}) copy-start(bf16[2,256,1024]{2,1,0:T(8,128)(2,1)} %get-tuple-element.62) | copy-start | bytes 3145732
  135.0 13.0 %copy-start.7 = (bf16[8,2,16,1024]{3,2,1,0:T(8,128)(2,1)S(1)}, bf16[8,2,16,1024]{3,2,1,0:T(8,128)(2,1)}, u32[]{:S(2)}) copy-start(bf16[8,2,16,1024]{3,2,1,0:T(8,128)(2,1)} %get-tuple-element.59) | copy-start | bytes 1572868
  135.0 13.0 %collective-permute-start.22 = (bf16[8,2,16,1024]{3,2,1,0:T(8,128)(2,1)}, bf16[8,2,16,1024]{3,2,1,0:T(8,128)(2,1)S(1)}, u32[]{:S(2)}, u32[]{:S(2)}) collective-permute-start(bf16[8,2,16,1024]{3,2,1,0:T(8,128)(2,1)} %get-tuple-element.60), channel_id=1, source_target_pairs={{0,2},{2,0},{4,6},{6,4},{8,10},{10,8},{12,14},{14,12},{16,18},{18,... | collective-permute-start | bytes 1572872 | tf_op jit(solution)/shard_map/ppermute | solution.py:654
  136.5 13.4 %collective-permute-start.18 = (bf16[2,2,16,2048]{3,2,1,0:T(8,128)(2,1)S(1)}, bf16[2,2,16,2048]{3,2,1,0:T(8,128)(2,1)S(1)}, u32[]{:S(2)}, u32[]{:S(2)}) collective-permute-start(bf16[2,2,16,2048]{3,2,1,0:T(8,128)(2,1)S(1)} %slice.127), channel_id=1, source_target_pairs={{16,0},{18,2},{20,4},{22,6},{24,8},{26,10},{28,12},{30,14},{17,1},... | collective-permute-start | bytes 786440 | tf_op jit(solution)/shard_map/ppermute | solution.py:668
  138.2 13.0 %collective-permute-start.21 = (bf16[4,2,16,1024]{3,2,1,0:T(8,128)(2,1)S(1)}, bf16[4,2,16,1024]{3,2,1,0:T(8,128)(2,1)S(1)}, u32[]{:S(2)}, u32[]{:S(2)}) collective-permute-start(bf16[4,2,16,1024]{3,2,1,0:T(8,128)(2,1)S(1)} %slice.131), channel_id=1, source_target_pairs={{0,4},{2,6},{4,0},{6,2},{8,12},{10,14},{12,8},{14,10},{16,20},{18,... | collective-permute-start | bytes 786440 | tf_op jit(solution)/shard_map/ppermute | solution.py:657
  139.8 28.2 %collective-permute-start.28 = (bf16[2,256,1024]{2,1,0:T(8,128)(2,1)S(1)}, bf16[2,256,1024]{2,1,0:T(8,128)(2,1)S(1)}, u32[]{:S(2)}, u32[]{:S(2)}) collective-permute-start(bf16[2,256,1024]{2,1,0:T(8,128)(2,1)S(1)} %copy-done.12), channel_id=1, source_target_pairs={{1,0},{3,2},{5,4},{7,6},{9,8},{11,10},{13,12},{15,14},{17,16},{19,... | collective-permute-start | bytes 3145736 | tf_op jit(solution)/shard_map/ppermute | solution.py:705
  148.3 7.2 %collective-permute-start.24 = (bf16[4,2,16,1024]{3,2,1,0:T(8,128)(2,1)S(1)}, bf16[4,2,16,1024]{3,2,1,0:T(8,128)(2,1)S(1)}, u32[]{:S(2)}, u32[]{:S(2)}) collective-permute-start(bf16[4,2,16,1024]{3,2,1,0:T(8,128)(2,1)S(1)} %slice.134), channel_id=1, source_target_pairs={{0,4},{2,6},{4,0},{6,2},{8,12},{10,14},{12,8},{14,10},{16,20},{18,... | collective-permute-start | bytes 786440 | tf_op jit(solution)/shard_map/ppermute | solution.py:657
  149.9 13.1 %collective-permute-start.19 = (bf16[1,2,16,2048]{3,2,1,0:T(8,128)(2,1)S(1)}, bf16[1,2,16,2048]{3,2,1,0:T(8,128)(2,1)S(1)}, u32[]{:S(2)}, u32[]{:S(2)}) collective-permute-start(bf16[1,2,16,2048]{3,2,1,0:T(8,128)(2,1)S(1)} %slice.129), channel_id=1, source_target_pairs={{8,0},{10,2},{12,4},{14,6},{16,8},{18,10},{20,12},{22,14},{24,16},... | collective-permute-start | bytes 393224 | tf_op jit(solution)/shard_map/ppermute | solution.py:668
  155.6 14.4 %collective-permute-start.25 = (bf16[2,16,2048]{2,1,0:T(8,128)(2,1)S(1)}, bf16[2,16,2048]{2,1,0:T(8,128)(2,1)S(1)}, u32[]{:S(2)}, u32[]{:S(2)}) collective-permute-start(bf16[2,16,2048]{2,1,0:T(8,128)(2,1)S(1)} %get-tuple-element.70), channel_id=1, source_target_pairs={{8,0},{10,2},{12,4},{14,6},{16,8},{18,10},{20,12},{22,14},{24,16},... | collective-permute-start | bytes 393224 | tf_op jit(solution)/shard_map/ppermute | solution.py:662
  156.9 20.1 %collective-permute-start.26 = (bf16[2,16,2048]{2,1,0:T(8,128)(2,1)S(1)}, bf16[2,16,2048]{2,1,0:T(8,128)(2,1)S(1)}, u32[]{:S(2)}, u32[]{:S(2)}) collective-permute-start(bf16[2,16,2048]{2,1,0:T(8,128)(2,1)S(1)} %get-tuple-element.72), channel_id=1, source_target_pairs={{16,0},{18,2},{20,4},{22,6},{24,8},{26,10},{28,12},{30,14},{17,1},... | collective-permute-start | bytes 393224 | tf_op jit(solution)/shard_map/ppermute | solution.py:662
  158.2 18.8 %collective-permute-start.27 = (bf16[2,16,2048]{2,1,0:T(8,128)(2,1)S(1)}, bf16[2,16,2048]{2,1,0:T(8,128)(2,1)S(1)}, u32[]{:S(2)}, u32[]{:S(2)}) collective-permute-start(bf16[2,16,2048]{2,1,0:T(8,128)(2,1)S(1)} %get-tuple-element.71), channel_id=1, source_target_pairs={{24,0},{26,2},{28,4},{30,6},{25,1},{27,3},{29,5},{31,7}} | collective-permute-start | bytes 393224 | tf_op jit(solution)/shard_map/ppermute | solution.py:662
  168.0 14.8 %copy-start.5 = (bf16[2,256,1024]{2,1,0:T(8,128)(2,1)}, bf16[2,256,1024]{2,1,0:T(8,128)(2,1)S(1)}, u32[]{:S(2)}) copy-start(bf16[2,256,1024]{2,1,0:T(8,128)(2,1)S(1)} %collective-permute-done.28.refs_3_) | copy-start | bytes 3145732
  177.1 5.0 %collective-permute-start.29 = (bf16[2,8,4096]{2,1,0:T(8,128)(2,1)S(1)}, bf16[2,8,4096]{2,1,0:T(8,128)(2,1)S(1)}, u32[]{:S(2)}, u32[]{:S(2)}) collective-permute-start(bf16[2,8,4096]{2,1,0:T(8,128)(2,1)S(1)} %pad_maximum_fusion.3), channel_id=1, source_target_pairs={{0,1},{1,0},{2,3},{3,2},{4,5},{5,4},{6,7},{7,6},{8,9},{9,8},{10,11... | collective-permute-start | bytes 393224 | tf_op jit(solution)/shard_map/ppermute | solution.py:673

commit v3 on v2

--- a/solution.py
+++ b/solution.py
@@ -460,7 +460,7 @@
     wide_pair = jax.ShapeDtypeStruct((2, rows_here, total_width), jnp.bfloat16)
     wide_pair_spec = pl.BlockSpec((2, rows_here, tile), lambda i: (0, 0, first + i))
     summ = jax.ShapeDtypeStruct((half_slots, 2, per_group, round_width), jnp.bfloat16)
-    mark = jax.ShapeDtypeStruct((per_group, total_width // 2), jnp.bfloat16)
+    mark = jax.ShapeDtypeStruct((per_group, 5 * total_width // 8), jnp.bfloat16)
     keys = caps.shape[0]
     heads = width // HD
     ahead = 6 + len(summaries)
@@ -494,31 +494,22 @@
     )(caps, *full, lower, *summaries, *wide_done, *round_done, *after)
 
 
-def finish_step(bounds, picker_ref, summ_ref, local_ref, *refs):
+def merge_step(bounds, local_ref, *refs):
     outs = refs[-2:]
-    count = len(bounds) - 1
     step = pl.program_id(0)
-    picker = picker_ref[...]
-    for part in range(count):
+    for part in range(len(bounds) - 1):
 
         @pl.when((step >= bounds[part]) & (step < bounds[part + 1]))
         def _():
-            back_ref = refs[part]
             for kind, out_ref in enumerate(outs):
-                spread = lax.dot_general(
-                    picker,
-                    summ_ref[kind],
-                    (((0,), (0,)), ((), ())),
-                    preferred_element_type=jnp.float32,
-                )
-                total = local_ref[kind].astype(jnp.float32) + back_ref[kind].astype(jnp.float32)
-                out_ref[...] = (total + spread).astype(jnp.bfloat16)
-
-
-def finish_call(picker, summ, local, backs):
-    rows_here = picker.shape[1]
-    few, total_width = summ.shape[1:]
+                total = local_ref[kind].astype(jnp.float32) + refs[part][kind].astype(jnp.float32)
+                out_ref[...] = total.astype(jnp.bfloat16)
+
+
+def merge_call(local, backs, first_col, carried):
+    _, rows_here, total_width = local.shape
     tile = functools.reduce(math.gcd, [part.shape[2] for part in backs], 4 * HD)
+    first = first_col // tile
     bounds = [sum(part.shape[2] for part in backs[:i]) // tile for i in range(len(backs) + 1)]
 
     def part_spec(part):
@@ -527,31 +518,88 @@
             (2, rows_here, tile), lambda i: (0, 0, jnp.clip(i - low, 0, high - low - 1))
         )
 
-    specs = [part_spec(part) for part in range(len(backs))]
-    wide_spec = pl.BlockSpec((rows_here, tile), lambda i: (0, i))
+    wide_spec = pl.BlockSpec((rows_here, tile), lambda i: (0, first + i))
     wide = jax.ShapeDtypeStruct((rows_here, total_width), jnp.bfloat16)
     return pl.pallas_call(
-        functools.partial(finish_step, bounds),
+        functools.partial(merge_step, bounds),
         grid=(bounds[-1],),
-        in_specs=[
-            pl.BlockSpec(picker.shape, lambda i: (0, 0)),
-            pl.BlockSpec((2, few, tile), lambda i: (0, 0, i)),
-        ]
-        + [pl.BlockSpec((2, rows_here, tile), lambda i: (0, 0, i))]
-        + specs,
+        in_specs=[pl.BlockSpec((2, rows_here, tile), lambda i: (0, 0, first + i))]
+        + [part_spec(part) for part in range(len(backs))]
+        + [pl.BlockSpec(memory_space=pl.ANY)] * len(carried),
         out_specs=[wide_spec, wide_spec],
         out_shape=[wide, wide],
+        input_output_aliases={1 + len(backs) + i: i for i in range(len(carried))},
         compiler_params=pltpu.CompilerParams(vmem_limit_bytes=VMEM_GRANT),
         cost_estimate=pl.CostEstimate(
-            flops=4 * few * rows_here * total_width,
-            bytes_accessed=6 * 2 * rows_here * total_width,
+            flops=2 * rows_here * tile * bounds[-1],
+            bytes_accessed=12 * rows_here * tile * bounds[-1],
             transcendentals=0,
         ),
-    )(picker, summ, local, *backs)
-
-
-def pick_step(place_ref, rows_ref, key_ref, val_ref, out_ref, picker_ref):
-    few, rows_here = picker_ref.shape
+    )(local, *backs, *carried)
+
+
+def place_step(rows_ref, summ_ref, key_ref, val_ref, key_out_ref, val_out_ref, tiles, sems):
+    _, few, tile, _ = tiles.shape
+
+    def copies(refs, back):
+        for kind, ref in enumerate(refs):
+            for step in range(few):
+                first = pl.multiple_of(rows_ref[step] // tile * tile, tile)
+                there = ref.at[pl.ds(first, tile), :]
+                here = tiles.at[kind, step]
+                yield pltpu.make_async_copy(
+                    here if back else there, there if back else here, sems.at[kind, step]
+                )
+
+    for copy in copies((key_ref, val_ref), False):
+        copy.start()
+    for copy in copies((key_ref, val_ref), False):
+        copy.wait()
+    row = lax.broadcasted_iota(jnp.int32, (tile, few), 0)
+    slot = lax.broadcasted_iota(jnp.int32, (tile, few), 1)
+    for step in range(few):
+        place = lax.rem(rows_ref[step], tile)
+        spread = jnp.where((row == place) & (slot == step), 1.0, 0.0).astype(jnp.bfloat16)
+        for kind in range(2):
+            moved = jnp.dot(spread, summ_ref[kind], preferred_element_type=jnp.float32)
+            total = tiles[kind, step].astype(jnp.float32) + moved
+            tiles[kind, step] = total.astype(jnp.bfloat16)
+    for copy in copies((key_out_ref, val_out_ref), True):
+        copy.start()
+    for copy in copies((key_out_ref, val_out_ref), True):
+        copy.wait()
+
+
+def place_call(rows, summ, key_grad, val_grad):
+    _, few, total_width = summ.shape
+    any_spec = pl.BlockSpec(memory_space=pl.ANY)
+    wide = jax.ShapeDtypeStruct(key_grad.shape, key_grad.dtype)
+    return pl.pallas_call(
+        place_step,
+        in_specs=[
+            pl.BlockSpec(memory_space=pltpu.SMEM),
+            pl.BlockSpec(memory_space=pltpu.VMEM),
+            any_spec,
+            any_spec,
+        ],
+        out_specs=[any_spec, any_spec],
+        out_shape=[wide, wide],
+        scratch_shapes=[
+            pltpu.VMEM((2, few, 16, total_width), jnp.bfloat16),
+            pltpu.SemaphoreType.DMA((2, few)),
+        ],
+        input_output_aliases={2: 0, 3: 1},
+        compiler_params=pltpu.CompilerParams(vmem_limit_bytes=VMEM_GRANT),
+        cost_estimate=pl.CostEstimate(
+            flops=64 * few * few * total_width,
+            bytes_accessed=128 * few * total_width,
+            transcendentals=0,
+        ),
+    )(rows, summ, key_grad, val_grad)
+
+
+def pick_step(place_ref, rows_ref, key_ref, val_ref, out_ref):
+    few, rows_here = out_ref.shape[1], key_ref.shape[0]
     half = place_ref[0]
     row = lax.broadcasted_iota(jnp.int32, (few, rows_here), 0)
     wanted = jnp.full((few, rows_here), -1, jnp.int32)
@@ -559,7 +607,6 @@
         wanted = jnp.where(row == i, rows_ref[0, half * few + i] - half * rows_here, wanted)
     hit = lax.broadcasted_iota(jnp.int32, (few, rows_here), 1) == wanted
     picker = jnp.where(hit, 1.0, 0.0).astype(jnp.bfloat16)
-    picker_ref[...] = picker
     for kind, ref in enumerate((key_ref, val_ref)):
         rows = jnp.dot(picker, ref[...], preferred_element_type=jnp.float32)
         out_ref[kind] = rows.astype(jnp.bfloat16)
@@ -575,14 +622,8 @@
         pick_step,
         grid=(total_width // tile,),
         in_specs=[smem, smem, wide_spec, wide_spec],
-        out_specs=[
-            pl.BlockSpec((2, few, tile), lambda i: (0, 0, i)),
-            pl.BlockSpec((few, rows_here), lambda i: (0, 0)),
-        ],
-        out_shape=[
-            jax.ShapeDtypeStruct((2, few, total_width), jnp.bfloat16),
-            jax.ShapeDtypeStruct((few, rows_here), jnp.bfloat16),
-        ],
+        out_specs=pl.BlockSpec((2, few, tile), lambda i: (0, 0, i)),
+        out_shape=jax.ShapeDtypeStruct((2, few, total_width), jnp.bfloat16),
         compiler_params=pltpu.CompilerParams(vmem_limit_bytes=VMEM_GRANT),
     )(half[None], summary_rows, key_vectors, value_vectors)
 
@@ -621,11 +662,11 @@
         return [(i + 4 * step, i) for i in range(seq_count - 4 * step)]
 
     unit = total_width // 8
-    chunks = [1, 3, 2, 2]
+    chunks = [1, 2, 3, 2]
     gather_starts = [0, 2]
     edges = [sum(chunks[:i]) for i in range(len(chunks) + 1)]
 
-    mine, picker = pick_call(half, summary_rows, key_vectors, value_vectors)
+    mine = pick_call(half, summary_rows, key_vectors, value_vectors)
     other = lax.ppermute(mine, "head", flip_half)
 
     def lower_pair(first, last, zeros=None):
@@ -641,8 +682,10 @@
     def span(first, last):
         return slice(edges[first] * unit, edges[last] * unit)
 
-    def climb_stages(first, last):
+    def climb_stages(first, last, before=None):
         ladder = both[:, :, span(first, last)][None]
+        if before is not None:
+            ladder = ladder + jnp.minimum(jnp.abs(before[1, :1, :1, :1]), 0)
         return jnp.concatenate(
             [ladder] + [lax.ppermute(ladder, "seq", climb(i)) for i in range(1, stages)], axis=0
         )
@@ -706,21 +749,25 @@
         marks.append(out[-1])
         return tuple(out[4:-1])
 
+    rows_mine = lax.dynamic_slice_in_dim(summary_rows[0], half * few, few, 0) - half * rows_here
 
     lower_pair(0, 2)
     ladder = climb_stages(0, 2)
+    first_ladder = ladder
     side = lax.ppermute(ladder, "seq", flip_side)
     lower_pair(2, 3, jnp.minimum(jnp.abs(side[0, 0]), 0))
     gathered.append(with_other_core(jnp.concatenate([ladder, side], axis=0)))
-    ladder = climb_stages(2, 4)
-    side = lax.ppermute(ladder, "seq", flip_side)
+    ladder = climb_stages(2, 4, first_ladder)
     done = attend(0, 0, 0, 2, (), ())
     lower_pair(3, 4, marks[0])
-    near = wait_for(jnp.concatenate([ladder, side], axis=0), marks[0])
+    ladder = wait_for(ladder, marks[0])
+    side = lax.ppermute(ladder, "seq", flip_side)
+    done = attend(1, 0, 0, 2, done, ())
+    near = wait_for(jnp.concatenate([ladder, side], axis=0), marks[1])
+    near = wait_for_moved(near, backs[0])
     gathered.append(with_other_core(near))
-    done = attend(1, 0, 0, 2, done, ())
     chip_a = reduce_chip(*done)
-    done = attend(2, 1, 2, 3, (), (backs[0],))
+    done = attend(2, 1, 2, 3, (), ())
     chip_a = wait_for(chip_a, marks[2])
     plane_a = reduce_plane(chip_a)
     chip_b = reduce_chip(*done)
@@ -730,9 +777,11 @@
     chip_c = wait_for_moved(reduce_chip(*done), backs[2])
     plane_c = reduce_plane(chip_c)
     group_a = reduce_group_halving(plane_a)
-    group_b = reduce_group(jnp.concatenate([plane_b, plane_c], axis=3))
-    group_b = wait_for_moved(group_b, backs[3])
-    finished = finish_call(picker, reduce_half([group_a, group_b]), wide_done[2], backs)
+    merged = merge_call(wide_done[2], backs[:3], 0, ())
+    plane_b = wait_for_moved(jnp.concatenate([plane_b, plane_c], axis=3), merged[0][None])
+    group_b = wait_for_moved(reduce_group(plane_b), backs[3])
+    merged = merge_call(wide_done[2], backs[3:], edges[3] * unit, tuple(merged))
+    finished = place_call(rows_mine, reduce_half([group_a, group_b]), *merged)
     return (*wide_done[:2], *finished)
 
 

time: 193 us -> 184 us (0.953)
  waiting for transfers between devices: 58.9 us -> 37.7 us
  Pallas kernels: 55.5 us -> 60.1 us
  other arithmetic: 10.7 us -> 14.4 us
  between operations: 2.62 us -> 4.6 us
    ppermute x2, waiting for transfers between devices: 12.1 us -> 5.13 us  [token_split(): side = lax.ppermute(ladder, 'seq', flip_side)]
    ppermute x2, waiting for transfers between devices: 3.58 us -> 9.8 us  [reduce_group_halving(): lax.ppermute(plane[size:], 'seq', descend(size))]
    ppermute x4, waiting for transfers between devices: 18.7 us -> 13.8 us  [attend(): backs.append(lax.ppermute(out[3], 'head', [(1, 0)]))]
    ppermute x1, waiting for transfers between devices: 4.95 us -> 0.36 us  [reduce_half(): lax.ppermute(group[:, few:], 'head', flip_half)]
    pallas_call x1 -> x3, Pallas kernels: 8.95 us -> 13.5 us  [the longest x2 8.82 us: merge_call(): pl.pallas_call(functools.partial(merge_step, bounds), grid=(bounds[-1],),...]
    ppermute x3, waiting for transfers between devices: 4.15 us -> 0.01 us  [reduce_plane(): lax.ppermute(chip[stages:], 'seq', flip_side)]
    ppermute x3, starting transfers between devices: 4.61 us -> 1.76 us  [reduce_plane(): lax.ppermute(chip[stages:], 'seq', flip_side)]
    ppermute x3, waiting for transfers between devices: 5.27 us -> 2.87 us  [lower_pair(): lowers.append(lax.ppermute(pair, 'head', [(0, 1)]))]
  transfers between devices with their start and end apart: 30 -> 30, of which waited for: 13 -> 8; matrix products, arithmetic and copies ran while one was open for 10% -> 14% of each run, Pallas kernels for 22% -> 28%
where the time goes in v3:
time: 184 us; the launch traced here: 183 us
  Pallas kernels  60.1 us (33%)
  starting transfers between devices  52.7 us (29%)
  waiting for transfers between devices  37.7 us (20%)
  other arithmetic  14.4 us (8%)
  local copies, waits for them, and re-layouts  13.5 us (7%)
  between operations  4.6 us (2%)
    pallas_call x4, Pallas kernels, attention_call(): pl.pallas_call(functools.partial(attention_step, len(summaries)), grid=(w...  40.6 us
    ppermute x6, starting transfers between devices, climb_stages(): lax.ppermute(ladder, 'seq', climb(i))  19 us
    ppermute x4, waiting for transfers between devices, attend(): backs.append(lax.ppermute(out[3], 'head', [(1, 0)]))  13.8 us
    ppermute x3, starting transfers between devices, lower_pair(): lowers.append(lax.ppermute(pair, 'head', [(0, 1)]))  12.2 us
    ppermute x2, waiting for transfers between devices, reduce_group_halving(): lax.ppermute(plane[size:], 'seq', descend(size))  9.8 us
    pallas_call x2, Pallas kernels, merge_call(): pl.pallas_call(functools.partial(merge_step, bounds), grid=(bounds[-1],),...  8.82 us
    ppermute x3, waiting for transfers between devices, reduce_group(): lax.ppermute(plane[i], 'seq', descend(i))  5.63 us
    ppermute x4, starting transfers between devices, attend(): backs.append(lax.ppermute(out[3], 'head', [(1, 0)]))  5.26 us
  transfers between devices with their start and end apart: 30, of which 8 were waited for; matrix products, arithmetic and copies ran while one was open for 14% of the time, Pallas kernels for 28%

profile of v3, /device:TPU:0, one launch (start us, length us, event | category | flops | bytes accessed | tf_op | source)
XLA Modules:
  0.0 183.1 jit_solution(3861461976953293765)
XLA Ops:
  0.6 4.4 %shard_map.94 = bf16[2,8,4096]{2,1,0:T(8,128)(2,1)} custom-call(s32[1]{0:T(128)} %bitcast.place_ref, s32[1,16]{1,0:T(1,128)} %rows_ref.1, bf16[256,4096]{1,0:T(8,128)(2,1)} %key_ref.9, bf16[256,4096]{1,0:T(8,128)(2,1)} %val_ref.9), custom_call_target="tpu_custom_call" | custom-call | tf_op jit(solution)/shard_map/pallas_call | solution.py:621
  5.0 3.0 %collective-permute-start.1 = (bf16[2,8,4096]{2,1,0:T(8,128)(2,1)}, bf16[2,8,4096]{2,1,0:T(8,128)(2,1)S(1)}, u32[]{:S(2)}, u32[]{:S(2)}) collective-permute-start(bf16[2,8,4096]{2,1,0:T(8,128)(2,1)} %shard_map.94), channel_id=1, source_target_pairs={{0,1},{1,0},{2,3},{3,2},{4,5},{5,4},{6,7},{7,6},{8,9},{9,8},{10,11... | collective-permute-start | bytes 393224 | tf_op jit(solution)/shard_map/ppermute | solution.py:670
  8.0 1.6 slice_bitcast_fusion
  9.6 1.3 pad_maximum_fusion
  10.9 3.1 %collective-permute-start = (bf16[2,256,1536]{2,1,0:T(8,128)(2,1)}, bf16[2,256,1536]{2,1,0:T(8,128)(2,1)}, u32[]{:S(2)}, u32[]{:S(2)}) collective-permute-start(bf16[2,256,1536]{2,1,0:T(8,128)(2,1)} %pad_maximum_fusion), channel_id=1, source_target_pairs={{0,1},{2,3},{4,5},{6,7},{8,9},{10,11},{12,13},{14,15},{16,17},{18,... | collective-permute-start | bytes 4718600 | tf_op jit(solution)/shard_map/ppermute | solution.py:677
  14.7 4.0 %collective-permute-start.2 = (bf16[1,2,16,1536]{3,2,1,0:T(8,128)(2,1)S(1)}, bf16[1,2,16,1536]{3,2,1,0:T(8,128)(2,1)S(1)}, u32[]{:S(2)}, u32[]{:S(2)}) collective-permute-start(bf16[1,2,16,1536]{3,2,1,0:T(8,128)(2,1)S(1)} %get-tuple-element.73), channel_id=1, source_target_pairs={{0,8},{2,10},{4,12},{6,14},{8,16},{10,18},{12,20},{14,22},{16,24},... | collective-permute-start | bytes 294920 | tf_op jit(solution)/shard_map/ppermute | solution.py:690
  18.7 4.5 %collective-permute-start.3 = (bf16[1,2,16,1536]{3,2,1,0:T(8,128)(2,1)S(1)}, bf16[1,2,16,1536]{3,2,1,0:T(8,128)(2,1)S(1)}, u32[]{:S(2)}, u32[]{:S(2)}) collective-permute-start(bf16[1,2,16,1536]{3,2,1,0:T(8,128)(2,1)S(1)} %get-tuple-element.73), channel_id=1, source_target_pairs={{0,16},{2,18},{4,20},{6,22},{8,24},{10,26},{12,28},{14,30},{1,17},... | collective-permute-start | bytes 294920 | tf_op jit(solution)/shard_map/ppermute | solution.py:690
  23.2 1.3 collective-permute-start.4
  25.2 1.7 shard_map.93.caps_ref
  27.0 1.6 collective-permute-start.5
  31.7 5.1 %collective-permute-done.5 = bf16[4,2,16,1536]{3,2,1,0:T(8,128)(2,1)S(1)} collective-permute-done((bf16[4,2,16,1536]{3,2,1,0:T(8,128)(2,1)S(1)}, bf16[4,2,16,1536]{3,2,1,0:T(8,128)(2,1)S(1)}, u32[]{:S(2)}, u32[]{:S(2)}) %collective-permute-start.5) | collective-permute-done | bytes 393248 | tf_op jit(solution)/shard_map/ppermute | solution.py:757
  37.6 5.4 %collective-permute-start.10 = (bf16[1,2,16,2560]{3,2,1,0:T(8,128)(2,1)S(1)}, bf16[1,2,16,2560]{3,2,1,0:T(8,128)(2,1)S(1)}, u32[]{:S(2)}, u32[]{:S(2)}) collective-permute-start(bf16[1,2,16,2560]{3,2,1,0:T(8,128)(2,1)S(1)} %fusion.9), channel_id=1, source_target_pairs={{0,24},{2,26},{4,28},{6,30},{1,25},{3,27},{5,29},{7,31}} | collective-permute-start | bytes 491528 | tf_op jit(solution)/shard_map/ppermute | solution.py:690
  43.1 1.3 collective-permute-start.8
  44.4 2.5 %collective-permute-start.9 = (bf16[1,2,16,2560]{3,2,1,0:T(8,128)(2,1)S(1)}, bf16[1,2,16,2560]{3,2,1,0:T(8,128)(2,1)S(1)}, u32[]{:S(2)}, u32[]{:S(2)}) collective-permute-start(bf16[1,2,16,2560]{3,2,1,0:T(8,128)(2,1)S(1)} %fusion.9), channel_id=1, source_target_pairs={{0,16},{2,18},{4,20},{6,22},{8,24},{10,26},{12,28},{14,30},{1,17},... | collective-permute-start | bytes 491528 | tf_op jit(solution)/shard_map/ppermute | solution.py:690
  46.9 1.3 maximum_add_fusion
  48.2 2.5 %collective-permute-start.14 = (bf16[2,256,1536]{2,1,0:T(8,128)(2,1)}, bf16[2,256,1536]{2,1,0:T(8,128)(2,1)}, u32[]{:S(2)}, u32[]{:S(2)}) collective-permute-start(bf16[2,256,1536]{2,1,0:T(8,128)(2,1)} %maximum_add_fusion), channel_id=1, source_target_pairs={{0,1},{2,3},{4,5},{6,7},{8,9},{10,11},{12,13},{14,15},{16,17},{18,... | collective-permute-start | bytes 4718600 | tf_op jit(solution)/shard_map/ppermute | solution.py:677
  50.7 6.4 %shard_map.95 = (bf16[256,4096]{1,0:T(8,128)(2,1)}, bf16[256,4096]{1,0:T(8,128)(2,1)}, bf16[2,256,4096]{2,1,0:T(8,128)(2,1)}, bf16[2,256,512]{2,1,0:T(8,128)(2,1...) custom-call(f32[768,256]{1,0:T(8,128)} %shard_map.93.caps_ref, ...), custom_call_target="tpu_custom_call" | custom-call | flops 5637144576 | bytes 4194304 | tf_op jit(solution)/shard_map/pallas_call | solution.py:469
  58.0 1.6 collective-permute-start.11
  59.6 1.3 collective-permute-start.12
  60.9 10.1 %shard_map.96 = (bf16[256,4096]{1,0:T(8,128)(2,1)}, bf16[256,4096]{1,0:T(8,128)(2,1)}, bf16[2,256,4096]{2,1,0:T(8,128)(2,1)}, bf16[2,256,1024]{2,1,0:T(8,128)(2,...) custom-call(f32[768,256]{1,0:T(8,128)} %shard_map.93.caps_ref, ...), custom_call_target="tpu_custom_call", output_to_operand_aliasing={{0}: (8, {}), {1}: (9, {}), {2}: (10, {}), {4}: (11, {}), {... | custom-call | flops 11274289152 | bytes 8388608 | tf_op jit(solution)/shard_map/pallas_call | solution.py:469
  71.0 4.2 %collective-permute-done.12.refs_0_ = bf16[2,256,512]{2,1,0:T(8,128)(2,1)S(1)} collective-permute-done((bf16[2,256,512]{2,1,0:T(8,128)(2,1)}, bf16[2,256,512]{2,1,0:T(8,128)(2,1)S(1)}, u32[]{:S(2)}, u32[]{:S(2)}) %collective-permute-start.12) | collective-permute-done | bytes 524320 | tf_op jit(solution)/shard_map/ppermute | solution.py:748
  77.5 1.7 slice_bitcast_fusion.4
  79.4 1.3 collective-permute-start.15
  81.4 1.1 maximum_add_fusion.2
  82.5 6.6 %collective-permute-start.7 = (bf16[2,256,1024]{2,1,0:T(8,128)(2,1)}, bf16[2,256,1024]{2,1,0:T(8,128)(2,1)}, u32[]{:S(2)}, u32[]{:S(2)}) collective-permute-start(bf16[2,256,1024]{2,1,0:T(8,128)(2,1)} %maximum_add_fusion.2), channel_id=1, source_target_pairs={{0,1},{2,3},{4,5},{6,7},{8,9},{10,11},{12,13},{14,15},{16,17},{18,... | collective-permute-start | bytes 3145736 | tf_op jit(solution)/shard_map/ppermute | solution.py:677
  89.1 1.1 copy-done.11
  90.2 13.9 %shard_map.97 = (bf16[256,4096]{1,0:T(8,128)(2,1)}, bf16[256,4096]{1,0:T(8,128)(2,1)}, bf16[2,256,4096]{2,1,0:T(8,128)(2,1)}, bf16[2,256,1536]{2,1,0:T(8,128)(2,...) custom-call(f32[768,256]{1,0:T(8,128)} %shard_map.93.caps_ref, ...), custom_call_target="tpu_custom_call", output_to_operand_aliasing={{0}: (8, {}), {1}: (9, {}), {2}: (10, {})} | custom-call | flops 16911433728 | bytes 12582912 | tf_op jit(solution)/shard_map/pallas_call | solution.py:469
  104.9 1.3 collective-permute-start.23
  106.2 1.4 fusion.1.rest_6_
  108.2 2.9 %collective-permute-done.7.lower_ref = bf16[2,256,1024]{2,1,0:T(8,128)(2,1)} collective-permute-done((bf16[2,256,1024]{2,1,0:T(8,128)(2,1)}, bf16[2,256,1024]{2,1,0:T(8,128)(2,1)}, u32[]{:S(2)}, u32[]{:S(2)}) %collective-permute-start.7) | collective-permute-done | bytes 1048608 | tf_op jit(solution)/shard_map/ppermute | solution.py:677
  111.1 10.2 %shard_map.98 = (bf16[256,4096]{1,0:T(8,128)(2,1)}, bf16[256,4096]{1,0:T(8,128)(2,1)}, bf16[2,256,4096]{2,1,0:T(8,128)(2,1)}, bf16[2,256,1024]{2,1,0:T(8,128)(2,...) custom-call(f32[768,256]{1,0:T(8,128)} %shard_map.93.caps_ref, ...), custom_call_target="tpu_custom_call", output_to_operand_aliasing={{0}: (8, {}), {1}: (9, {}), {2}: (10, {})} | custom-call | flops 11274289152 | bytes 8388608 | tf_op jit(solution)/shard_map/pallas_call | solution.py:469
  121.3 1.4 collective-permute-start.28
  123.5 1.2 add_convert_fusion.4
  124.8 1.5 collective-permute-start.18
  126.3 1.5 fusion.2
  128.4 9.8 %collective-permute-done.18 = bf16[2,2,16,1536]{3,2,1,0:T(8,128)(2,1)S(1)} collective-permute-done((bf16[2,2,16,1536]{3,2,1,0:T(8,128)(2,1)S(1)}, bf16[2,2,16,1536]{3,2,1,0:T(8,128)(2,1)S(1)}, u32[]{:S(2)}, u32[]{:S(2)}) %collective-permute-start.18) | collective-permute-done | bytes 196640 | tf_op jit(solution)/shard_map/ppermute | solution.py:711
  138.2 1.3 collective-permute-start.19
  139.6 4.7 %collective-permute-done.23.refs_2_ = bf16[2,256,1536]{2,1,0:T(8,128)(2,1)S(1)} collective-permute-done((bf16[2,256,1536]{2,1,0:T(8,128)(2,1)}, bf16[2,256,1536]{2,1,0:T(8,128)(2,1)S(1)}, u32[]{:S(2)}, u32[]{:S(2)}) %collective-permute-start.23) | collective-permute-done | bytes 1572896 | tf_op jit(solution)/shard_map/ppermute | solution.py:748
  146.4 6.4 %shard_map.99 = (bf16[256,4096]{1,0:T(8,128)(2,1)}, bf16[256,4096]{1,0:T(8,128)(2,1)}) custom-call(bf16[2,256,4096]{2,1,0:T(8,128)(2,1)} %get-tuple-element.64.local_ref, bf16[2,256,512]{2,1,0:T(8,128)(2,1)} %copy-done.8, bf16[2,256,1024]{2,1,0:T(8,128)(2,1)} %collective-permute-done.15.rest_5_.refs_1_, bf16[2,256,1536]{2,1,0:T(8,128)(2,1)} %copy-done.2), custom_call_target="tpu_custom_call" | custom-call | flops 1572864 | bytes 9437184 | tf_op jit(solution)/shard_map/pallas_call | solution.py:523
  152.8 1.2 slice.152
  155.8 1.3 collective-permute-start.25
  157.1 1.3 collective-permute-start.26
  158.4 1.3 collective-permute-start.27
  160.7 4.9 %collective-permute-done.28.refs_0_ = bf16[2,256,1024]{2,1,0:T(8,128)(2,1)S(1)} collective-permute-done((bf16[2,256,1024]{2,1,0:T(8,128)(2,1)}, bf16[2,256,1024]{2,1,0:T(8,128)(2,1)S(1)}, u32[]{:S(2)}, u32[]{:S(2)}) %collective-permute-start.28) | collective-permute-done | bytes 1048608 | tf_op jit(solution)/shard_map/ppermute | solution.py:748
  166.8 5.6 %collective-permute-done.26 = bf16[2,16,2560]{2,1,0:T(8,128)(2,1)S(1)} collective-permute-done((bf16[2,16,2560]{2,1,0:T(8,128)(2,1)S(1)}, bf16[2,16,2560]{2,1,0:T(8,128)(2,1)S(1)}, u32[]{:S(2)}, u32[]{:S(2)}) %collective-permute-start.26) | collective-permute-done | bytes 163872 | tf_op jit(solution)/shard_map/ppermute | solution.py:705
  172.6 1.6 collective-permute-start.29
  174.8 2.4 %shard_map.100 = (bf16[256,4096]{1,0:T(8,128)(2,1)}, bf16[256,4096]{1,0:T(8,128)(2,1)}) custom-call(bf16[2,256,4096]{2,1,0:T(8,128)(2,1)} %get-tuple-element.64.local_ref, bf16[2,256,1024]{2,1,0:T(8,128)(2,1)} %copy-done.5, bf16[256,4096]{1,0:T(8,128)(2,1)} %get-tuple-element.65.refs_1_, ...), custom_call_target="tpu_custom_call", output_to_operand_aliasing={{0}: (2, {}), {1}: (3, {})} | custom-call | flops 524288 | bytes 3145728 | tf_op jit(solution)/shard_map/pallas_call | solution.py:523
  178.3 4.6 %shard_map.101 = (bf16[256,4096]{1,0:T(8,128)(2,1)}, bf16[256,4096]{1,0:T(8,128)(2,1)}) custom-call(s32[8]{0:T(128)} %subtract_bitcast_fusion.rows_ref, bf16[2,8,4096]{2,1,0:T(8,128)(2,1)} %add_convert_fusion.7.summ_ref, bf16[256,4096]{1,0:T(8,128)(2,1)} %get-tuple-element.68.key_ref, ...), custom_call_target="tpu_custom_call", output_to_operand_aliasing={{0}: (2, {}), {1}: (3, {})} | custom-call | flops 16777216 | bytes 4194304 | tf_op jit(solution)/shard_map/pallas_call | solution.py:577
  (95 shorter events, 17.2 us)
Async XLA Ops:
  0.6 7.4 %copy-start = (bf16[256,4096]{1,0:T(8,128)(2,1)S(1)}, bf16[256,4096]{1,0:T(8,128)(2,1)}, u32[]{:S(2)}) copy-start(bf16[256,4096]{1,0:T(8,128)(2,1)} %key_ref.9) | copy-start | bytes 6291460
  5.0 9.0 %collective-permute-start.1 = (bf16[2,8,4096]{2,1,0:T(8,128)(2,1)}, bf16[2,8,4096]{2,1,0:T(8,128)(2,1)S(1)}, u32[]{:S(2)}, u32[]{:S(2)}) collective-permute-start(bf16[2,8,4096]{2,1,0:T(8,128)(2,1)} %shard_map.94), channel_id=1, source_target_pairs={{0,1},{1,0},{2,3},{3,2},{4,5},{5,4},{6,7},{7,6},{8,9},{9,8},{10,11... | collective-permute-start | bytes 393224 | tf_op jit(solution)/shard_map/ppermute | solution.py:670
  9.6 4.5 %copy-start.4 = (bf16[2,8,4096]{2,1,0:T(8,128)(2,1)S(1)}, bf16[2,8,4096]{2,1,0:T(8,128)(2,1)}, u32[]{:S(2)}) copy-start(bf16[2,8,4096]{2,1,0:T(8,128)(2,1)} %shard_map.94) | copy-start | bytes 393220
  10.9 39.8 %collective-permute-start = (bf16[2,256,1536]{2,1,0:T(8,128)(2,1)}, bf16[2,256,1536]{2,1,0:T(8,128)(2,1)}, u32[]{:S(2)}, u32[]{:S(2)}) collective-permute-start(bf16[2,256,1536]{2,1,0:T(8,128)(2,1)} %pad_maximum_fusion), channel_id=1, source_target_pairs={{0,1},{2,3},{4,5},{6,7},{8,9},{10,11},{12,13},{14,15},{16,17},{18,... | collective-permute-start | bytes 4718600 | tf_op jit(solution)/shard_map/ppermute | solution.py:677
  14.7 12.2 %collective-permute-start.2 = (bf16[1,2,16,1536]{3,2,1,0:T(8,128)(2,1)S(1)}, bf16[1,2,16,1536]{3,2,1,0:T(8,128)(2,1)S(1)}, u32[]{:S(2)}, u32[]{:S(2)}) collective-permute-start(bf16[1,2,16,1536]{3,2,1,0:T(8,128)(2,1)S(1)} %get-tuple-element.73), channel_id=1, source_target_pairs={{0,8},{2,10},{4,12},{6,14},{8,16},{10,18},{12,20},{14,22},{16,24},... | collective-permute-start | bytes 294920 | tf_op jit(solution)/shard_map/ppermute | solution.py:690
  18.7 8.2 %collective-permute-start.3 = (bf16[1,2,16,1536]{3,2,1,0:T(8,128)(2,1)S(1)}, bf16[1,2,16,1536]{3,2,1,0:T(8,128)(2,1)S(1)}, u32[]{:S(2)}, u32[]{:S(2)}) collective-permute-start(bf16[1,2,16,1536]{3,2,1,0:T(8,128)(2,1)S(1)} %get-tuple-element.73), channel_id=1, source_target_pairs={{0,16},{2,18},{4,20},{6,22},{8,24},{10,26},{12,28},{14,30},{1,17},... | collective-permute-start | bytes 294920 | tf_op jit(solution)/shard_map/ppermute | solution.py:690
  23.2 3.7 %collective-permute-start.4 = (bf16[1,2,16,1536]{3,2,1,0:T(8,128)(2,1)S(1)}, bf16[1,2,16,1536]{3,2,1,0:T(8,128)(2,1)S(1)}, u32[]{:S(2)}, u32[]{:S(2)}) collective-permute-start(bf16[1,2,16,1536]{3,2,1,0:T(8,128)(2,1)S(1)} %get-tuple-element.73), channel_id=1, source_target_pairs={{0,24},{2,26},{4,28},{6,30},{1,25},{3,27},{5,29},{7,31}} | collective-permute-start | bytes 294920 | tf_op jit(solution)/shard_map/ppermute | solution.py:690
  27.0 9.8 %collective-permute-start.5 = (bf16[4,2,16,1536]{3,2,1,0:T(8,128)(2,1)S(1)}, bf16[4,2,16,1536]{3,2,1,0:T(8,128)(2,1)S(1)}, u32[]{:S(2)}, u32[]{:S(2)}) collective-permute-start(bf16[4,2,16,1536]{3,2,1,0:T(8,128)(2,1)S(1)} %pad_maximum_fusion.1), channel_id=1, source_target_pairs={{0,4},{2,6},{4,0},{6,2},{8,12},{10,14},{12,8},{14,10},{16,20},{18,... | collective-permute-start | bytes 1179656 | tf_op jit(solution)/shard_map/ppermute | solution.py:757
  37.6 10.6 %collective-permute-start.6 = (bf16[8,2,16,1536]{3,2,1,0:T(8,128)(2,1)}, bf16[8,2,16,1536]{3,2,1,0:T(8,128)(2,1)}, u32[]{:S(2)}, u32[]{:S(2)}) collective-permute-start(bf16[8,2,16,1536]{3,2,1,0:T(8,128)(2,1)} %constant_dynamic-update-slice_fusion.rest_0_), channel_id=1, source_target_pairs={{0,2},{2,0},{4,6},{6,4},{8,10},{10,8},{12,14},{14,12},{16,18},{18,... | collective-permute-start | bytes 2359304 | tf_op jit(solution)/shard_map/ppermute | solution.py:694
  37.6 19.4 %collective-permute-start.10 = (bf16[1,2,16,2560]{3,2,1,0:T(8,128)(2,1)S(1)}, bf16[1,2,16,2560]{3,2,1,0:T(8,128)(2,1)S(1)}, u32[]{:S(2)}, u32[]{:S(2)}) collective-permute-start(bf16[1,2,16,2560]{3,2,1,0:T(8,128)(2,1)S(1)} %fusion.9), channel_id=1, source_target_pairs={{0,24},{2,26},{4,28},{6,30},{1,25},{3,27},{5,29},{7,31}} | collective-permute-start | bytes 491528 | tf_op jit(solution)/shard_map/ppermute | solution.py:690
  43.1 14.0 %collective-permute-start.8 = (bf16[1,2,16,2560]{3,2,1,0:T(8,128)(2,1)S(1)}, bf16[1,2,16,2560]{3,2,1,0:T(8,128)(2,1)S(1)}, u32[]{:S(2)}, u32[]{:S(2)}) collective-permute-start(bf16[1,2,16,2560]{3,2,1,0:T(8,128)(2,1)S(1)} %fusion.9), channel_id=1, source_target_pairs={{0,8},{2,10},{4,12},{6,14},{8,16},{10,18},{12,20},{14,22},{16,24},... | collective-permute-start | bytes 491528 | tf_op jit(solution)/shard_map/ppermute | solution.py:690
  44.4 12.7 %collective-permute-start.9 = (bf16[1,2,16,2560]{3,2,1,0:T(8,128)(2,1)S(1)}, bf16[1,2,16,2560]{3,2,1,0:T(8,128)(2,1)S(1)}, u32[]{:S(2)}, u32[]{:S(2)}) collective-permute-start(bf16[1,2,16,2560]{3,2,1,0:T(8,128)(2,1)S(1)} %fusion.9), channel_id=1, source_target_pairs={{0,16},{2,18},{4,20},{6,22},{8,24},{10,26},{12,28},{14,30},{1,17},... | collective-permute-start | bytes 491528 | tf_op jit(solution)/shard_map/ppermute | solution.py:690
  48.2 40.9 %collective-permute-start.14 = (bf16[2,256,1536]{2,1,0:T(8,128)(2,1)}, bf16[2,256,1536]{2,1,0:T(8,128)(2,1)}, u32[]{:S(2)}, u32[]{:S(2)}) collective-permute-start(bf16[2,256,1536]{2,1,0:T(8,128)(2,1)} %maximum_add_fusion), channel_id=1, source_target_pairs={{0,1},{2,3},{4,5},{6,7},{8,9},{10,11},{12,13},{14,15},{16,17},{18,... | collective-permute-start | bytes 4718600 | tf_op jit(solution)/shard_map/ppermute | solution.py:677
  58.0 18.4 %collective-permute-start.11 = (bf16[4,2,16,2560]{3,2,1,0:T(8,128)(2,1)S(1)}, bf16[4,2,16,2560]{3,2,1,0:T(8,128)(2,1)S(1)}, u32[]{:S(2)}, u32[]{:S(2)}) collective-permute-start(bf16[4,2,16,2560]{3,2,1,0:T(8,128)(2,1)S(1)} %maximum_add_fusion.3), channel_id=1, source_target_pairs={{0,4},{2,6},{4,0},{6,2},{8,12},{10,14},{12,8},{14,10},{16,20},{18,... | collective-permute-start | bytes 1966088 | tf_op jit(solution)/shard_map/ppermute | solution.py:764
  59.6 15.6 %collective-permute-start.12 = (bf16[2,256,512]{2,1,0:T(8,128)(2,1)}, bf16[2,256,512]{2,1,0:T(8,128)(2,1)S(1)}, u32[]{:S(2)}, u32[]{:S(2)}) collective-permute-start(bf16[2,256,512]{2,1,0:T(8,128)(2,1)} %get-tuple-element.45), channel_id=1, source_target_pairs={{1,0},{3,2},{5,4},{7,6},{9,8},{11,10},{13,12},{15,14},{17,16},{19,... | collective-permute-start | bytes 1572872 | tf_op jit(solution)/shard_map/ppermute | solution.py:748
  75.2 4.0 %copy-start.8 = (bf16[2,256,512]{2,1,0:T(8,128)(2,1)}, bf16[2,256,512]{2,1,0:T(8,128)(2,1)S(1)}, u32[]{:S(2)}) copy-start(bf16[2,256,512]{2,1,0:T(8,128)(2,1)S(1)} %collective-permute-done.12.refs_0_) | copy-start | bytes 1572868
  77.4 5.0 %copy-start.3 = (bf16[8,2,16,2560]{3,2,1,0:T(8,128)(2,1)}, bf16[8,2,16,2560]{3,2,1,0:T(8,128)(2,1)S(1)}, u32[]{:S(2)}) copy-start(bf16[8,2,16,2560]{3,2,1,0:T(8,128)(2,1)S(1)} %fusion.rest_0_) | copy-start | bytes 3932164
  77.4 11.7 %collective-permute-start.13 = (bf16[8,2,16,2560]{3,2,1,0:T(8,128)(2,1)S(1)}, bf16[8,2,16,2560]{3,2,1,0:T(8,128)(2,1)S(1)}, u32[]{:S(2)}, u32[]{:S(2)}) collective-permute-start(bf16[8,2,16,2560]{3,2,1,0:T(8,128)(2,1)S(1)} %fusion.rest_0_), channel_id=1, source_target_pairs={{0,2},{2,0},{4,6},{6,4},{8,10},{10,8},{12,14},{14,12},{16,18},{18,... | collective-permute-start | bytes 3932168 | tf_op jit(solution)/shard_map/ppermute | solution.py:694
  79.2 27.0 %collective-permute-start.16 = (bf16[8,2,16,1536]{3,2,1,0:T(8,128)(2,1)}, bf16[8,2,16,1536]{3,2,1,0:T(8,128)(2,1)}, u32[]{:S(2)}, u32[]{:S(2)}) collective-permute-start(bf16[8,2,16,1536]{3,2,1,0:T(8,128)(2,1)} %get-tuple-element.54), channel_id=1, source_target_pairs={{0,2},{2,0},{4,6},{6,4},{8,10},{10,8},{12,14},{14,12},{16,18},{18,... | collective-permute-start | bytes 2359304 | tf_op jit(solution)/shard_map/ppermute | solution.py:697
  79.4 28.9 %collective-permute-start.15 = (bf16[2,256,1024]{2,1,0:T(8,128)(2,1)}, bf16[2,256,1024]{2,1,0:T(8,128)(2,1)}, u32[]{:S(2)}, u32[]{:S(2)}) collective-permute-start(bf16[2,256,1024]{2,1,0:T(8,128)(2,1)} %get-tuple-element.52), channel_id=1, source_target_pairs={{1,0},{3,2},{5,4},{7,6},{9,8},{11,10},{13,12},{15,14},{17,16},{19,... | collective-permute-start | bytes 3145736 | tf_op jit(solution)/shard_map/ppermute | solution.py:748
  82.5 28.6 %collective-permute-start.7 = (bf16[2,256,1024]{2,1,0:T(8,128)(2,1)}, bf16[2,256,1024]{2,1,0:T(8,128)(2,1)}, u32[]{:S(2)}, u32[]{:S(2)}) collective-permute-start(bf16[2,256,1024]{2,1,0:T(8,128)(2,1)} %maximum_add_fusion.2), channel_id=1, source_target_pairs={{0,1},{2,3},{4,5},{6,7},{8,9},{10,11},{12,13},{14,15},{16,17},{18,... | collective-permute-start | bytes 3145736 | tf_op jit(solution)/shard_map/ppermute | solution.py:677
  89.1 1.1 copy-start.11
  90.2 16.0 %copy-start.7 = (bf16[8,2,16,1536]{3,2,1,0:T(8,128)(2,1)S(1)}, bf16[8,2,16,1536]{3,2,1,0:T(8,128)(2,1)}, u32[]{:S(2)}) copy-start(bf16[8,2,16,1536]{3,2,1,0:T(8,128)(2,1)} %get-tuple-element.53) | copy-start | bytes 2359300
  104.9 39.4 %collective-permute-start.23 = (bf16[2,256,1536]{2,1,0:T(8,128)(2,1)}, bf16[2,256,1536]{2,1,0:T(8,128)(2,1)S(1)}, u32[]{:S(2)}, u32[]{:S(2)}) collective-permute-start(bf16[2,256,1536]{2,1,0:T(8,128)(2,1)} %get-tuple-element.63), channel_id=1, source_target_pairs={{1,0},{3,2},{5,4},{7,6},{9,8},{11,10},{13,12},{15,14},{17,16},{19,... | collective-permute-start | bytes 4718600 | tf_op jit(solution)/shard_map/ppermute | solution.py:748
  107.6 3.5 %copy-start.1 = (bf16[8,2,16,1536]{3,2,1,0:T(8,128)(2,1)}, bf16[8,2,16,1536]{3,2,1,0:T(8,128)(2,1)S(1)}, u32[]{:S(2)}) copy-start(bf16[8,2,16,1536]{3,2,1,0:T(8,128)(2,1)S(1)} %fusion.1.rest_6_) | copy-start | bytes 2359300
  107.7 15.9 %collective-permute-start.17 = (bf16[4,2,16,1536]{3,2,1,0:T(8,128)(2,1)S(1)}, bf16[4,2,16,1536]{3,2,1,0:T(8,128)(2,1)}, u32[]{:S(2)}, u32[]{:S(2)}) collective-permute-start(bf16[4,2,16,1536]{3,2,1,0:T(8,128)(2,1)S(1)} %slice.142), channel_id=1, source_target_pairs={{0,4},{2,6},{4,0},{6,2},{8,12},{10,14},{12,8},{14,10},{16,20},{18,... | collective-permute-start | bytes 1179656 | tf_op jit(solution)/shard_map/ppermute | solution.py:700
  108.2 18.0 %collective-permute-start.20 = (bf16[8,2,16,1536]{3,2,1,0:T(8,128)(2,1)}, bf16[8,2,16,1536]{3,2,1,0:T(8,128)(2,1)}, u32[]{:S(2)}, u32[]{:S(2)}) collective-permute-start(bf16[8,2,16,1536]{3,2,1,0:T(8,128)(2,1)} %get-tuple-element.59), channel_id=1, source_target_pairs={{0,2},{2,0},{4,6},{6,4},{8,10},{10,8},{12,14},{14,12},{16,18},{18,... | collective-permute-start | bytes 2359304 | tf_op jit(solution)/shard_map/ppermute | solution.py:697
  121.3 5.0 %copy-start.6 = (bf16[8,2,16,1536]{3,2,1,0:T(8,128)(2,1)S(1)}, bf16[8,2,16,1536]{3,2,1,0:T(8,128)(2,1)}, u32[]{:S(2)}) copy-start(bf16[8,2,16,1536]{3,2,1,0:T(8,128)(2,1)} %get-tuple-element.58) | copy-start | bytes 2359300
  121.3 44.3 %collective-permute-start.28 = (bf16[2,256,1024]{2,1,0:T(8,128)(2,1)}, bf16[2,256,1024]{2,1,0:T(8,128)(2,1)S(1)}, u32[]{:S(2)}, u32[]{:S(2)}) collective-permute-start(bf16[2,256,1024]{2,1,0:T(8,128)(2,1)} %get-tuple-element.66), channel_id=1, source_target_pairs={{1,0},{3,2},{5,4},{7,6},{9,8},{11,10},{13,12},{15,14},{17,16},{19,... | collective-permute-start | bytes 3145736 | tf_op jit(solution)/shard_map/ppermute | solution.py:748
  123.5 21.9 %collective-permute-start.22 = (bf16[8,2,16,1024]{3,2,1,0:T(8,128)(2,1)}, bf16[8,2,16,1024]{3,2,1,0:T(8,128)(2,1)S(1)}, u32[]{:S(2)}, u32[]{:S(2)}) collective-permute-start(bf16[8,2,16,1024]{3,2,1,0:T(8,128)(2,1)} %get-tuple-element.62), channel_id=1, source_target_pairs={{0,2},{2,0},{4,6},{6,4},{8,10},{10,8},{12,14},{14,12},{16,18},{18,... | collective-permute-start | bytes 1572872 | tf_op jit(solution)/shard_map/ppermute | solution.py:697
  124.8 13.4 %collective-permute-start.18 = (bf16[2,2,16,1536]{3,2,1,0:T(8,128)(2,1)S(1)}, bf16[2,2,16,1536]{3,2,1,0:T(8,128)(2,1)S(1)}, u32[]{:S(2)}, u32[]{:S(2)}) collective-permute-start(bf16[2,2,16,1536]{3,2,1,0:T(8,128)(2,1)S(1)} %slice.144), channel_id=1, source_target_pairs={{16,0},{18,2},{20,4},{22,6},{24,8},{26,10},{28,12},{30,14},{17,1},... | collective-permute-start | bytes 589832 | tf_op jit(solution)/shard_map/ppermute | solution.py:711
  126.3 19.2 %copy-start.9 = (bf16[8,2,16,1024]{3,2,1,0:T(8,128)(2,1)S(1)}, bf16[8,2,16,1024]{3,2,1,0:T(8,128)(2,1)}, u32[]{:S(2)}) copy-start(bf16[8,2,16,1024]{3,2,1,0:T(8,128)(2,1)} %get-tuple-element.61) | copy-start | bytes 1572868
  127.8 18.5 %collective-permute-start.21 = (bf16[4,2,16,1536]{3,2,1,0:T(8,128)(2,1)S(1)}, bf16[4,2,16,1536]{3,2,1,0:T(8,128)(2,1)S(1)}, u32[]{:S(2)}, u32[]{:S(2)}) collective-permute-start(bf16[4,2,16,1536]{3,2,1,0:T(8,128)(2,1)S(1)} %slice.148), channel_id=1, source_target_pairs={{0,4},{2,6},{4,0},{6,2},{8,12},{10,14},{12,8},{14,10},{16,20},{18,... | collective-permute-start | bytes 1179656 | tf_op jit(solution)/shard_map/ppermute | solution.py:700
  138.2 21.5 %collective-permute-start.19 = (bf16[1,2,16,1536]{3,2,1,0:T(8,128)(2,1)S(1)}, bf16[1,2,16,1536]{3,2,1,0:T(8,128)(2,1)}, u32[]{:S(2)}, u32[]{:S(2)}) collective-permute-start(bf16[1,2,16,1536]{3,2,1,0:T(8,128)(2,1)S(1)} %slice.146), channel_id=1, source_target_pairs={{8,0},{10,2},{12,4},{14,6},{16,8},{18,10},{20,12},{22,14},{24,16},... | collective-permute-start | bytes 294920 | tf_op jit(solution)/shard_map/ppermute | solution.py:711
  144.3 2.2 %copy-start.2 = (bf16[2,256,1536]{2,1,0:T(8,128)(2,1)}, bf16[2,256,1536]{2,1,0:T(8,128)(2,1)S(1)}, u32[]{:S(2)}) copy-start(bf16[2,256,1536]{2,1,0:T(8,128)(2,1)S(1)} %collective-permute-done.23.refs_2_) | copy-start | bytes 4718596
  145.7 8.9 %collective-permute-start.24 = (bf16[4,2,16,1024]{3,2,1,0:T(8,128)(2,1)S(1)}, bf16[4,2,16,1024]{3,2,1,0:T(8,128)(2,1)}, u32[]{:S(2)}, u32[]{:S(2)}) collective-permute-start(bf16[4,2,16,1024]{3,2,1,0:T(8,128)(2,1)S(1)} %slice.151), channel_id=1, source_target_pairs={{0,4},{2,6},{4,0},{6,2},{8,12},{10,14},{12,8},{14,10},{16,20},{18,... | collective-permute-start | bytes 786440 | tf_op jit(solution)/shard_map/ppermute | solution.py:700
  155.8 18.4 %copy-start.10 = (s32[1,16]{1,0:T(1,128)S(1)}, s32[1,16]{1,0:T(1,128)}, u32[]{:S(2)}) copy-start(s32[1,16]{1,0:T(1,128)} %rows_ref.1) | copy-start | bytes 196
  155.8 11.0 %collective-permute-start.25 = (bf16[2,16,2560]{2,1,0:T(8,128)(2,1)S(1)}, bf16[2,16,2560]{2,1,0:T(8,128)(2,1)S(1)}, u32[]{:S(2)}, u32[]{:S(2)}) collective-permute-start(bf16[2,16,2560]{2,1,0:T(8,128)(2,1)S(1)} %get-tuple-element.78), channel_id=1, source_target_pairs={{8,0},{10,2},{12,4},{14,6},{16,8},{18,10},{20,12},{22,14},{24,16},... | collective-permute-start | bytes 491528 | tf_op jit(solution)/shard_map/ppermute | solution.py:705
  157.1 15.3 %collective-permute-start.26 = (bf16[2,16,2560]{2,1,0:T(8,128)(2,1)S(1)}, bf16[2,16,2560]{2,1,0:T(8,128)(2,1)S(1)}, u32[]{:S(2)}, u32[]{:S(2)}) collective-permute-start(bf16[2,16,2560]{2,1,0:T(8,128)(2,1)S(1)} %get-tuple-element.80), channel_id=1, source_target_pairs={{16,0},{18,2},{20,4},{22,6},{24,8},{26,10},{28,12},{30,14},{17,1},... | collective-permute-start | bytes 491528 | tf_op jit(solution)/shard_map/ppermute | solution.py:705
  158.4 14.0 %collective-permute-start.27 = (bf16[2,16,2560]{2,1,0:T(8,128)(2,1)S(1)}, bf16[2,16,2560]{2,1,0:T(8,128)(2,1)S(1)}, u32[]{:S(2)}, u32[]{:S(2)}) collective-permute-start(bf16[2,16,2560]{2,1,0:T(8,128)(2,1)S(1)} %get-tuple-element.79), channel_id=1, source_target_pairs={{24,0},{26,2},{28,4},{30,6},{25,1},{27,3},{29,5},{31,7}} | collective-permute-start | bytes 491528 | tf_op jit(solution)/shard_map/ppermute | solution.py:705
  165.6 9.2 %copy-start.5 = (bf16[2,256,1024]{2,1,0:T(8,128)(2,1)}, bf16[2,256,1024]{2,1,0:T(8,128)(2,1)S(1)}, u32[]{:S(2)}) copy-start(bf16[2,256,1024]{2,1,0:T(8,128)(2,1)S(1)} %collective-permute-done.28.refs_0_) | copy-start | bytes 3145732
  172.6 5.0 %collective-permute-start.29 = (bf16[2,8,4096]{2,1,0:T(8,128)(2,1)S(1)}, bf16[2,8,4096]{2,1,0:T(8,128)(2,1)S(1)}, u32[]{:S(2)}, u32[]{:S(2)}) collective-permute-start(bf16[2,8,4096]{2,1,0:T(8,128)(2,1)S(1)} %pad_maximum_fusion.3), channel_id=1, source_target_pairs={{0,1},{1,0},{2,3},{3,2},{4,5},{5,4},{6,7},{7,6},{8,9},{9,8},{10,11... | collective-permute-start | bytes 393224 | tf_op jit(solution)/shard_map/ppermute | solution.py:716

commit v4 on v3

--- a/solution.py
+++ b/solution.py
@@ -440,6 +440,7 @@
     round_col,
     round_done,
     after,
+    effort,
 ):
     rows_here, total_width = full[0].shape
     tile = math.gcd(width, 2 * HD)
@@ -487,7 +488,7 @@
         input_output_aliases=aliases,
         compiler_params=pltpu.CompilerParams(vmem_limit_bytes=VMEM_GRANT),
         cost_estimate=pl.CostEstimate(
-            flops=56 * heads * keys * rows_here * HD,
+            flops=effort * heads * keys * rows_here * HD,
             bytes_accessed=heads * 16 * 2 * rows_here * HD,
             transcendentals=heads * keys * rows_here,
         ),
@@ -598,32 +599,50 @@
     )(rows, summ, key_grad, val_grad)
 
 
-def pick_step(place_ref, rows_ref, key_ref, val_ref, out_ref):
-    few, rows_here = out_ref.shape[1], key_ref.shape[0]
+def pick_step(place_ref, rows_ref, key_ref, val_ref, out_ref, tiles, sems):
+    _, few, tile, _ = tiles.shape
+    rows_here = key_ref.shape[0]
     half = place_ref[0]
-    row = lax.broadcasted_iota(jnp.int32, (few, rows_here), 0)
-    wanted = jnp.full((few, rows_here), -1, jnp.int32)
-    for i in range(few):
-        wanted = jnp.where(row == i, rows_ref[0, half * few + i] - half * rows_here, wanted)
-    hit = lax.broadcasted_iota(jnp.int32, (few, rows_here), 1) == wanted
-    picker = jnp.where(hit, 1.0, 0.0).astype(jnp.bfloat16)
-    for kind, ref in enumerate((key_ref, val_ref)):
-        rows = jnp.dot(picker, ref[...], preferred_element_type=jnp.float32)
+
+    def here(step):
+        return rows_ref[0, half * few + step] - half * rows_here
+
+    def copies():
+        for kind, ref in enumerate((key_ref, val_ref)):
+            for step in range(few):
+                first = pl.multiple_of(here(step) // tile * tile, tile)
+                yield pltpu.make_async_copy(
+                    ref.at[pl.ds(first, tile), :], tiles.at[kind, step], sems.at[kind, step]
+                )
+
+    for copy in copies():
+        copy.start()
+    for copy in copies():
+        copy.wait()
+    row = lax.broadcasted_iota(jnp.int32, (few, tile), 0)
+    lane = lax.broadcasted_iota(jnp.int32, (few, tile), 1)
+    for kind in range(2):
+        rows = jnp.zeros(out_ref.shape[1:], jnp.float32)
+        for step in range(few):
+            hit = (row == step) & (lane == lax.rem(here(step), tile))
+            picker = jnp.where(hit, 1.0, 0.0).astype(jnp.bfloat16)
+            rows = rows + jnp.dot(picker, tiles[kind, step], preferred_element_type=jnp.float32)
         out_ref[kind] = rows.astype(jnp.bfloat16)
 
 
 def pick_call(half, summary_rows, key_vectors, value_vectors):
-    rows_here, total_width = key_vectors.shape
+    total_width = key_vectors.shape[1]
     few = summary_rows.shape[1] // 2
-    tile = math.gcd(total_width, 8 * HD)
-    wide_spec = pl.BlockSpec((rows_here, tile), lambda i: (0, i))
+    any_spec = pl.BlockSpec(memory_space=pl.ANY)
     smem = pl.BlockSpec(memory_space=pltpu.SMEM)
     return pl.pallas_call(
         pick_step,
-        grid=(total_width // tile,),
-        in_specs=[smem, smem, wide_spec, wide_spec],
-        out_specs=pl.BlockSpec((2, few, tile), lambda i: (0, 0, i)),
+        in_specs=[smem, smem, any_spec, any_spec],
         out_shape=jax.ShapeDtypeStruct((2, few, total_width), jnp.bfloat16),
+        scratch_shapes=[
+            pltpu.VMEM((2, few, 16, total_width), jnp.bfloat16),
+            pltpu.SemaphoreType.DMA((2, few)),
+        ],
         compiler_params=pltpu.CompilerParams(vmem_limit_bytes=VMEM_GRANT),
     )(half[None], summary_rows, key_vectors, value_vectors)
 
@@ -726,7 +745,7 @@
     wide_done = ()
     backs = []
 
-    def attend(chunk, source, reduce_first, reduce_last, round_done, after):
+    def attend(chunk, source, reduce_first, reduce_last, round_done, after, effort=56):
         nonlocal wide_done
         low = max(start for start in lower_starts if start <= chunk)
         out = attention_call(
@@ -743,6 +762,7 @@
             (edges[chunk] - edges[reduce_first]) * unit,
             round_done,
             after,
+            effort,
         )
         wide_done = tuple(out[:3])
         backs.append(lax.ppermute(out[3], "head", [(1, 0)]))
@@ -759,15 +779,15 @@
     gathered.append(with_other_core(jnp.concatenate([ladder, side], axis=0)))
     ladder = climb_stages(2, 4, first_ladder)
     done = attend(0, 0, 0, 2, (), ())
-    lower_pair(3, 4, marks[0])
     ladder = wait_for(ladder, marks[0])
     side = lax.ppermute(ladder, "seq", flip_side)
     done = attend(1, 0, 0, 2, done, ())
     near = wait_for(jnp.concatenate([ladder, side], axis=0), marks[1])
     near = wait_for_moved(near, backs[0])
     gathered.append(with_other_core(near))
+    lower_pair(3, 4, jnp.minimum(jnp.abs(near[0, 0]), 0))
     chip_a = reduce_chip(*done)
-    done = attend(2, 1, 2, 3, (), ())
+    done = attend(2, 1, 2, 3, (), (), 16)
     chip_a = wait_for(chip_a, marks[2])
     plane_a = reduce_plane(chip_a)
     chip_b = reduce_chip(*done)

time: 184 us -> 183 us (level)
  no operation moved by 1% of the time
where the time goes in v4:
time: 183 us; the launch traced here: 182 us
  Pallas kernels  59.6 us (33%)
  starting transfers between devices  51.8 us (28%)
  waiting for transfers between devices  37.3 us (20%)
  other arithmetic  14.9 us (8%)
  local copies, waits for them, and re-layouts  13.4 us (7%)
  between operations  4.65 us (3%)
    pallas_call x4, Pallas kernels, attention_call(): pl.pallas_call(functools.partial(attention_step, len(summaries)), grid=(w...  40.5 us
    ppermute x6, starting transfers between devices, climb_stages(): lax.ppermute(ladder, 'seq', climb(i))  19 us
    ppermute x4, waiting for transfers between devices, attend(): backs.append(lax.ppermute(out[3], 'head', [(1, 0)]))  13.7 us
    ppermute x3, starting transfers between devices, lower_pair(): lowers.append(lax.ppermute(pair, 'head', [(0, 1)]))  11.1 us
    ppermute x2, waiting for transfers between devices, reduce_group_halving(): lax.ppermute(plane[size:], 'seq', descend(size))  10.3 us
    pallas_call x2, Pallas kernels, merge_call(): pl.pallas_call(functools.partial(merge_step, bounds), grid=(bounds[-1],),...  8.82 us
    ppermute x3, waiting for transfers between devices, reduce_group(): lax.ppermute(plane[i], 'seq', descend(i))  5.63 us
    ppermute x4, starting transfers between devices, attend(): backs.append(lax.ppermute(out[3], 'head', [(1, 0)]))  5.44 us
  transfers between devices with their start and end apart: 30, of which 8 were waited for; matrix products, arithmetic and copies ran while one was open for 14% of the time, Pallas kernels for 28%

profile of v4, /device:TPU:0, one launch (start us, length us, event | category | flops | bytes accessed | tf_op | source)
XLA Modules:
  0.0 181.7 jit_solution(4176993037293797503)
XLA Ops:
  0.6 3.9 %shard_map.94 = bf16[2,8,4096]{2,1,0:T(8,128)(2,1)} custom-call(s32[1]{0:T(128)} %bitcast.place_ref, s32[1,16]{1,0:T(1,128)} %rows_ref.1, bf16[256,4096]{1,0:T(8,128)(2,1)} %key_ref.9, bf16[256,4096]{1,0:T(8,128)(2,1)} %val_ref.9), custom_call_target="tpu_custom_call" | custom-call | tf_op jit(solution)/shard_map/pallas_call | solution.py:638
  4.5 3.0 %collective-permute-start = (bf16[2,8,4096]{2,1,0:T(8,128)(2,1)}, bf16[2,8,4096]{2,1,0:T(8,128)(2,1)S(1)}, u32[]{:S(2)}, u32[]{:S(2)}) collective-permute-start(bf16[2,8,4096]{2,1,0:T(8,128)(2,1)} %shard_map.94), channel_id=1, source_target_pairs={{0,1},{1,0},{2,3},{3,2},{4,5},{5,4},{6,7},{7,6},{8,9},{9,8},{10,11... | collective-permute-start | bytes 393224 | tf_op jit(solution)/shard_map/ppermute | solution.py:689
  7.6 1.6 slice_bitcast_fusion
  9.2 1.3 pad_maximum_fusion
  10.5 3.1 %collective-permute-start.5 = (bf16[2,256,1536]{2,1,0:T(8,128)(2,1)}, bf16[2,256,1536]{2,1,0:T(8,128)(2,1)}, u32[]{:S(2)}, u32[]{:S(2)}) collective-permute-start(bf16[2,256,1536]{2,1,0:T(8,128)(2,1)} %pad_maximum_fusion), channel_id=1, source_target_pairs={{0,1},{2,3},{4,5},{6,7},{8,9},{10,11},{12,13},{14,15},{16,17},{18,... | collective-permute-start | bytes 4718600 | tf_op jit(solution)/shard_map/ppermute | solution.py:696
  14.4 4.0 %collective-permute-start.1 = (bf16[1,2,16,1536]{3,2,1,0:T(8,128)(2,1)S(1)}, bf16[1,2,16,1536]{3,2,1,0:T(8,128)(2,1)S(1)}, u32[]{:S(2)}, u32[]{:S(2)}) collective-permute-start(bf16[1,2,16,1536]{3,2,1,0:T(8,128)(2,1)S(1)} %get-tuple-element.73), channel_id=1, source_target_pairs={{0,8},{2,10},{4,12},{6,14},{8,16},{10,18},{12,20},{14,22},{16,24},... | collective-permute-start | bytes 294920 | tf_op jit(solution)/shard_map/ppermute | solution.py:709
  18.3 4.5 %collective-permute-start.6 = (bf16[1,2,16,1536]{3,2,1,0:T(8,128)(2,1)S(1)}, bf16[1,2,16,1536]{3,2,1,0:T(8,128)(2,1)S(1)}, u32[]{:S(2)}, u32[]{:S(2)}) collective-permute-start(bf16[1,2,16,1536]{3,2,1,0:T(8,128)(2,1)S(1)} %get-tuple-element.73), channel_id=1, source_target_pairs={{0,16},{2,18},{4,20},{6,22},{8,24},{10,26},{12,28},{14,30},{1,17},... | collective-permute-start | bytes 294920 | tf_op jit(solution)/shard_map/ppermute | solution.py:709
  22.9 1.3 collective-permute-start.7
  24.8 1.7 shard_map.93.caps_ref
  26.6 1.6 collective-permute-start.8
  31.3 5.1 %collective-permute-done.8 = bf16[4,2,16,1536]{3,2,1,0:T(8,128)(2,1)S(1)} collective-permute-done((bf16[4,2,16,1536]{3,2,1,0:T(8,128)(2,1)S(1)}, bf16[4,2,16,1536]{3,2,1,0:T(8,128)(2,1)S(1)}, u32[]{:S(2)}, u32[]{:S(2)}) %collective-permute-start.8) | collective-permute-done | bytes 393248 | tf_op jit(solution)/shard_map/ppermute | solution.py:777
  37.3 1.9 %collective-permute-start.2 = (bf16[1,2,16,2560]{3,2,1,0:T(8,128)(2,1)S(1)}, bf16[1,2,16,2560]{3,2,1,0:T(8,128)(2,1)S(1)}, u32[]{:S(2)}, u32[]{:S(2)}) collective-permute-start(bf16[1,2,16,2560]{3,2,1,0:T(8,128)(2,1)S(1)} %fusion.9), channel_id=1, source_target_pairs={{0,8},{2,10},{4,12},{6,14},{8,16},{10,18},{12,20},{14,22},{16,24},... | collective-permute-start | bytes 491528 | tf_op jit(solution)/shard_map/ppermute | solution.py:709
  39.2 6.0 %collective-permute-start.3 = (bf16[1,2,16,2560]{3,2,1,0:T(8,128)(2,1)S(1)}, bf16[1,2,16,2560]{3,2,1,0:T(8,128)(2,1)S(1)}, u32[]{:S(2)}, u32[]{:S(2)}) collective-permute-start(bf16[1,2,16,2560]{3,2,1,0:T(8,128)(2,1)S(1)} %fusion.9), channel_id=1, source_target_pairs={{0,16},{2,18},{4,20},{6,22},{8,24},{10,26},{12,28},{14,30},{1,17},... | collective-permute-start | bytes 491528 | tf_op jit(solution)/shard_map/ppermute | solution.py:709
  45.2 1.3 collective-permute-start.4
  46.5 1.3 maximum_add_fusion
  47.8 1.4 collective-permute-start.14
  49.2 6.4 %shard_map.95 = (bf16[256,4096]{1,0:T(8,128)(2,1)}, bf16[256,4096]{1,0:T(8,128)(2,1)}, bf16[2,256,4096]{2,1,0:T(8,128)(2,1)}, bf16[2,256,512]{2,1,0:T(8,128)(2,1...) custom-call(f32[768,256]{1,0:T(8,128)} %shard_map.93.caps_ref, ...), custom_call_target="tpu_custom_call" | custom-call | flops 5637144576 | bytes 4194304 | tf_op jit(solution)/shard_map/pallas_call | solution.py:470
  56.6 1.6 collective-permute-start.10
  58.2 1.3 collective-permute-start.11
  59.5 10.1 %shard_map.96 = (bf16[256,4096]{1,0:T(8,128)(2,1)}, bf16[256,4096]{1,0:T(8,128)(2,1)}, bf16[2,256,4096]{2,1,0:T(8,128)(2,1)}, bf16[2,256,1024]{2,1,0:T(8,128)(2,...) custom-call(f32[768,256]{1,0:T(8,128)} %shard_map.93.caps_ref, ...), custom_call_target="tpu_custom_call", output_to_operand_aliasing={{0}: (8, {}), {1}: (9, {}), {2}: (10, {}), {4}: (11, {}), {... | custom-call | flops 11274289152 | bytes 8388608 | tf_op jit(solution)/shard_map/pallas_call | solution.py:470
  69.6 4.2 %collective-permute-done.11.refs_0_ = bf16[2,256,512]{2,1,0:T(8,128)(2,1)S(1)} collective-permute-done((bf16[2,256,512]{2,1,0:T(8,128)(2,1)}, bf16[2,256,512]{2,1,0:T(8,128)(2,1)S(1)}, u32[]{:S(2)}, u32[]{:S(2)}) %collective-permute-start.11) | collective-permute-done | bytes 524320 | tf_op jit(solution)/shard_map/ppermute | solution.py:768
  75.0 1.2 fusion.rest_0_
  76.3 1.7 slice_bitcast_fusion.4
  78.2 1.3 collective-permute-start.15
  80.6 6.6 %collective-permute-start.12 = (bf16[2,256,1024]{2,1,0:T(8,128)(2,1)}, bf16[2,256,1024]{2,1,0:T(8,128)(2,1)}, u32[]{:S(2)}, u32[]{:S(2)}) collective-permute-start(bf16[2,256,1024]{2,1,0:T(8,128)(2,1)} %maximum_add_fusion.2), channel_id=1, source_target_pairs={{0,1},{2,3},{4,5},{6,7},{8,9},{10,11},{12,13},{14,15},{16,17},{18,... | collective-permute-start | bytes 3145736 | tf_op jit(solution)/shard_map/ppermute | solution.py:696
  87.1 1.1 copy-done.5
  88.7 13.9 %shard_map.97 = (bf16[256,4096]{1,0:T(8,128)(2,1)}, bf16[256,4096]{1,0:T(8,128)(2,1)}, bf16[2,256,4096]{2,1,0:T(8,128)(2,1)}, bf16[2,256,1536]{2,1,0:T(8,128)(2,...) custom-call(f32[768,256]{1,0:T(8,128)} %shard_map.93.caps_ref, ...), custom_call_target="tpu_custom_call", output_to_operand_aliasing={{0}: (8, {}), {1}: (9, {}), {2}: (10, {})} | custom-call | flops 4831838208 | bytes 12582912 | tf_op jit(solution)/shard_map/pallas_call | solution.py:470
  103.4 1.3 collective-permute-start.23
  104.7 1.6 fusion.1.rest_6_
  107.0 2.2 %collective-permute-done.12.lower_ref = bf16[2,256,1024]{2,1,0:T(8,128)(2,1)} collective-permute-done((bf16[2,256,1024]{2,1,0:T(8,128)(2,1)}, bf16[2,256,1024]{2,1,0:T(8,128)(2,1)}, u32[]{:S(2)}, u32[]{:S(2)}) %collective-permute-start.12) | collective-permute-done | bytes 1048608 | tf_op jit(solution)/shard_map/ppermute | solution.py:696
  109.2 10.1 %shard_map.98 = (bf16[256,4096]{1,0:T(8,128)(2,1)}, bf16[256,4096]{1,0:T(8,128)(2,1)}, bf16[2,256,4096]{2,1,0:T(8,128)(2,1)}, bf16[2,256,1024]{2,1,0:T(8,128)(2,...) custom-call(f32[768,256]{1,0:T(8,128)} %shard_map.93.caps_ref, ...), custom_call_target="tpu_custom_call", output_to_operand_aliasing={{0}: (8, {}), {1}: (9, {}), {2}: (10, {})} | custom-call | flops 11274289152 | bytes 8388608 | tf_op jit(solution)/shard_map/pallas_call | solution.py:470
  119.3 1.6 collective-permute-start.28
  121.8 1.2 add_convert_fusion.4
  123.0 1.3 collective-permute-start.18
  124.3 1.5 fusion.2
  126.4 10.3 %collective-permute-done.18 = bf16[2,2,16,1536]{3,2,1,0:T(8,128)(2,1)S(1)} collective-permute-done((bf16[2,2,16,1536]{3,2,1,0:T(8,128)(2,1)S(1)}, bf16[2,2,16,1536]{3,2,1,0:T(8,128)(2,1)S(1)}, u32[]{:S(2)}, u32[]{:S(2)}) %collective-permute-start.18) | collective-permute-done | bytes 196640 | tf_op jit(solution)/shard_map/ppermute | solution.py:730
  136.8 1.3 collective-permute-start.19
  138.1 4.6 %collective-permute-done.23.refs_2_ = bf16[2,256,1536]{2,1,0:T(8,128)(2,1)S(1)} collective-permute-done((bf16[2,256,1536]{2,1,0:T(8,128)(2,1)}, bf16[2,256,1536]{2,1,0:T(8,128)(2,1)S(1)}, u32[]{:S(2)}, u32[]{:S(2)}) %collective-permute-start.23) | collective-permute-done | bytes 1572896 | tf_op jit(solution)/shard_map/ppermute | solution.py:768
  144.9 6.4 %shard_map.99 = (bf16[256,4096]{1,0:T(8,128)(2,1)}, bf16[256,4096]{1,0:T(8,128)(2,1)}) custom-call(bf16[2,256,4096]{2,1,0:T(8,128)(2,1)} %get-tuple-element.64.local_ref, bf16[2,256,512]{2,1,0:T(8,128)(2,1)} %copy-done.9, bf16[2,256,1024]{2,1,0:T(8,128)(2,1)} %collective-permute-done.15.rest_5_.refs_1_, bf16[2,256,1536]{2,1,0:T(8,128)(2,1)} %copy-done.3), custom_call_target="tpu_custom_call" | custom-call | flops 1572864 | bytes 9437184 | tf_op jit(solution)/shard_map/pallas_call | solution.py:524
  151.3 1.2 slice.160
  154.4 1.3 collective-permute-start.25
  155.7 1.3 collective-permute-start.26
  157.0 1.3 collective-permute-start.27
  159.2 4.9 %collective-permute-done.28.refs_0_ = bf16[2,256,1024]{2,1,0:T(8,128)(2,1)S(1)} collective-permute-done((bf16[2,256,1024]{2,1,0:T(8,128)(2,1)}, bf16[2,256,1024]{2,1,0:T(8,128)(2,1)S(1)}, u32[]{:S(2)}, u32[]{:S(2)}) %collective-permute-start.28) | collective-permute-done | bytes 1048608 | tf_op jit(solution)/shard_map/ppermute | solution.py:768
  165.4 5.6 %collective-permute-done.26 = bf16[2,16,2560]{2,1,0:T(8,128)(2,1)S(1)} collective-permute-done((bf16[2,16,2560]{2,1,0:T(8,128)(2,1)S(1)}, bf16[2,16,2560]{2,1,0:T(8,128)(2,1)S(1)}, u32[]{:S(2)}, u32[]{:S(2)}) %collective-permute-start.26) | collective-permute-done | bytes 163872 | tf_op jit(solution)/shard_map/ppermute | solution.py:724
  171.1 1.7 collective-permute-start.29
  173.4 2.4 %shard_map.100 = (bf16[256,4096]{1,0:T(8,128)(2,1)}, bf16[256,4096]{1,0:T(8,128)(2,1)}) custom-call(bf16[2,256,4096]{2,1,0:T(8,128)(2,1)} %get-tuple-element.64.local_ref, bf16[2,256,1024]{2,1,0:T(8,128)(2,1)} %copy-done.7, bf16[256,4096]{1,0:T(8,128)(2,1)} %get-tuple-element.65.refs_1_, ...), custom_call_target="tpu_custom_call", output_to_operand_aliasing={{0}: (2, {}), {1}: (3, {})} | custom-call | flops 524288 | bytes 3145728 | tf_op jit(solution)/shard_map/pallas_call | solution.py:524
  176.8 4.6 %shard_map.101 = (bf16[256,4096]{1,0:T(8,128)(2,1)}, bf16[256,4096]{1,0:T(8,128)(2,1)}) custom-call(s32[8]{0:T(128)} %subtract_bitcast_fusion.rows_ref, bf16[2,8,4096]{2,1,0:T(8,128)(2,1)} %add_convert_fusion.7.summ_ref, bf16[256,4096]{1,0:T(8,128)(2,1)} %get-tuple-element.68.key_ref, ...), custom_call_target="tpu_custom_call", output_to_operand_aliasing={{0}: (2, {}), {1}: (3, {})} | custom-call | flops 16777216 | bytes 4194304 | tf_op jit(solution)/shard_map/pallas_call | solution.py:578
  (98 shorter events, 17.0 us)
Async XLA Ops:
  0.6 6.9 %copy-start = (bf16[256,4096]{1,0:T(8,128)(2,1)S(1)}, bf16[256,4096]{1,0:T(8,128)(2,1)}, u32[]{:S(2)}) copy-start(bf16[256,4096]{1,0:T(8,128)(2,1)} %key_ref.9) | copy-start | bytes 6291460
  4.5 9.2 %collective-permute-start = (bf16[2,8,4096]{2,1,0:T(8,128)(2,1)}, bf16[2,8,4096]{2,1,0:T(8,128)(2,1)S(1)}, u32[]{:S(2)}, u32[]{:S(2)}) collective-permute-start(bf16[2,8,4096]{2,1,0:T(8,128)(2,1)} %shard_map.94), channel_id=1, source_target_pairs={{0,1},{1,0},{2,3},{3,2},{4,5},{5,4},{6,7},{7,6},{8,9},{9,8},{10,11... | collective-permute-start | bytes 393224 | tf_op jit(solution)/shard_map/ppermute | solution.py:689
  9.2 4.5 %copy-start.6 = (bf16[2,8,4096]{2,1,0:T(8,128)(2,1)S(1)}, bf16[2,8,4096]{2,1,0:T(8,128)(2,1)}, u32[]{:S(2)}) copy-start(bf16[2,8,4096]{2,1,0:T(8,128)(2,1)} %shard_map.94) | copy-start | bytes 393220
  10.5 38.7 %collective-permute-start.5 = (bf16[2,256,1536]{2,1,0:T(8,128)(2,1)}, bf16[2,256,1536]{2,1,0:T(8,128)(2,1)}, u32[]{:S(2)}, u32[]{:S(2)}) collective-permute-start(bf16[2,256,1536]{2,1,0:T(8,128)(2,1)} %pad_maximum_fusion), channel_id=1, source_target_pairs={{0,1},{2,3},{4,5},{6,7},{8,9},{10,11},{12,13},{14,15},{16,17},{18,... | collective-permute-start | bytes 4718600 | tf_op jit(solution)/shard_map/ppermute | solution.py:696
  14.4 12.2 %collective-permute-start.1 = (bf16[1,2,16,1536]{3,2,1,0:T(8,128)(2,1)S(1)}, bf16[1,2,16,1536]{3,2,1,0:T(8,128)(2,1)S(1)}, u32[]{:S(2)}, u32[]{:S(2)}) collective-permute-start(bf16[1,2,16,1536]{3,2,1,0:T(8,128)(2,1)S(1)} %get-tuple-element.73), channel_id=1, source_target_pairs={{0,8},{2,10},{4,12},{6,14},{8,16},{10,18},{12,20},{14,22},{16,24},... | collective-permute-start | bytes 294920 | tf_op jit(solution)/shard_map/ppermute | solution.py:709
  18.3 8.2 %collective-permute-start.6 = (bf16[1,2,16,1536]{3,2,1,0:T(8,128)(2,1)S(1)}, bf16[1,2,16,1536]{3,2,1,0:T(8,128)(2,1)S(1)}, u32[]{:S(2)}, u32[]{:S(2)}) collective-permute-start(bf16[1,2,16,1536]{3,2,1,0:T(8,128)(2,1)S(1)} %get-tuple-element.73), channel_id=1, source_target_pairs={{0,16},{2,18},{4,20},{6,22},{8,24},{10,26},{12,28},{14,30},{1,17},... | collective-permute-start | bytes 294920 | tf_op jit(solution)/shard_map/ppermute | solution.py:709
  22.9 3.7 %collective-permute-start.7 = (bf16[1,2,16,1536]{3,2,1,0:T(8,128)(2,1)S(1)}, bf16[1,2,16,1536]{3,2,1,0:T(8,128)(2,1)S(1)}, u32[]{:S(2)}, u32[]{:S(2)}) collective-permute-start(bf16[1,2,16,1536]{3,2,1,0:T(8,128)(2,1)S(1)} %get-tuple-element.73), channel_id=1, source_target_pairs={{0,24},{2,26},{4,28},{6,30},{1,25},{3,27},{5,29},{7,31}} | collective-permute-start | bytes 294920 | tf_op jit(solution)/shard_map/ppermute | solution.py:709
  26.6 9.8 %collective-permute-start.8 = (bf16[4,2,16,1536]{3,2,1,0:T(8,128)(2,1)S(1)}, bf16[4,2,16,1536]{3,2,1,0:T(8,128)(2,1)S(1)}, u32[]{:S(2)}, u32[]{:S(2)}) collective-permute-start(bf16[4,2,16,1536]{3,2,1,0:T(8,128)(2,1)S(1)} %pad_maximum_fusion.1), channel_id=1, source_target_pairs={{0,4},{2,6},{4,0},{6,2},{8,12},{10,14},{12,8},{14,10},{16,20},{18,... | collective-permute-start | bytes 1179656 | tf_op jit(solution)/shard_map/ppermute | solution.py:777
  37.2 10.6 %collective-permute-start.9 = (bf16[8,2,16,1536]{3,2,1,0:T(8,128)(2,1)}, bf16[8,2,16,1536]{3,2,1,0:T(8,128)(2,1)S(1)}, u32[]{:S(2)}, u32[]{:S(2)}) collective-permute-start(bf16[8,2,16,1536]{3,2,1,0:T(8,128)(2,1)} %constant_dynamic-update-slice_fusion.rest_0_), channel_id=1, source_target_pairs={{0,2},{2,0},{4,6},{6,4},{8,10},{10,8},{12,14},{14,12},{16,18},{18,... | collective-permute-start | bytes 2359304 | tf_op jit(solution)/shard_map/ppermute | solution.py:713
  37.3 18.3 %collective-permute-start.2 = (bf16[1,2,16,2560]{3,2,1,0:T(8,128)(2,1)S(1)}, bf16[1,2,16,2560]{3,2,1,0:T(8,128)(2,1)S(1)}, u32[]{:S(2)}, u32[]{:S(2)}) collective-permute-start(bf16[1,2,16,2560]{3,2,1,0:T(8,128)(2,1)S(1)} %fusion.9), channel_id=1, source_target_pairs={{0,8},{2,10},{4,12},{6,14},{8,16},{10,18},{12,20},{14,22},{16,24},... | collective-permute-start | bytes 491528 | tf_op jit(solution)/shard_map/ppermute | solution.py:709
  39.2 16.4 %collective-permute-start.3 = (bf16[1,2,16,2560]{3,2,1,0:T(8,128)(2,1)S(1)}, bf16[1,2,16,2560]{3,2,1,0:T(8,128)(2,1)S(1)}, u32[]{:S(2)}, u32[]{:S(2)}) collective-permute-start(bf16[1,2,16,2560]{3,2,1,0:T(8,128)(2,1)S(1)} %fusion.9), channel_id=1, source_target_pairs={{0,16},{2,18},{4,20},{6,22},{8,24},{10,26},{12,28},{14,30},{1,17},... | collective-permute-start | bytes 491528 | tf_op jit(solution)/shard_map/ppermute | solution.py:709
  45.2 10.4 %collective-permute-start.4 = (bf16[1,2,16,2560]{3,2,1,0:T(8,128)(2,1)S(1)}, bf16[1,2,16,2560]{3,2,1,0:T(8,128)(2,1)S(1)}, u32[]{:S(2)}, u32[]{:S(2)}) collective-permute-start(bf16[1,2,16,2560]{3,2,1,0:T(8,128)(2,1)S(1)} %fusion.9), channel_id=1, source_target_pairs={{0,24},{2,26},{4,28},{6,30},{1,25},{3,27},{5,29},{7,31}} | collective-permute-start | bytes 491528 | tf_op jit(solution)/shard_map/ppermute | solution.py:709
  47.8 1.4 copy-start.12
  47.8 39.3 %collective-permute-start.14 = (bf16[2,256,1536]{2,1,0:T(8,128)(2,1)}, bf16[2,256,1536]{2,1,0:T(8,128)(2,1)S(1)}, u32[]{:S(2)}, u32[]{:S(2)}) collective-permute-start(bf16[2,256,1536]{2,1,0:T(8,128)(2,1)} %maximum_add_fusion), channel_id=1, source_target_pairs={{0,1},{2,3},{4,5},{6,7},{8,9},{10,11},{12,13},{14,15},{16,17},{18,... | collective-permute-start | bytes 4718600 | tf_op jit(solution)/shard_map/ppermute | solution.py:696
  56.6 18.4 %collective-permute-start.10 = (bf16[4,2,16,2560]{3,2,1,0:T(8,128)(2,1)S(1)}, bf16[4,2,16,2560]{3,2,1,0:T(8,128)(2,1)}, u32[]{:S(2)}, u32[]{:S(2)}) collective-permute-start(bf16[4,2,16,2560]{3,2,1,0:T(8,128)(2,1)S(1)} %maximum_add_fusion.3), channel_id=1, source_target_pairs={{0,4},{2,6},{4,0},{6,2},{8,12},{10,14},{12,8},{14,10},{16,20},{18,... | collective-permute-start | bytes 1966088 | tf_op jit(solution)/shard_map/ppermute | solution.py:783
  58.2 15.6 %collective-permute-start.11 = (bf16[2,256,512]{2,1,0:T(8,128)(2,1)}, bf16[2,256,512]{2,1,0:T(8,128)(2,1)S(1)}, u32[]{:S(2)}, u32[]{:S(2)}) collective-permute-start(bf16[2,256,512]{2,1,0:T(8,128)(2,1)} %get-tuple-element.45), channel_id=1, source_target_pairs={{1,0},{3,2},{5,4},{7,6},{9,8},{11,10},{13,12},{15,14},{17,16},{19,... | collective-permute-start | bytes 1572872 | tf_op jit(solution)/shard_map/ppermute | solution.py:768
  73.8 1.2 copy-start.9
  76.2 4.3 %copy-start.1 = (bf16[8,2,16,2560]{3,2,1,0:T(8,128)(2,1)}, bf16[8,2,16,2560]{3,2,1,0:T(8,128)(2,1)S(1)}, u32[]{:S(2)}) copy-start(bf16[8,2,16,2560]{3,2,1,0:T(8,128)(2,1)S(1)} %fusion.rest_0_) | copy-start | bytes 3932164
  76.2 10.9 %collective-permute-start.13 = (bf16[8,2,16,2560]{3,2,1,0:T(8,128)(2,1)S(1)}, bf16[8,2,16,2560]{3,2,1,0:T(8,128)(2,1)S(1)}, u32[]{:S(2)}, u32[]{:S(2)}) collective-permute-start(bf16[8,2,16,2560]{3,2,1,0:T(8,128)(2,1)S(1)} %fusion.rest_0_), channel_id=1, source_target_pairs={{0,2},{2,0},{4,6},{6,4},{8,10},{10,8},{12,14},{14,12},{16,18},{18,... | collective-permute-start | bytes 3932168 | tf_op jit(solution)/shard_map/ppermute | solution.py:713
  78.0 26.7 %collective-permute-start.16 = (bf16[8,2,16,1536]{3,2,1,0:T(8,128)(2,1)}, bf16[8,2,16,1536]{3,2,1,0:T(8,128)(2,1)}, u32[]{:S(2)}, u32[]{:S(2)}) collective-permute-start(bf16[8,2,16,1536]{3,2,1,0:T(8,128)(2,1)} %get-tuple-element.54), channel_id=1, source_target_pairs={{0,2},{2,0},{4,6},{6,4},{8,10},{10,8},{12,14},{14,12},{16,18},{18,... | collective-permute-start | bytes 2359304 | tf_op jit(solution)/shard_map/ppermute | solution.py:716
  78.2 28.8 %collective-permute-start.15 = (bf16[2,256,1024]{2,1,0:T(8,128)(2,1)}, bf16[2,256,1024]{2,1,0:T(8,128)(2,1)}, u32[]{:S(2)}, u32[]{:S(2)}) collective-permute-start(bf16[2,256,1024]{2,1,0:T(8,128)(2,1)} %get-tuple-element.52), channel_id=1, source_target_pairs={{1,0},{3,2},{5,4},{7,6},{9,8},{11,10},{13,12},{15,14},{17,16},{19,... | collective-permute-start | bytes 3145736 | tf_op jit(solution)/shard_map/ppermute | solution.py:768
  80.6 28.6 %collective-permute-start.12 = (bf16[2,256,1024]{2,1,0:T(8,128)(2,1)}, bf16[2,256,1024]{2,1,0:T(8,128)(2,1)}, u32[]{:S(2)}, u32[]{:S(2)}) collective-permute-start(bf16[2,256,1024]{2,1,0:T(8,128)(2,1)} %maximum_add_fusion.2), channel_id=1, source_target_pairs={{0,1},{2,3},{4,5},{6,7},{8,9},{10,11},{12,13},{14,15},{16,17},{18,... | collective-permute-start | bytes 3145736 | tf_op jit(solution)/shard_map/ppermute | solution.py:696
  87.1 1.6 copy-start.4
  87.1 1.1 copy-start.5
  103.4 39.4 %collective-permute-start.23 = (bf16[2,256,1536]{2,1,0:T(8,128)(2,1)}, bf16[2,256,1536]{2,1,0:T(8,128)(2,1)S(1)}, u32[]{:S(2)}, u32[]{:S(2)}) collective-permute-start(bf16[2,256,1536]{2,1,0:T(8,128)(2,1)} %get-tuple-element.63), channel_id=1, source_target_pairs={{1,0},{3,2},{5,4},{7,6},{9,8},{11,10},{13,12},{15,14},{17,16},{19,... | collective-permute-start | bytes 4718600 | tf_op jit(solution)/shard_map/ppermute | solution.py:768
  106.3 2.8 %copy-start.2 = (bf16[8,2,16,1536]{3,2,1,0:T(8,128)(2,1)}, bf16[8,2,16,1536]{3,2,1,0:T(8,128)(2,1)S(1)}, u32[]{:S(2)}) copy-start(bf16[8,2,16,1536]{3,2,1,0:T(8,128)(2,1)S(1)} %fusion.1.rest_6_) | copy-start | bytes 2359300
  106.4 15.4 %collective-permute-start.17 = (bf16[4,2,16,1536]{3,2,1,0:T(8,128)(2,1)S(1)}, bf16[4,2,16,1536]{3,2,1,0:T(8,128)(2,1)}, u32[]{:S(2)}, u32[]{:S(2)}) collective-permute-start(bf16[4,2,16,1536]{3,2,1,0:T(8,128)(2,1)S(1)} %slice.150), channel_id=1, source_target_pairs={{0,4},{2,6},{4,0},{6,2},{8,12},{10,14},{12,8},{14,10},{16,20},{18,... | collective-permute-start | bytes 1179656 | tf_op jit(solution)/shard_map/ppermute | solution.py:719
  107.0 17.3 %collective-permute-start.20 = (bf16[8,2,16,1536]{3,2,1,0:T(8,128)(2,1)}, bf16[8,2,16,1536]{3,2,1,0:T(8,128)(2,1)}, u32[]{:S(2)}, u32[]{:S(2)}) collective-permute-start(bf16[8,2,16,1536]{3,2,1,0:T(8,128)(2,1)} %get-tuple-element.59), channel_id=1, source_target_pairs={{0,2},{2,0},{4,6},{6,4},{8,10},{10,8},{12,14},{14,12},{16,18},{18,... | collective-permute-start | bytes 2359304 | tf_op jit(solution)/shard_map/ppermute | solution.py:716
  119.3 5.0 %copy-start.8 = (bf16[8,2,16,1536]{3,2,1,0:T(8,128)(2,1)S(1)}, bf16[8,2,16,1536]{3,2,1,0:T(8,128)(2,1)}, u32[]{:S(2)}) copy-start(bf16[8,2,16,1536]{3,2,1,0:T(8,128)(2,1)} %get-tuple-element.58) | copy-start | bytes 2359300
  119.3 44.8 %collective-permute-start.28 = (bf16[2,256,1024]{2,1,0:T(8,128)(2,1)}, bf16[2,256,1024]{2,1,0:T(8,128)(2,1)S(1)}, u32[]{:S(2)}, u32[]{:S(2)}) collective-permute-start(bf16[2,256,1024]{2,1,0:T(8,128)(2,1)} %get-tuple-element.66), channel_id=1, source_target_pairs={{1,0},{3,2},{5,4},{7,6},{9,8},{11,10},{13,12},{15,14},{17,16},{19,... | collective-permute-start | bytes 3145736 | tf_op jit(solution)/shard_map/ppermute | solution.py:768
  121.8 22.2 %collective-permute-start.22 = (bf16[8,2,16,1024]{3,2,1,0:T(8,128)(2,1)}, bf16[8,2,16,1024]{3,2,1,0:T(8,128)(2,1)S(1)}, u32[]{:S(2)}, u32[]{:S(2)}) collective-permute-start(bf16[8,2,16,1024]{3,2,1,0:T(8,128)(2,1)} %get-tuple-element.62), channel_id=1, source_target_pairs={{0,2},{2,0},{4,6},{6,4},{8,10},{10,8},{12,14},{14,12},{16,18},{18,... | collective-permute-start | bytes 1572872 | tf_op jit(solution)/shard_map/ppermute | solution.py:716
  123.0 13.8 %collective-permute-start.18 = (bf16[2,2,16,1536]{3,2,1,0:T(8,128)(2,1)S(1)}, bf16[2,2,16,1536]{3,2,1,0:T(8,128)(2,1)S(1)}, u32[]{:S(2)}, u32[]{:S(2)}) collective-permute-start(bf16[2,2,16,1536]{3,2,1,0:T(8,128)(2,1)S(1)} %slice.152), channel_id=1, source_target_pairs={{16,0},{18,2},{20,4},{22,6},{24,8},{26,10},{28,12},{30,14},{17,1},... | collective-permute-start | bytes 589832 | tf_op jit(solution)/shard_map/ppermute | solution.py:730
  124.3 19.7 %copy-start.10 = (bf16[8,2,16,1024]{3,2,1,0:T(8,128)(2,1)S(1)}, bf16[8,2,16,1024]{3,2,1,0:T(8,128)(2,1)}, u32[]{:S(2)}) copy-start(bf16[8,2,16,1024]{3,2,1,0:T(8,128)(2,1)} %get-tuple-element.61) | copy-start | bytes 1572868
  125.8 19.0 %collective-permute-start.21 = (bf16[4,2,16,1536]{3,2,1,0:T(8,128)(2,1)S(1)}, bf16[4,2,16,1536]{3,2,1,0:T(8,128)(2,1)S(1)}, u32[]{:S(2)}, u32[]{:S(2)}) collective-permute-start(bf16[4,2,16,1536]{3,2,1,0:T(8,128)(2,1)S(1)} %slice.156), channel_id=1, source_target_pairs={{0,4},{2,6},{4,0},{6,2},{8,12},{10,14},{12,8},{14,10},{16,20},{18,... | collective-permute-start | bytes 1179656 | tf_op jit(solution)/shard_map/ppermute | solution.py:719
  136.8 21.5 %collective-permute-start.19 = (bf16[1,2,16,1536]{3,2,1,0:T(8,128)(2,1)S(1)}, bf16[1,2,16,1536]{3,2,1,0:T(8,128)(2,1)}, u32[]{:S(2)}, u32[]{:S(2)}) collective-permute-start(bf16[1,2,16,1536]{3,2,1,0:T(8,128)(2,1)S(1)} %slice.154), channel_id=1, source_target_pairs={{8,0},{10,2},{12,4},{14,6},{16,8},{18,10},{20,12},{22,14},{24,16},... | collective-permute-start | bytes 294920 | tf_op jit(solution)/shard_map/ppermute | solution.py:730
  142.7 2.2 %copy-start.3 = (bf16[2,256,1536]{2,1,0:T(8,128)(2,1)}, bf16[2,256,1536]{2,1,0:T(8,128)(2,1)S(1)}, u32[]{:S(2)}) copy-start(bf16[2,256,1536]{2,1,0:T(8,128)(2,1)S(1)} %collective-permute-done.23.refs_2_) | copy-start | bytes 4718596
  144.2 9.0 %collective-permute-start.24 = (bf16[4,2,16,1024]{3,2,1,0:T(8,128)(2,1)S(1)}, bf16[4,2,16,1024]{3,2,1,0:T(8,128)(2,1)}, u32[]{:S(2)}, u32[]{:S(2)}) collective-permute-start(bf16[4,2,16,1024]{3,2,1,0:T(8,128)(2,1)S(1)} %slice.159), channel_id=1, source_target_pairs={{0,4},{2,6},{4,0},{6,2},{8,12},{10,14},{12,8},{14,10},{16,20},{18,... | collective-permute-start | bytes 786440 | tf_op jit(solution)/shard_map/ppermute | solution.py:719
  154.3 18.5 %copy-start.11 = (s32[1,16]{1,0:T(1,128)S(1)}, s32[1,16]{1,0:T(1,128)}, u32[]{:S(2)}) copy-start(s32[1,16]{1,0:T(1,128)} %rows_ref.1) | copy-start | bytes 196
  154.4 11.0 %collective-permute-start.25 = (bf16[2,16,2560]{2,1,0:T(8,128)(2,1)S(1)}, bf16[2,16,2560]{2,1,0:T(8,128)(2,1)S(1)}, u32[]{:S(2)}, u32[]{:S(2)}) collective-permute-start(bf16[2,16,2560]{2,1,0:T(8,128)(2,1)S(1)} %get-tuple-element.78), channel_id=1, source_target_pairs={{8,0},{10,2},{12,4},{14,6},{16,8},{18,10},{20,12},{22,14},{24,16},... | collective-permute-start | bytes 491528 | tf_op jit(solution)/shard_map/ppermute | solution.py:724
  155.7 15.3 %collective-permute-start.26 = (bf16[2,16,2560]{2,1,0:T(8,128)(2,1)S(1)}, bf16[2,16,2560]{2,1,0:T(8,128)(2,1)S(1)}, u32[]{:S(2)}, u32[]{:S(2)}) collective-permute-start(bf16[2,16,2560]{2,1,0:T(8,128)(2,1)S(1)} %get-tuple-element.80), channel_id=1, source_target_pairs={{16,0},{18,2},{20,4},{22,6},{24,8},{26,10},{28,12},{30,14},{17,1},... | collective-permute-start | bytes 491528 | tf_op jit(solution)/shard_map/ppermute | solution.py:724
  157.0 14.0 %collective-permute-start.27 = (bf16[2,16,2560]{2,1,0:T(8,128)(2,1)S(1)}, bf16[2,16,2560]{2,1,0:T(8,128)(2,1)S(1)}, u32[]{:S(2)}, u32[]{:S(2)}) collective-permute-start(bf16[2,16,2560]{2,1,0:T(8,128)(2,1)S(1)} %get-tuple-element.79), channel_id=1, source_target_pairs={{24,0},{26,2},{28,4},{30,6},{25,1},{27,3},{29,5},{31,7}} | collective-permute-start | bytes 491528 | tf_op jit(solution)/shard_map/ppermute | solution.py:724
  164.1 9.3 %copy-start.7 = (bf16[2,256,1024]{2,1,0:T(8,128)(2,1)}, bf16[2,256,1024]{2,1,0:T(8,128)(2,1)S(1)}, u32[]{:S(2)}) copy-start(bf16[2,256,1024]{2,1,0:T(8,128)(2,1)S(1)} %collective-permute-done.28.refs_0_) | copy-start | bytes 3145732
  171.1 5.0 %collective-permute-start.29 = (bf16[2,8,4096]{2,1,0:T(8,128)(2,1)S(1)}, bf16[2,8,4096]{2,1,0:T(8,128)(2,1)S(1)}, u32[]{:S(2)}, u32[]{:S(2)}) collective-permute-start(bf16[2,8,4096]{2,1,0:T(8,128)(2,1)S(1)} %pad_maximum_fusion.2), channel_id=1, source_target_pairs={{0,1},{1,0},{2,3},{3,2},{4,5},{5,4},{6,7},{7,6},{8,9},{9,8},{10,11... | collective-permute-start | bytes 393224 | tf_op jit(solution)/shard_map/ppermute | solution.py:735

commit v5 on v4

--- a/solution.py
+++ b/solution.py
@@ -12,7 +12,7 @@
 
 
 neg_big = -1e30
-pos_big = 3e38
+pos_big = 3.4028235e38
 
 
 def head_scores(query_heads, key_heads, factor):

time: 183 us -> 183 us (level)
  no operation moved by 1% of the time
where the time goes in v5:
time: 183 us; the launch traced here: 182 us
  Pallas kernels  59.6 us (33%)
  starting transfers between devices  51.8 us (28%)
  waiting for transfers between devices  37.3 us (20%)
  other arithmetic  14.9 us (8%)
  local copies, waits for them, and re-layouts  13.4 us (7%)
  between operations  4.65 us (3%)
    pallas_call x4, Pallas kernels, attention_call(): pl.pallas_call(functools.partial(attention_step, len(summaries)), grid=(w...  40.5 us
    ppermute x6, starting transfers between devices, climb_stages(): lax.ppermute(ladder, 'seq', climb(i))  19 us
    ppermute x4, waiting for transfers between devices, attend(): backs.append(lax.ppermute(out[3], 'head', [(1, 0)]))  13.7 us
    ppermute x3, starting transfers between devices, lower_pair(): lowers.append(lax.ppermute(pair, 'head', [(0, 1)]))  11.1 us
    ppermute x2, waiting for transfers between devices, reduce_group_halving(): lax.ppermute(plane[size:], 'seq', descend(size))  10.3 us
    pallas_call x2, Pallas kernels, merge_call(): pl.pallas_call(functools.partial(merge_step, bounds), grid=(bounds[-1],),...  8.82 us
    ppermute x3, waiting for transfers between devices, reduce_group(): lax.ppermute(plane[i], 'seq', descend(i))  5.63 us
    ppermute x4, starting transfers between devices, attend(): backs.append(lax.ppermute(out[3], 'head', [(1, 0)]))  5.44 us
  transfers between devices with their start and end apart: 30, of which 8 were waited for; matrix products, arithmetic and copies ran while one was open for 14% of the time, Pallas kernels for 28%

profile of v5, /device:TPU:0, one launch (start us, length us, event | category | flops | bytes accessed | tf_op | source)
XLA Modules:
  0.0 181.7 jit_solution(12734459757259739539)
XLA Ops:
  0.6 3.9 %shard_map.94 = bf16[2,8,4096]{2,1,0:T(8,128)(2,1)} custom-call(s32[1]{0:T(128)} %bitcast.place_ref, s32[1,16]{1,0:T(1,128)} %rows_ref.1, bf16[256,4096]{1,0:T(8,128)(2,1)} %key_ref.9, bf16[256,4096]{1,0:T(8,128)(2,1)} %val_ref.9), custom_call_target="tpu_custom_call" | custom-call | tf_op jit(solution)/shard_map/pallas_call | solution.py:638
  4.5 3.0 %collective-permute-start = (bf16[2,8,4096]{2,1,0:T(8,128)(2,1)}, bf16[2,8,4096]{2,1,0:T(8,128)(2,1)S(1)}, u32[]{:S(2)}, u32[]{:S(2)}) collective-permute-start(bf16[2,8,4096]{2,1,0:T(8,128)(2,1)} %shard_map.94), channel_id=1, source_target_pairs={{0,1},{1,0},{2,3},{3,2},{4,5},{5,4},{6,7},{7,6},{8,9},{9,8},{10,11... | collective-permute-start | bytes 393224 | tf_op jit(solution)/shard_map/ppermute | solution.py:689
  7.6 1.6 slice_bitcast_fusion
  9.2 1.3 pad_maximum_fusion
  10.5 3.1 %collective-permute-start.5 = (bf16[2,256,1536]{2,1,0:T(8,128)(2,1)}, bf16[2,256,1536]{2,1,0:T(8,128)(2,1)}, u32[]{:S(2)}, u32[]{:S(2)}) collective-permute-start(bf16[2,256,1536]{2,1,0:T(8,128)(2,1)} %pad_maximum_fusion), channel_id=1, source_target_pairs={{0,1},{2,3},{4,5},{6,7},{8,9},{10,11},{12,13},{14,15},{16,17},{18,... | collective-permute-start | bytes 4718600 | tf_op jit(solution)/shard_map/ppermute | solution.py:696
  14.4 4.0 %collective-permute-start.1 = (bf16[1,2,16,1536]{3,2,1,0:T(8,128)(2,1)S(1)}, bf16[1,2,16,1536]{3,2,1,0:T(8,128)(2,1)S(1)}, u32[]{:S(2)}, u32[]{:S(2)}) collective-permute-start(bf16[1,2,16,1536]{3,2,1,0:T(8,128)(2,1)S(1)} %get-tuple-element.73), channel_id=1, source_target_pairs={{0,8},{2,10},{4,12},{6,14},{8,16},{10,18},{12,20},{14,22},{16,24},... | collective-permute-start | bytes 294920 | tf_op jit(solution)/shard_map/ppermute | solution.py:709
  18.3 4.5 %collective-permute-start.6 = (bf16[1,2,16,1536]{3,2,1,0:T(8,128)(2,1)S(1)}, bf16[1,2,16,1536]{3,2,1,0:T(8,128)(2,1)S(1)}, u32[]{:S(2)}, u32[]{:S(2)}) collective-permute-start(bf16[1,2,16,1536]{3,2,1,0:T(8,128)(2,1)S(1)} %get-tuple-element.73), channel_id=1, source_target_pairs={{0,16},{2,18},{4,20},{6,22},{8,24},{10,26},{12,28},{14,30},{1,17},... | collective-permute-start | bytes 294920 | tf_op jit(solution)/shard_map/ppermute | solution.py:709
  22.9 1.3 collective-permute-start.7
  24.8 1.7 shard_map.93.caps_ref
  26.6 1.6 collective-permute-start.8
  31.3 5.1 %collective-permute-done.8 = bf16[4,2,16,1536]{3,2,1,0:T(8,128)(2,1)S(1)} collective-permute-done((bf16[4,2,16,1536]{3,2,1,0:T(8,128)(2,1)S(1)}, bf16[4,2,16,1536]{3,2,1,0:T(8,128)(2,1)S(1)}, u32[]{:S(2)}, u32[]{:S(2)}) %collective-permute-start.8) | collective-permute-done | bytes 393248 | tf_op jit(solution)/shard_map/ppermute | solution.py:777
  37.3 1.9 %collective-permute-start.2 = (bf16[1,2,16,2560]{3,2,1,0:T(8,128)(2,1)S(1)}, bf16[1,2,16,2560]{3,2,1,0:T(8,128)(2,1)S(1)}, u32[]{:S(2)}, u32[]{:S(2)}) collective-permute-start(bf16[1,2,16,2560]{3,2,1,0:T(8,128)(2,1)S(1)} %fusion.9), channel_id=1, source_target_pairs={{0,8},{2,10},{4,12},{6,14},{8,16},{10,18},{12,20},{14,22},{16,24},... | collective-permute-start | bytes 491528 | tf_op jit(solution)/shard_map/ppermute | solution.py:709
  39.2 6.0 %collective-permute-start.3 = (bf16[1,2,16,2560]{3,2,1,0:T(8,128)(2,1)S(1)}, bf16[1,2,16,2560]{3,2,1,0:T(8,128)(2,1)S(1)}, u32[]{:S(2)}, u32[]{:S(2)}) collective-permute-start(bf16[1,2,16,2560]{3,2,1,0:T(8,128)(2,1)S(1)} %fusion.9), channel_id=1, source_target_pairs={{0,16},{2,18},{4,20},{6,22},{8,24},{10,26},{12,28},{14,30},{1,17},... | collective-permute-start | bytes 491528 | tf_op jit(solution)/shard_map/ppermute | solution.py:709
  45.2 1.3 collective-permute-start.4
  46.5 1.3 maximum_add_fusion
  47.8 1.4 collective-permute-start.14
  49.2 6.4 %shard_map.95 = (bf16[256,4096]{1,0:T(8,128)(2,1)}, bf16[256,4096]{1,0:T(8,128)(2,1)}, bf16[2,256,4096]{2,1,0:T(8,128)(2,1)}, bf16[2,256,512]{2,1,0:T(8,128)(2,1...) custom-call(f32[768,256]{1,0:T(8,128)} %shard_map.93.caps_ref, ...), custom_call_target="tpu_custom_call" | custom-call | flops 5637144576 | bytes 4194304 | tf_op jit(solution)/shard_map/pallas_call | solution.py:470
  56.6 1.6 collective-permute-start.10
  58.2 1.3 collective-permute-start.11
  59.5 10.1 %shard_map.96 = (bf16[256,4096]{1,0:T(8,128)(2,1)}, bf16[256,4096]{1,0:T(8,128)(2,1)}, bf16[2,256,4096]{2,1,0:T(8,128)(2,1)}, bf16[2,256,1024]{2,1,0:T(8,128)(2,...) custom-call(f32[768,256]{1,0:T(8,128)} %shard_map.93.caps_ref, ...), custom_call_target="tpu_custom_call", output_to_operand_aliasing={{0}: (8, {}), {1}: (9, {}), {2}: (10, {}), {4}: (11, {}), {... | custom-call | flops 11274289152 | bytes 8388608 | tf_op jit(solution)/shard_map/pallas_call | solution.py:470
  69.6 4.2 %collective-permute-done.11.refs_0_ = bf16[2,256,512]{2,1,0:T(8,128)(2,1)S(1)} collective-permute-done((bf16[2,256,512]{2,1,0:T(8,128)(2,1)}, bf16[2,256,512]{2,1,0:T(8,128)(2,1)S(1)}, u32[]{:S(2)}, u32[]{:S(2)}) %collective-permute-start.11) | collective-permute-done | bytes 524320 | tf_op jit(solution)/shard_map/ppermute | solution.py:768
  75.0 1.2 fusion.rest_0_
  76.3 1.7 slice_bitcast_fusion.4
  78.2 1.3 collective-permute-start.15
  80.6 6.6 %collective-permute-start.12 = (bf16[2,256,1024]{2,1,0:T(8,128)(2,1)}, bf16[2,256,1024]{2,1,0:T(8,128)(2,1)}, u32[]{:S(2)}, u32[]{:S(2)}) collective-permute-start(bf16[2,256,1024]{2,1,0:T(8,128)(2,1)} %maximum_add_fusion.2), channel_id=1, source_target_pairs={{0,1},{2,3},{4,5},{6,7},{8,9},{10,11},{12,13},{14,15},{16,17},{18,... | collective-permute-start | bytes 3145736 | tf_op jit(solution)/shard_map/ppermute | solution.py:696
  87.1 1.1 copy-done.5
  88.7 13.9 %shard_map.97 = (bf16[256,4096]{1,0:T(8,128)(2,1)}, bf16[256,4096]{1,0:T(8,128)(2,1)}, bf16[2,256,4096]{2,1,0:T(8,128)(2,1)}, bf16[2,256,1536]{2,1,0:T(8,128)(2,...) custom-call(f32[768,256]{1,0:T(8,128)} %shard_map.93.caps_ref, ...), custom_call_target="tpu_custom_call", output_to_operand_aliasing={{0}: (8, {}), {1}: (9, {}), {2}: (10, {})} | custom-call | flops 4831838208 | bytes 12582912 | tf_op jit(solution)/shard_map/pallas_call | solution.py:470
  103.4 1.3 collective-permute-start.23
  104.7 1.6 fusion.1.rest_6_
  107.0 2.2 %collective-permute-done.12.lower_ref = bf16[2,256,1024]{2,1,0:T(8,128)(2,1)} collective-permute-done((bf16[2,256,1024]{2,1,0:T(8,128)(2,1)}, bf16[2,256,1024]{2,1,0:T(8,128)(2,1)}, u32[]{:S(2)}, u32[]{:S(2)}) %collective-permute-start.12) | collective-permute-done | bytes 1048608 | tf_op jit(solution)/shard_map/ppermute | solution.py:696
  109.2 10.1 %shard_map.98 = (bf16[256,4096]{1,0:T(8,128)(2,1)}, bf16[256,4096]{1,0:T(8,128)(2,1)}, bf16[2,256,4096]{2,1,0:T(8,128)(2,1)}, bf16[2,256,1024]{2,1,0:T(8,128)(2,...) custom-call(f32[768,256]{1,0:T(8,128)} %shard_map.93.caps_ref, ...), custom_call_target="tpu_custom_call", output_to_operand_aliasing={{0}: (8, {}), {1}: (9, {}), {2}: (10, {})} | custom-call | flops 11274289152 | bytes 8388608 | tf_op jit(solution)/shard_map/pallas_call | solution.py:470
  119.3 1.6 collective-permute-start.28
  121.8 1.2 add_convert_fusion.4
  123.0 1.3 collective-permute-start.18
  124.3 1.5 fusion.2
  126.4 10.3 %collective-permute-done.18 = bf16[2,2,16,1536]{3,2,1,0:T(8,128)(2,1)S(1)} collective-permute-done((bf16[2,2,16,1536]{3,2,1,0:T(8,128)(2,1)S(1)}, bf16[2,2,16,1536]{3,2,1,0:T(8,128)(2,1)S(1)}, u32[]{:S(2)}, u32[]{:S(2)}) %collective-permute-start.18) | collective-permute-done | bytes 196640 | tf_op jit(solution)/shard_map/ppermute | solution.py:730
  136.8 1.3 collective-permute-start.19
  138.1 4.6 %collective-permute-done.23.refs_2_ = bf16[2,256,1536]{2,1,0:T(8,128)(2,1)S(1)} collective-permute-done((bf16[2,256,1536]{2,1,0:T(8,128)(2,1)}, bf16[2,256,1536]{2,1,0:T(8,128)(2,1)S(1)}, u32[]{:S(2)}, u32[]{:S(2)}) %collective-permute-start.23) | collective-permute-done | bytes 1572896 | tf_op jit(solution)/shard_map/ppermute | solution.py:768
  144.9 6.4 %shard_map.99 = (bf16[256,4096]{1,0:T(8,128)(2,1)}, bf16[256,4096]{1,0:T(8,128)(2,1)}) custom-call(bf16[2,256,4096]{2,1,0:T(8,128)(2,1)} %get-tuple-element.64.local_ref, bf16[2,256,512]{2,1,0:T(8,128)(2,1)} %copy-done.9, bf16[2,256,1024]{2,1,0:T(8,128)(2,1)} %collective-permute-done.15.rest_5_.refs_1_, bf16[2,256,1536]{2,1,0:T(8,128)(2,1)} %copy-done.3), custom_call_target="tpu_custom_call" | custom-call | flops 1572864 | bytes 9437184 | tf_op jit(solution)/shard_map/pallas_call | solution.py:524
  151.3 1.2 slice.160
  154.4 1.3 collective-permute-start.25
  155.7 1.3 collective-permute-start.26
  157.0 1.3 collective-permute-start.27
  159.2 4.9 %collective-permute-done.28.refs_0_ = bf16[2,256,1024]{2,1,0:T(8,128)(2,1)S(1)} collective-permute-done((bf16[2,256,1024]{2,1,0:T(8,128)(2,1)}, bf16[2,256,1024]{2,1,0:T(8,128)(2,1)S(1)}, u32[]{:S(2)}, u32[]{:S(2)}) %collective-permute-start.28) | collective-permute-done | bytes 1048608 | tf_op jit(solution)/shard_map/ppermute | solution.py:768
  165.4 5.6 %collective-permute-done.26 = bf16[2,16,2560]{2,1,0:T(8,128)(2,1)S(1)} collective-permute-done((bf16[2,16,2560]{2,1,0:T(8,128)(2,1)S(1)}, bf16[2,16,2560]{2,1,0:T(8,128)(2,1)S(1)}, u32[]{:S(2)}, u32[]{:S(2)}) %collective-permute-start.26) | collective-permute-done | bytes 163872 | tf_op jit(solution)/shard_map/ppermute | solution.py:724
  171.1 1.7 collective-permute-start.29
  173.4 2.4 %shard_map.100 = (bf16[256,4096]{1,0:T(8,128)(2,1)}, bf16[256,4096]{1,0:T(8,128)(2,1)}) custom-call(bf16[2,256,4096]{2,1,0:T(8,128)(2,1)} %get-tuple-element.64.local_ref, bf16[2,256,1024]{2,1,0:T(8,128)(2,1)} %copy-done.7, bf16[256,4096]{1,0:T(8,128)(2,1)} %get-tuple-element.65.refs_1_, ...), custom_call_target="tpu_custom_call", output_to_operand_aliasing={{0}: (2, {}), {1}: (3, {})} | custom-call | flops 524288 | bytes 3145728 | tf_op jit(solution)/shard_map/pallas_call | solution.py:524
  176.8 4.6 %shard_map.101 = (bf16[256,4096]{1,0:T(8,128)(2,1)}, bf16[256,4096]{1,0:T(8,128)(2,1)}) custom-call(s32[8]{0:T(128)} %subtract_bitcast_fusion.rows_ref, bf16[2,8,4096]{2,1,0:T(8,128)(2,1)} %add_convert_fusion.7.summ_ref, bf16[256,4096]{1,0:T(8,128)(2,1)} %get-tuple-element.68.key_ref, ...), custom_call_target="tpu_custom_call", output_to_operand_aliasing={{0}: (2, {}), {1}: (3, {})} | custom-call | flops 16777216 | bytes 4194304 | tf_op jit(solution)/shard_map/pallas_call | solution.py:578
  (98 shorter events, 17.0 us)
Async XLA Ops:
  0.6 6.9 %copy-start = (bf16[256,4096]{1,0:T(8,128)(2,1)S(1)}, bf16[256,4096]{1,0:T(8,128)(2,1)}, u32[]{:S(2)}) copy-start(bf16[256,4096]{1,0:T(8,128)(2,1)} %key_ref.9) | copy-start | bytes 6291460
  4.5 9.2 %collective-permute-start = (bf16[2,8,4096]{2,1,0:T(8,128)(2,1)}, bf16[2,8,4096]{2,1,0:T(8,128)(2,1)S(1)}, u32[]{:S(2)}, u32[]{:S(2)}) collective-permute-start(bf16[2,8,4096]{2,1,0:T(8,128)(2,1)} %shard_map.94), channel_id=1, source_target_pairs={{0,1},{1,0},{2,3},{3,2},{4,5},{5,4},{6,7},{7,6},{8,9},{9,8},{10,11... | collective-permute-start | bytes 393224 | tf_op jit(solution)/shard_map/ppermute | solution.py:689
  9.2 4.5 %copy-start.6 = (bf16[2,8,4096]{2,1,0:T(8,128)(2,1)S(1)}, bf16[2,8,4096]{2,1,0:T(8,128)(2,1)}, u32[]{:S(2)}) copy-start(bf16[2,8,4096]{2,1,0:T(8,128)(2,1)} %shard_map.94) | copy-start | bytes 393220
  10.5 38.7 %collective-permute-start.5 = (bf16[2,256,1536]{2,1,0:T(8,128)(2,1)}, bf16[2,256,1536]{2,1,0:T(8,128)(2,1)}, u32[]{:S(2)}, u32[]{:S(2)}) collective-permute-start(bf16[2,256,1536]{2,1,0:T(8,128)(2,1)} %pad_maximum_fusion), channel_id=1, source_target_pairs={{0,1},{2,3},{4,5},{6,7},{8,9},{10,11},{12,13},{14,15},{16,17},{18,... | collective-permute-start | bytes 4718600 | tf_op jit(solution)/shard_map/ppermute | solution.py:696
  14.4 12.2 %collective-permute-start.1 = (bf16[1,2,16,1536]{3,2,1,0:T(8,128)(2,1)S(1)}, bf16[1,2,16,1536]{3,2,1,0:T(8,128)(2,1)S(1)}, u32[]{:S(2)}, u32[]{:S(2)}) collective-permute-start(bf16[1,2,16,1536]{3,2,1,0:T(8,128)(2,1)S(1)} %get-tuple-element.73), channel_id=1, source_target_pairs={{0,8},{2,10},{4,12},{6,14},{8,16},{10,18},{12,20},{14,22},{16,24},... | collective-permute-start | bytes 294920 | tf_op jit(solution)/shard_map/ppermute | solution.py:709
  18.3 8.2 %collective-permute-start.6 = (bf16[1,2,16,1536]{3,2,1,0:T(8,128)(2,1)S(1)}, bf16[1,2,16,1536]{3,2,1,0:T(8,128)(2,1)S(1)}, u32[]{:S(2)}, u32[]{:S(2)}) collective-permute-start(bf16[1,2,16,1536]{3,2,1,0:T(8,128)(2,1)S(1)} %get-tuple-element.73), channel_id=1, source_target_pairs={{0,16},{2,18},{4,20},{6,22},{8,24},{10,26},{12,28},{14,30},{1,17},... | collective-permute-start | bytes 294920 | tf_op jit(solution)/shard_map/ppermute | solution.py:709
  22.9 3.7 %collective-permute-start.7 = (bf16[1,2,16,1536]{3,2,1,0:T(8,128)(2,1)S(1)}, bf16[1,2,16,1536]{3,2,1,0:T(8,128)(2,1)S(1)}, u32[]{:S(2)}, u32[]{:S(2)}) collective-permute-start(bf16[1,2,16,1536]{3,2,1,0:T(8,128)(2,1)S(1)} %get-tuple-element.73), channel_id=1, source_target_pairs={{0,24},{2,26},{4,28},{6,30},{1,25},{3,27},{5,29},{7,31}} | collective-permute-start | bytes 294920 | tf_op jit(solution)/shard_map/ppermute | solution.py:709
  26.6 9.8 %collective-permute-start.8 = (bf16[4,2,16,1536]{3,2,1,0:T(8,128)(2,1)S(1)}, bf16[4,2,16,1536]{3,2,1,0:T(8,128)(2,1)S(1)}, u32[]{:S(2)}, u32[]{:S(2)}) collective-permute-start(bf16[4,2,16,1536]{3,2,1,0:T(8,128)(2,1)S(1)} %pad_maximum_fusion.1), channel_id=1, source_target_pairs={{0,4},{2,6},{4,0},{6,2},{8,12},{10,14},{12,8},{14,10},{16,20},{18,... | collective-permute-start | bytes 1179656 | tf_op jit(solution)/shard_map/ppermute | solution.py:777
  37.2 10.6 %collective-permute-start.9 = (bf16[8,2,16,1536]{3,2,1,0:T(8,128)(2,1)}, bf16[8,2,16,1536]{3,2,1,0:T(8,128)(2,1)S(1)}, u32[]{:S(2)}, u32[]{:S(2)}) collective-permute-start(bf16[8,2,16,1536]{3,2,1,0:T(8,128)(2,1)} %constant_dynamic-update-slice_fusion.rest_0_), channel_id=1, source_target_pairs={{0,2},{2,0},{4,6},{6,4},{8,10},{10,8},{12,14},{14,12},{16,18},{18,... | collective-permute-start | bytes 2359304 | tf_op jit(solution)/shard_map/ppermute | solution.py:713
  37.3 18.3 %collective-permute-start.2 = (bf16[1,2,16,2560]{3,2,1,0:T(8,128)(2,1)S(1)}, bf16[1,2,16,2560]{3,2,1,0:T(8,128)(2,1)S(1)}, u32[]{:S(2)}, u32[]{:S(2)}) collective-permute-start(bf16[1,2,16,2560]{3,2,1,0:T(8,128)(2,1)S(1)} %fusion.9), channel_id=1, source_target_pairs={{0,8},{2,10},{4,12},{6,14},{8,16},{10,18},{12,20},{14,22},{16,24},... | collective-permute-start | bytes 491528 | tf_op jit(solution)/shard_map/ppermute | solution.py:709
  39.2 16.4 %collective-permute-start.3 = (bf16[1,2,16,2560]{3,2,1,0:T(8,128)(2,1)S(1)}, bf16[1,2,16,2560]{3,2,1,0:T(8,128)(2,1)S(1)}, u32[]{:S(2)}, u32[]{:S(2)}) collective-permute-start(bf16[1,2,16,2560]{3,2,1,0:T(8,128)(2,1)S(1)} %fusion.9), channel_id=1, source_target_pairs={{0,16},{2,18},{4,20},{6,22},{8,24},{10,26},{12,28},{14,30},{1,17},... | collective-permute-start | bytes 491528 | tf_op jit(solution)/shard_map/ppermute | solution.py:709
  45.2 10.4 %collective-permute-start.4 = (bf16[1,2,16,2560]{3,2,1,0:T(8,128)(2,1)S(1)}, bf16[1,2,16,2560]{3,2,1,0:T(8,128)(2,1)S(1)}, u32[]{:S(2)}, u32[]{:S(2)}) collective-permute-start(bf16[1,2,16,2560]{3,2,1,0:T(8,128)(2,1)S(1)} %fusion.9), channel_id=1, source_target_pairs={{0,24},{2,26},{4,28},{6,30},{1,25},{3,27},{5,29},{7,31}} | collective-permute-start | bytes 491528 | tf_op jit(solution)/shard_map/ppermute | solution.py:709
  47.8 1.4 copy-start.12
  47.8 39.3 %collective-permute-start.14 = (bf16[2,256,1536]{2,1,0:T(8,128)(2,1)}, bf16[2,256,1536]{2,1,0:T(8,128)(2,1)S(1)}, u32[]{:S(2)}, u32[]{:S(2)}) collective-permute-start(bf16[2,256,1536]{2,1,0:T(8,128)(2,1)} %maximum_add_fusion), channel_id=1, source_target_pairs={{0,1},{2,3},{4,5},{6,7},{8,9},{10,11},{12,13},{14,15},{16,17},{18,... | collective-permute-start | bytes 4718600 | tf_op jit(solution)/shard_map/ppermute | solution.py:696
  56.6 18.4 %collective-permute-start.10 = (bf16[4,2,16,2560]{3,2,1,0:T(8,128)(2,1)S(1)}, bf16[4,2,16,2560]{3,2,1,0:T(8,128)(2,1)}, u32[]{:S(2)}, u32[]{:S(2)}) collective-permute-start(bf16[4,2,16,2560]{3,2,1,0:T(8,128)(2,1)S(1)} %maximum_add_fusion.3), channel_id=1, source_target_pairs={{0,4},{2,6},{4,0},{6,2},{8,12},{10,14},{12,8},{14,10},{16,20},{18,... | collective-permute-start | bytes 1966088 | tf_op jit(solution)/shard_map/ppermute | solution.py:783
  58.2 15.6 %collective-permute-start.11 = (bf16[2,256,512]{2,1,0:T(8,128)(2,1)}, bf16[2,256,512]{2,1,0:T(8,128)(2,1)S(1)}, u32[]{:S(2)}, u32[]{:S(2)}) collective-permute-start(bf16[2,256,512]{2,1,0:T(8,128)(2,1)} %get-tuple-element.45), channel_id=1, source_target_pairs={{1,0},{3,2},{5,4},{7,6},{9,8},{11,10},{13,12},{15,14},{17,16},{19,... | collective-permute-start | bytes 1572872 | tf_op jit(solution)/shard_map/ppermute | solution.py:768
  73.8 1.2 copy-start.9
  76.2 4.3 %copy-start.1 = (bf16[8,2,16,2560]{3,2,1,0:T(8,128)(2,1)}, bf16[8,2,16,2560]{3,2,1,0:T(8,128)(2,1)S(1)}, u32[]{:S(2)}) copy-start(bf16[8,2,16,2560]{3,2,1,0:T(8,128)(2,1)S(1)} %fusion.rest_0_) | copy-start | bytes 3932164
  76.2 10.9 %collective-permute-start.13 = (bf16[8,2,16,2560]{3,2,1,0:T(8,128)(2,1)S(1)}, bf16[8,2,16,2560]{3,2,1,0:T(8,128)(2,1)S(1)}, u32[]{:S(2)}, u32[]{:S(2)}) collective-permute-start(bf16[8,2,16,2560]{3,2,1,0:T(8,128)(2,1)S(1)} %fusion.rest_0_), channel_id=1, source_target_pairs={{0,2},{2,0},{4,6},{6,4},{8,10},{10,8},{12,14},{14,12},{16,18},{18,... | collective-permute-start | bytes 3932168 | tf_op jit(solution)/shard_map/ppermute | solution.py:713
  78.0 26.7 %collective-permute-start.16 = (bf16[8,2,16,1536]{3,2,1,0:T(8,128)(2,1)}, bf16[8,2,16,1536]{3,2,1,0:T(8,128)(2,1)}, u32[]{:S(2)}, u32[]{:S(2)}) collective-permute-start(bf16[8,2,16,1536]{3,2,1,0:T(8,128)(2,1)} %get-tuple-element.54), channel_id=1, source_target_pairs={{0,2},{2,0},{4,6},{6,4},{8,10},{10,8},{12,14},{14,12},{16,18},{18,... | collective-permute-start | bytes 2359304 | tf_op jit(solution)/shard_map/ppermute | solution.py:716
  78.2 28.8 %collective-permute-start.15 = (bf16[2,256,1024]{2,1,0:T(8,128)(2,1)}, bf16[2,256,1024]{2,1,0:T(8,128)(2,1)}, u32[]{:S(2)}, u32[]{:S(2)}) collective-permute-start(bf16[2,256,1024]{2,1,0:T(8,128)(2,1)} %get-tuple-element.52), channel_id=1, source_target_pairs={{1,0},{3,2},{5,4},{7,6},{9,8},{11,10},{13,12},{15,14},{17,16},{19,... | collective-permute-start | bytes 3145736 | tf_op jit(solution)/shard_map/ppermute | solution.py:768
  80.6 28.6 %collective-permute-start.12 = (bf16[2,256,1024]{2,1,0:T(8,128)(2,1)}, bf16[2,256,1024]{2,1,0:T(8,128)(2,1)}, u32[]{:S(2)}, u32[]{:S(2)}) collective-permute-start(bf16[2,256,1024]{2,1,0:T(8,128)(2,1)} %maximum_add_fusion.2), channel_id=1, source_target_pairs={{0,1},{2,3},{4,5},{6,7},{8,9},{10,11},{12,13},{14,15},{16,17},{18,... | collective-permute-start | bytes 3145736 | tf_op jit(solution)/shard_map/ppermute | solution.py:696
  87.1 1.6 copy-start.4
  87.1 1.1 copy-start.5
  103.4 39.4 %collective-permute-start.23 = (bf16[2,256,1536]{2,1,0:T(8,128)(2,1)}, bf16[2,256,1536]{2,1,0:T(8,128)(2,1)S(1)}, u32[]{:S(2)}, u32[]{:S(2)}) collective-permute-start(bf16[2,256,1536]{2,1,0:T(8,128)(2,1)} %get-tuple-element.63), channel_id=1, source_target_pairs={{1,0},{3,2},{5,4},{7,6},{9,8},{11,10},{13,12},{15,14},{17,16},{19,... | collective-permute-start | bytes 4718600 | tf_op jit(solution)/shard_map/ppermute | solution.py:768
  106.3 2.8 %copy-start.2 = (bf16[8,2,16,1536]{3,2,1,0:T(8,128)(2,1)}, bf16[8,2,16,1536]{3,2,1,0:T(8,128)(2,1)S(1)}, u32[]{:S(2)}) copy-start(bf16[8,2,16,1536]{3,2,1,0:T(8,128)(2,1)S(1)} %fusion.1.rest_6_) | copy-start | bytes 2359300
  106.4 15.4 %collective-permute-start.17 = (bf16[4,2,16,1536]{3,2,1,0:T(8,128)(2,1)S(1)}, bf16[4,2,16,1536]{3,2,1,0:T(8,128)(2,1)}, u32[]{:S(2)}, u32[]{:S(2)}) collective-permute-start(bf16[4,2,16,1536]{3,2,1,0:T(8,128)(2,1)S(1)} %slice.150), channel_id=1, source_target_pairs={{0,4},{2,6},{4,0},{6,2},{8,12},{10,14},{12,8},{14,10},{16,20},{18,... | collective-permute-start | bytes 1179656 | tf_op jit(solution)/shard_map/ppermute | solution.py:719
  107.0 17.3 %collective-permute-start.20 = (bf16[8,2,16,1536]{3,2,1,0:T(8,128)(2,1)}, bf16[8,2,16,1536]{3,2,1,0:T(8,128)(2,1)}, u32[]{:S(2)}, u32[]{:S(2)}) collective-permute-start(bf16[8,2,16,1536]{3,2,1,0:T(8,128)(2,1)} %get-tuple-element.59), channel_id=1, source_target_pairs={{0,2},{2,0},{4,6},{6,4},{8,10},{10,8},{12,14},{14,12},{16,18},{18,... | collective-permute-start | bytes 2359304 | tf_op jit(solution)/shard_map/ppermute | solution.py:716
  119.3 5.0 %copy-start.8 = (bf16[8,2,16,1536]{3,2,1,0:T(8,128)(2,1)S(1)}, bf16[8,2,16,1536]{3,2,1,0:T(8,128)(2,1)}, u32[]{:S(2)}) copy-start(bf16[8,2,16,1536]{3,2,1,0:T(8,128)(2,1)} %get-tuple-element.58) | copy-start | bytes 2359300
  119.3 44.8 %collective-permute-start.28 = (bf16[2,256,1024]{2,1,0:T(8,128)(2,1)}, bf16[2,256,1024]{2,1,0:T(8,128)(2,1)S(1)}, u32[]{:S(2)}, u32[]{:S(2)}) collective-permute-start(bf16[2,256,1024]{2,1,0:T(8,128)(2,1)} %get-tuple-element.66), channel_id=1, source_target_pairs={{1,0},{3,2},{5,4},{7,6},{9,8},{11,10},{13,12},{15,14},{17,16},{19,... | collective-permute-start | bytes 3145736 | tf_op jit(solution)/shard_map/ppermute | solution.py:768
  121.8 22.2 %collective-permute-start.22 = (bf16[8,2,16,1024]{3,2,1,0:T(8,128)(2,1)}, bf16[8,2,16,1024]{3,2,1,0:T(8,128)(2,1)S(1)}, u32[]{:S(2)}, u32[]{:S(2)}) collective-permute-start(bf16[8,2,16,1024]{3,2,1,0:T(8,128)(2,1)} %get-tuple-element.62), channel_id=1, source_target_pairs={{0,2},{2,0},{4,6},{6,4},{8,10},{10,8},{12,14},{14,12},{16,18},{18,... | collective-permute-start | bytes 1572872 | tf_op jit(solution)/shard_map/ppermute | solution.py:716
  123.0 13.8 %collective-permute-start.18 = (bf16[2,2,16,1536]{3,2,1,0:T(8,128)(2,1)S(1)}, bf16[2,2,16,1536]{3,2,1,0:T(8,128)(2,1)S(1)}, u32[]{:S(2)}, u32[]{:S(2)}) collective-permute-start(bf16[2,2,16,1536]{3,2,1,0:T(8,128)(2,1)S(1)} %slice.152), channel_id=1, source_target_pairs={{16,0},{18,2},{20,4},{22,6},{24,8},{26,10},{28,12},{30,14},{17,1},... | collective-permute-start | bytes 589832 | tf_op jit(solution)/shard_map/ppermute | solution.py:730
  124.3 19.7 %copy-start.10 = (bf16[8,2,16,1024]{3,2,1,0:T(8,128)(2,1)S(1)}, bf16[8,2,16,1024]{3,2,1,0:T(8,128)(2,1)}, u32[]{:S(2)}) copy-start(bf16[8,2,16,1024]{3,2,1,0:T(8,128)(2,1)} %get-tuple-element.61) | copy-start | bytes 1572868
  125.8 19.0 %collective-permute-start.21 = (bf16[4,2,16,1536]{3,2,1,0:T(8,128)(2,1)S(1)}, bf16[4,2,16,1536]{3,2,1,0:T(8,128)(2,1)S(1)}, u32[]{:S(2)}, u32[]{:S(2)}) collective-permute-start(bf16[4,2,16,1536]{3,2,1,0:T(8,128)(2,1)S(1)} %slice.156), channel_id=1, source_target_pairs={{0,4},{2,6},{4,0},{6,2},{8,12},{10,14},{12,8},{14,10},{16,20},{18,... | collective-permute-start | bytes 1179656 | tf_op jit(solution)/shard_map/ppermute | solution.py:719
  136.8 21.5 %collective-permute-start.19 = (bf16[1,2,16,1536]{3,2,1,0:T(8,128)(2,1)S(1)}, bf16[1,2,16,1536]{3,2,1,0:T(8,128)(2,1)}, u32[]{:S(2)}, u32[]{:S(2)}) collective-permute-start(bf16[1,2,16,1536]{3,2,1,0:T(8,128)(2,1)S(1)} %slice.154), channel_id=1, source_target_pairs={{8,0},{10,2},{12,4},{14,6},{16,8},{18,10},{20,12},{22,14},{24,16},... | collective-permute-start | bytes 294920 | tf_op jit(solution)/shard_map/ppermute | solution.py:730
  142.7 2.2 %copy-start.3 = (bf16[2,256,1536]{2,1,0:T(8,128)(2,1)}, bf16[2,256,1536]{2,1,0:T(8,128)(2,1)S(1)}, u32[]{:S(2)}) copy-start(bf16[2,256,1536]{2,1,0:T(8,128)(2,1)S(1)} %collective-permute-done.23.refs_2_) | copy-start | bytes 4718596
  144.2 9.0 %collective-permute-start.24 = (bf16[4,2,16,1024]{3,2,1,0:T(8,128)(2,1)S(1)}, bf16[4,2,16,1024]{3,2,1,0:T(8,128)(2,1)}, u32[]{:S(2)}, u32[]{:S(2)}) collective-permute-start(bf16[4,2,16,1024]{3,2,1,0:T(8,128)(2,1)S(1)} %slice.159), channel_id=1, source_target_pairs={{0,4},{2,6},{4,0},{6,2},{8,12},{10,14},{12,8},{14,10},{16,20},{18,... | collective-permute-start | bytes 786440 | tf_op jit(solution)/shard_map/ppermute | solution.py:719
  154.3 18.5 %copy-start.11 = (s32[1,16]{1,0:T(1,128)S(1)}, s32[1,16]{1,0:T(1,128)}, u32[]{:S(2)}) copy-start(s32[1,16]{1,0:T(1,128)} %rows_ref.1) | copy-start | bytes 196
  154.4 11.0 %collective-permute-start.25 = (bf16[2,16,2560]{2,1,0:T(8,128)(2,1)S(1)}, bf16[2,16,2560]{2,1,0:T(8,128)(2,1)S(1)}, u32[]{:S(2)}, u32[]{:S(2)}) collective-permute-start(bf16[2,16,2560]{2,1,0:T(8,128)(2,1)S(1)} %get-tuple-element.78), channel_id=1, source_target_pairs={{8,0},{10,2},{12,4},{14,6},{16,8},{18,10},{20,12},{22,14},{24,16},... | collective-permute-start | bytes 491528 | tf_op jit(solution)/shard_map/ppermute | solution.py:724
  155.7 15.3 %collective-permute-start.26 = (bf16[2,16,2560]{2,1,0:T(8,128)(2,1)S(1)}, bf16[2,16,2560]{2,1,0:T(8,128)(2,1)S(1)}, u32[]{:S(2)}, u32[]{:S(2)}) collective-permute-start(bf16[2,16,2560]{2,1,0:T(8,128)(2,1)S(1)} %get-tuple-element.80), channel_id=1, source_target_pairs={{16,0},{18,2},{20,4},{22,6},{24,8},{26,10},{28,12},{30,14},{17,1},... | collective-permute-start | bytes 491528 | tf_op jit(solution)/shard_map/ppermute | solution.py:724
  157.0 14.0 %collective-permute-start.27 = (bf16[2,16,2560]{2,1,0:T(8,128)(2,1)S(1)}, bf16[2,16,2560]{2,1,0:T(8,128)(2,1)S(1)}, u32[]{:S(2)}, u32[]{:S(2)}) collective-permute-start(bf16[2,16,2560]{2,1,0:T(8,128)(2,1)S(1)} %get-tuple-element.79), channel_id=1, source_target_pairs={{24,0},{26,2},{28,4},{30,6},{25,1},{27,3},{29,5},{31,7}} | collective-permute-start | bytes 491528 | tf_op jit(solution)/shard_map/ppermute | solution.py:724
  164.1 9.3 %copy-start.7 = (bf16[2,256,1024]{2,1,0:T(8,128)(2,1)}, bf16[2,256,1024]{2,1,0:T(8,128)(2,1)S(1)}, u32[]{:S(2)}) copy-start(bf16[2,256,1024]{2,1,0:T(8,128)(2,1)S(1)} %collective-permute-done.28.refs_0_) | copy-start | bytes 3145732
  171.1 5.0 %collective-permute-start.29 = (bf16[2,8,4096]{2,1,0:T(8,128)(2,1)S(1)}, bf16[2,8,4096]{2,1,0:T(8,128)(2,1)S(1)}, u32[]{:S(2)}, u32[]{:S(2)}) collective-permute-start(bf16[2,8,4096]{2,1,0:T(8,128)(2,1)S(1)} %pad_maximum_fusion.2), channel_id=1, source_target_pairs={{0,1},{1,0},{2,3},{3,2},{4,5},{5,4},{6,7},{7,6},{8,9},{9,8},{10,11... | collective-permute-start | bytes 393224 | tf_op jit(solution)/shard_map/ppermute | solution.py:735
